TPU v7x, 256 devices: a whole 4x4x8 slice. The times are simulated.
256 devices in a mesh: seq: 128 (over z, x, y), head: 2 (over core).
Axes of the slice: x: 4, y: 4, z: 8, core: 2. Of those that a mesh axis runs over, the one named last changes fastest.
Arguments:
- queries: bfloat16 [16384, 4096], P('seq', 'head'), may hold values from -8 to 8
- keys: bfloat16 [16384, 4096], P('seq', 'head'), may hold values from -8 to 8
- values: bfloat16 [16384, 4096], P('seq', 'head'), may hold values from -6 to 6
- out_grad: bfloat16 [16384, 4096], P('seq', 'head'), may hold values from -6 to 6
- cluster_ids: int32 [16384, 32], P('seq', 'head'), may hold values from 0 to 127, as said below
Outputs:
- attended: bfloat16 [16384, 4096], P('seq', 'head')
- grad_queries: bfloat16 [16384, 4096], P('seq', 'head')
- grad_keys: bfloat16 [16384, 4096], P('seq', 'head')
- grad_values: bfloat16 [16384, 4096], P('seq', 'head')
Inputs may be any that keep to these rules, and one draw needn't show every extreme that they name: `cluster_ids`: for each head the ids form 8 ranges of 16 consecutive ids, each used by exactly 2048 tokens; the tokens of one index of seq in one range number at most 24, reached in every head, and the counts of every index of seq over a head's ranges are the same numbers in some order.
All inputs are finite; a program needn't handle non-finite values.
Results may differ from a plain program's by a relative error of at most 0.012.
The roundings to bfloat16 on the way count: a program that leaves them out, or rounds other values in their place, can miss the bound.
Values may be sent and summed in bfloat16 or wider, within the bound.
No kernel may reach another device: no remote copies, remote signals or barrier semaphores. Data moves between devices by JAX's collectives and lax.ppermute only.
A program may use at most 64 MiB of HBM per device.

v0:
```python
import functools
import math

import jax
import jax.numpy as jnp
from jax import lax
from jax.experimental import pallas as pl
from jax.experimental.pallas import tpu as pltpu
from jax.sharding import PartitionSpec as P

WIDTH = 128
SPAN = 256
CLUSTER_GROUP = 16
RANGES = 8
TOK = 128
MOST = 24
ZN = 8
PLANE = 16
HPZ = 2
ALL = 4 * WIDTH
PAIR = HPZ * WIDTH
STRIDE = 32
BLOCK = 2048
SPANS = BLOCK // SPAN
TILE = 16
NONE = 4095
SCALING = 1.0 / math.sqrt(WIDTH)
BF = jnp.bfloat16
F32 = jnp.float32
I32 = jnp.int32

CHUNKS = ((0, 1, 7, 4), (2, 6, 3, 5))
PLANES = [[z * PLANE + i for i in range(PLANE)] for z in range(ZN)]
LINES = [[z * PLANE + i for z in range(ZN)] for i in range(PLANE)]


def z_pairs(step):
    return [
        (z * PLANE + i, ((z + step) % ZN) * PLANE + i)
        for z in range(ZN)
        for i in range(PLANE)
    ]


def whole():
    return pl.BlockSpec(memory_space=pltpu.VMEM)


def call(kernel, ins, outs, scratch=(), flops=0, specs=None, grid=()):
    size = sum(math.prod(o.shape) * o.dtype.itemsize for o in outs)
    size += sum(math.prod(a.shape) * a.dtype.itemsize for a in ins)
    specs = specs or {}
    return pl.pallas_call(
        kernel,
        out_shape=tuple(outs),
        grid=grid,
        in_specs=[specs.get(i) or whole() for i in range(len(ins))],
        out_specs=tuple(whole() for _ in outs),
        scratch_shapes=list(scratch),
        cost_estimate=pl.CostEstimate(flops=flops, bytes_accessed=size, transcendentals=0),
        compiler_params=pltpu.CompilerParams(vmem_limit_bytes=48 * 1024 * 1024),
    )(*ins)


SMEM = {0: pl.BlockSpec(memory_space=pltpu.SMEM)}


def out(shape, dtype):
    return jax.ShapeDtypeStruct(shape, dtype)


def iota(shape, dim):
    return lax.broadcasted_iota(I32, shape, dim)


def one_hot(mask):
    return mask.astype(F32).astype(BF)


def row_to_col(row):
    eye = iota((128, 128), 0) == iota((128, 128), 1)
    parts = []
    for i in range(row.shape[1] // 128):
        piece = row[:, i * 128 : (i + 1) * 128]
        parts.append(jnp.sum(jnp.where(eye, piece, 0.0), axis=1, keepdims=True))
    return jnp.concatenate(parts, axis=0)


def dot(a, b, dims=((1,), (0,))):
    return lax.dot_general(a, b, (dims, ((), ())), preferred_element_type=F32)


NT = ((1,), (1,))
TN = ((0,), (0,))


def prep_kernel(place_ref, *refs):
    arrays, blocks = refs[:4], refs[4:]
    z = place_ref[0]
    for d in range(ZN):
        cols = pl.ds(pl.multiple_of(((z + d) & (ZN - 1)) * PAIR, PAIR), PAIR)
        for t in range(4):
            blocks[d][t * TOK : (t + 1) * TOK, :] = arrays[t][:, cols]


def meta_kernel(ids_ref, code_ref, tile_ref):
    tri = one_hot(iota((TOK, TOK), 0) < iota((TOK, TOK), 1))
    for hh in range(HPZ):
        ids = ids_ref[:, hh, :]
        group = lax.shift_right_logical(ids, 4)
        local = (ids & (CLUSTER_GROUP - 1)) + 1
        slot = jnp.zeros((ZN, TOK), F32)
        for b in range(RANGES):
            hot = (group == b).astype(F32)
            slot = slot + hot * dot(hot.astype(BF), tri)
        code = group * STRIDE + slot.astype(I32)
        code_ref[hh] = code
        rows = []
        for i in range(ZN):
            pick = one_hot(iota((RANGES * STRIDE, TOK), 0) == code[i : i + 1, :])
            value = jnp.broadcast_to(local[i : i + 1, :], (TILE, TOK)).astype(F32).astype(BF)
            rows.append(dot(value, pick, NT)[0:1, :])
        rows.append(jnp.zeros((TILE - ZN, RANGES * STRIDE), F32))
        tile_ref[hh, :, 0 : RANGES * STRIDE] = jnp.concatenate(rows, axis=0).astype(BF)
        tile_ref[hh, :, RANGES * STRIDE :] = jnp.zeros((TILE, ALL - RANGES * STRIDE), BF)


def pack_kernel(chunk, with_tile, place_ref, code_ref, *refs):
    n = len(chunk)
    blocks, rest = refs[:n], refs[n:]
    tile_ref = rest[0] if with_tile else None
    send_ref, x_ref = rest[-2:]
    z = place_ref[0]
    rows = n * MOST
    for hh in range(HPZ):
        codes = []
        for i, d in enumerate(chunk):
            for t in range(4):
                x_ref[i * TOK : (i + 1) * TOK, t * WIDTH : (t + 1) * WIDTH] = blocks[i][
                    t * TOK : (t + 1) * TOK, hh * WIDTH : (hh + 1) * WIDTH
                ]
            codes.append(code_ref[hh, pl.ds((z - d) & (ZN - 1), 1), :] + i * MOST * RANGES * STRIDE)
        code = jnp.concatenate(codes, axis=1)
        group = lax.shift_right_logical(code, 5) & (RANGES - 1)
        position = (code & (STRIDE - 1)) + lax.shift_right_logical(code, 8)
        x = x_ref[...]
        for b in range(RANGES):
            target = jnp.where(group == b, position, -1)
            pick = one_hot(target == iota((rows, n * TOK), 0))
            send_ref[hh * RANGES + b, 0:rows, :] = dot(pick, x).astype(BF)
            if with_tile:
                send_ref[hh * RANGES + b, rows : rows + TILE, :] = tile_ref[hh]


def rank_kernel(place_ref, tile_ref, *refs):
    ranks, (high_ref, low_ref) = refs[: len(CHUNKS)], refs[len(CHUNKS) :]
    z = place_ref[0]
    mine = place_ref[2]
    tiles = tile_ref[...].reshape(PLANE * TILE, RANGES * STRIDE)
    lanes = iota((RANGES * STRIDE, 128), 1)
    cut = one_hot((iota((RANGES * STRIDE, 128), 0) == lanes + mine * STRIDE) & (lanes < MOST))
    row = iota((ZN * PLANE, PLANE * TILE), 0)
    col = iota((ZN * PLANE, PLANE * TILE), 1)
    order = one_hot(((col & (TILE - 1)) == lax.shift_right_logical(row, 4)) & (
        lax.shift_right_logical(col, 4) == (row & (PLANE - 1))
    ))
    cluster = dot(order, dot(tiles, cut).astype(BF))
    tri = one_hot(iota((128, 128), 0) < iota((128, 128), 1))
    low_tri = one_hot(iota((128, 128), 0) > iota((128, 128), 1))
    ones = jnp.ones((128, 128), BF)
    base = jnp.zeros((1, 128), F32)
    rank = jnp.zeros((128, 128), F32)
    for c in range(CLUSTER_GROUP):
        hot = (cluster == float(c + 1)).astype(F32)
        low = hot.astype(BF)
        count = dot(low, ones)
        rank = rank + hot * (base + dot(low_tri, count.astype(BF)) + dot(low, tri))
        base = base + jnp.sum(count, axis=0, keepdims=True)
    rank = jnp.where(cluster > 0.5, rank, float(NONE)).astype(I32)
    high_ref[...] = lax.shift_right_logical(rank, 8).astype(F32)
    low_ref[...] = (rank & 255).astype(F32)
    for chunk, rank_ref in zip(CHUNKS, ranks):
        rows = len(chunk) * MOST
        high = jnp.zeros((PLANE, rows), F32)
        low = jnp.zeros((PLANE, rows), F32)
        for i, d in enumerate(chunk):
            at = pl.ds(pl.multiple_of(((z - d) & (ZN - 1)) * PLANE, PLANE), PLANE)
            slot = iota((128, rows), 0)
            spread = one_hot((iota((128, rows), 1) == slot + i * MOST) & (slot < MOST))
            high = high + dot(high_ref[at, :].astype(BF), spread)
            low = low + dot(low_ref[at, :].astype(BF), spread)
        rank_ref[...] = (high * 256.0 + low).astype(I32)


def place_kernel(rows, last, rank_ref, recv_ref, *refs):
    x_ref = refs[-1]
    x_ref[...] = recv_ref[:, 0:rows, :].reshape(PLANE * rows, ALL)
    rank = rank_ref[...]
    x = x_ref[...]
    sorted_ref = refs[1] if last else refs[0]
    step = 2
    for c in range(0, SPANS, step):
        pick = one_hot(rank == iota((step * SPAN, PLANE * rows), 0) + c * SPAN)
        got = dot(pick, x).astype(BF).reshape(step, SPAN, ALL)
        if last:
            got = got + refs[0][c : c + step]
        sorted_ref[c : c + step] = got
    if last:
        refs[2][...] = sorted_ref[SPANS - 1, :, WIDTH : 3 * WIDTH]
        refs[3][...] = sorted_ref[0]


def span_math(q, g, k0, k1, v0, v1, keep):
    s0 = dot(q, k0, NT)
    s1 = dot(q, k1, NT)
    if keep is not None:
        s0 = jnp.where(keep, s0, -1e30)
    peak = jnp.maximum(
        jnp.max(s0, axis=1, keepdims=True), jnp.max(s1, axis=1, keepdims=True)
    )
    factor = SCALING * math.log2(math.e)
    p0 = jnp.exp2((s0 - peak) * factor)
    p1 = jnp.exp2((s1 - peak) * factor)
    inverse = 1.0 / (
        jnp.sum(p0, axis=1, keepdims=True) + jnp.sum(p1, axis=1, keepdims=True)
    )
    w0 = p0 * inverse
    w1 = p1 * inverse
    l0 = w0.astype(BF)
    l1 = w1.astype(BF)
    attended = (dot(l0, v0) + dot(l1, v1)).astype(BF)
    e0 = dot(g, v0, NT)
    e1 = dot(g, v1, NT)
    inner = jnp.sum(w0 * e0, axis=1, keepdims=True) + jnp.sum(w1 * e1, axis=1, keepdims=True)
    h0 = (w0 * (e0 - inner) * SCALING).astype(BF)
    h1 = (w1 * (e1 - inner) * SCALING).astype(BF)
    dq = (dot(h0, k0) + dot(h1, k1)).astype(BF)
    return attended, dq, dot(h0, q, TN), dot(h1, q, TN), dot(l0, g, TN), dot(l1, g, TN)


Q, K, V, G = (slice(t * WIDTH, (t + 1) * WIDTH) for t in range(4))


def main_kernel(in_ref, o_ref, part_ref, d_ref):
    d_ref[0] = jnp.zeros((SPAN, PAIR), F32)

    def one(c, carry):
        att, dq, dk0, dk1, dv0, dv1 = span_math(
            in_ref[c, :, Q], in_ref[c, :, G], in_ref[c - 1, :, K], in_ref[c, :, K],
            in_ref[c - 1, :, V], in_ref[c, :, V], None,
        )
        o_ref[c, :, Q] = att
        o_ref[c, :, K] = dq
        d_ref[c - 1, :, Q] += dk0
        d_ref[c - 1, :, K] += dv0
        d_ref[c, :, Q] = dk1
        d_ref[c, :, K] = dv1
        o_ref[c - 1, :, 2 * WIDTH :] = d_ref[c - 1].astype(BF)
        return carry

    lax.fori_loop(1, SPANS, one, 0)
    part_ref[0] = d_ref[0]
    part_ref[1] = d_ref[SPANS - 1]
    o_ref[0, :, 0 : 2 * WIDTH] = jnp.zeros((SPAN, 2 * WIDTH), BF)
    o_ref[SPANS - 1, :, 2 * WIDTH :] = jnp.zeros((SPAN, 2 * WIDTH), BF)


def pick_out(rank_ref, o, send_ref):
    col = row_to_col(rank_ref[...].astype(F32)).astype(I32)
    rows = send_ref.shape[1]
    step = 8
    for s in range(0, PLANE, step):
        part = col[s * rows : (s + step) * rows, :]
        pick = one_hot(part == iota((step * rows, BLOCK), 1))
        send_ref[s : s + step] = dot(pick, o).astype(BF).reshape(step, rows, ALL)


def edge_kernel(
    place_ref, rank_ref, in_ref, last_ref, tail_ref, head_ref, main_ref, part_ref, o_ref, send_ref
):
    o_ref[SPAN : BLOCK, :] = main_ref[1:].reshape(BLOCK - SPAN, ALL)
    keep = jnp.broadcast_to(place_ref[2], (SPAN, SPAN)) > 0
    att, dq, _, dk1, _, dv1 = span_math(
        in_ref[0, :, Q], in_ref[0, :, G], tail_ref[:, Q], in_ref[0, :, K],
        tail_ref[:, K], in_ref[0, :, V], keep,
    )
    o_ref[0:SPAN, Q] = att
    o_ref[0:SPAN, K] = dq
    o_ref[0:SPAN, V] = (part_ref[0, :, Q] + dk1).astype(BF)
    o_ref[0:SPAN, G] = (part_ref[0, :, K] + dv1).astype(BF)
    _, _, dk0, _, dv0, _ = span_math(
        head_ref[:, Q], head_ref[:, G], last_ref[0, :, K], head_ref[:, K],
        last_ref[0, :, V], head_ref[:, V], None,
    )
    o_ref[BLOCK - SPAN :, V] = (part_ref[1, :, Q] + dk0).astype(BF)
    o_ref[BLOCK - SPAN :, G] = (part_ref[1, :, K] + dv0).astype(BF)
    pick_out(rank_ref, o_ref[...], send_ref)


def pick_kernel(rank_ref, o_ref, send_ref):
    pick_out(rank_ref, o_ref[...], send_ref)


def unpack_kernel(chunk, place_ref, code_ref, recv_ref, *blocks):
    z = place_ref[0]
    n = len(chunk)
    rows = n * MOST
    for hh in range(HPZ):
        cols = []
        for i, d in enumerate(chunk):
            code = code_ref[hh, pl.ds((z - d) & (ZN - 1), 1), :]
            target = lax.shift_right_logical(code, 5) * rows + (code & (STRIDE - 1)) + i * MOST
            cols.append(row_to_col(target.astype(F32)).astype(I32))
        col = jnp.concatenate(cols, axis=0)
        pick = one_hot(col == iota((n * TOK, RANGES * rows), 1))
        x = recv_ref[hh * RANGES : (hh + 1) * RANGES].reshape(RANGES * rows, ALL)
        got = dot(pick, x).astype(BF)
        for i in range(n):
            for t in range(4):
                blocks[i][t * TOK : (t + 1) * TOK, hh * WIDTH : (hh + 1) * WIDTH] = got[
                    i * TOK : (i + 1) * TOK, t * WIDTH : (t + 1) * WIDTH
                ]


def join_kernel(place_ref, *refs):
    blocks, outs = refs[:ZN], refs[ZN:]
    z = place_ref[0]
    for d in range(ZN):
        cols = pl.ds(pl.multiple_of(((z + d) & (ZN - 1)) * PAIR, PAIR), PAIR)
        for t in range(4):
            outs[t][:, cols] = blocks[d][t * TOK : (t + 1) * TOK, :]


def exchange(array, groups):
    return lax.all_to_all(
        array, "seq", split_axis=0, concat_axis=0, axis_index_groups=groups, tiled=True
    )


def shift_owner(value, by):
    pairs = []
    for base in range(0, ZN * PLANE, RANGES):
        pairs += [(base + i, base + i + by) for i in range(RANGES) if 0 <= i + by < RANGES]
    return lax.ppermute(value, "seq", pairs)


def body(queries, keys, values, out_grad, cluster_ids):
    index = lax.axis_index("seq")
    place = jnp.stack([index // PLANE, index % PLANE, index % RANGES]).astype(I32)
    blocks = call(
        prep_kernel,
        [place, queries, keys, values, out_grad],
        [out((4 * TOK, PAIR), BF)] * ZN,
        specs=SMEM,
    )
    moved = {0: blocks[0]}
    for chunk in CHUNKS:
        for d in chunk:
            if d:
                moved[d] = lax.ppermute(blocks[d], "seq", z_pairs(d))
    ids = exchange(cluster_ids.T, LINES).reshape(ZN, HPZ, TOK)
    code, tile = call(
        meta_kernel,
        [ids],
        [out((HPZ, ZN, TOK), I32), out((HPZ, TILE, ALL), BF)],
        flops=10**8,
    )
    ranks = None
    placed = None
    for i, chunk in enumerate(CHUNKS):
        n = len(chunk)
        rows = n * MOST
        first = i == 0
        extra = TILE if first else 0
        (send,) = call(
            functools.partial(pack_kernel, chunk, first),
            [place, code] + [moved[d] for d in chunk] + ([tile] if first else []),
            [out((PLANE, rows + extra, ALL), BF)],
            [pltpu.VMEM((n * TOK, ALL), BF)],
            flops=2 * PLANE * rows * n * TOK * ALL,
            specs=SMEM,
        )
        got = exchange(send, PLANES)
        if first:
            ranks = call(
                rank_kernel,
                [place, got],
                [out((PLANE, len(c) * MOST), I32) for c in CHUNKS],
                [pltpu.VMEM((ZN * PLANE, 128), F32)] * 2,
                flops=10**8,
                specs={
                    0: SMEM[0],
                    1: pl.BlockSpec((PLANE, TILE, RANGES * STRIDE), lambda i: (0, rows // TILE, 0)),
                },
                grid=(1,),
            )
            ranks = [r.reshape(1, -1) for r in ranks]
        last = i == len(CHUNKS) - 1
        outs = [out((SPANS, SPAN, ALL), BF)]
        if last:
            outs += [out((SPAN, PAIR), BF), out((SPAN, ALL), BF)]
        placed = call(
            functools.partial(place_kernel, rows, last),
            [ranks[i], got] + ([placed[0]] if last else []),
            outs,
            [pltpu.VMEM((PLANE * rows, ALL), BF)],
            flops=2 * BLOCK * PLANE * rows * ALL,
        )
    rows_in, tail, head = placed
    tail = shift_owner(tail, 1)
    head = shift_owner(head, -1)
    main, part = call(
        main_kernel,
        [rows_in],
        [out((SPANS, SPAN, ALL), BF), out((2, SPAN, PAIR), F32)],
        [pltpu.VMEM((SPANS, SPAN, PAIR), F32)],
        flops=14 * SPANS * SPAN * 2 * SPAN * WIDTH,
    )
    span_spec = lambda c: pl.BlockSpec((1, SPAN, ALL), lambda i: (c, 0, 0))
    o = None
    back = {}
    for chunk, rank in reversed(list(zip(CHUNKS, ranks))):
        rows = len(chunk) * MOST
        send_shape = out((PLANE, rows, ALL), BF)
        flops = 2 * BLOCK * PLANE * rows * ALL
        if o is None:
            o, send = call(
                edge_kernel,
                [place, rank, rows_in, rows_in, tail, head, main, part],
                [out((BLOCK, ALL), BF), send_shape],
                flops=flops,
                specs={0: SMEM[0], 2: span_spec(0), 3: span_spec(SPANS - 1)},
                grid=(1,),
            )
        else:
            (send,) = call(pick_kernel, [rank, o], [send_shape], flops=flops)
        got = exchange(send, PLANES)
        pieces = call(
            functools.partial(unpack_kernel, chunk),
            [place, code, got],
            [out((4 * TOK, PAIR), BF)] * len(chunk),
            flops=4 * RANGES * rows * len(chunk) * TOK * ALL,
            specs=SMEM,
        )
        for d, piece in zip(chunk, pieces):
            back[d] = lax.ppermute(piece, "seq", z_pairs(-d)) if d else piece
    return call(
        join_kernel,
        [place] + [back[d] for d in range(ZN)],
        [out((TOK, ZN * PAIR), BF)] * 4,
        specs=SMEM,
    )


def solution(mesh):
    spec = P("seq", "head")
    return jax.shard_map(
        body,
        mesh=mesh,
        in_specs=(spec,) * 5,
        out_specs=(spec,) * 4,
        check_vma=False,
    )
```

profile of v0, /device:TPU:1, one launch (start us, length us, event | category | flops | bytes accessed | tf_op | source)
XLA Modules:
  0.0 218.0 jit_solution(14797149111761182358)
XLA Ops:
  0.7 1.0 copy-done.1
  1.8 1.0 copy-done.2
  2.8 1.0 copy-done.3
  3.9 1.0 copy-done.4
  4.9 0.8 shard_map.85
  5.8 2.5 %collective-permute-start = (bf16[512,256]{1,0:T(8,128)(2,1)S(1)}, bf16[512,256]{1,0:T(8,128)(2,1)S(1)}, u32[]{:S(2)}, u32[]{:S(2)}) collective-permute-start(bf16[512,256]{1,0:T(8,128)(2,1)S(1)} %get-tuple-element.33), channel_id=1, source_target_pairs={{0,32},{2,34},{4,36},{6,38},{8,40},{10,42},{12,44},{14,46},{16,48}... | collective-permute-start | bytes 786440 | tf_op jit(solution)/shard_map/ppermute | solution.py:360
  8.3 4.0 %collective-permute-start.1 = (bf16[512,256]{1,0:T(8,128)(2,1)S(1)}, bf16[512,256]{1,0:T(8,128)(2,1)S(1)}, u32[]{:S(2)}, u32[]{:S(2)}) collective-permute-start(bf16[512,256]{1,0:T(8,128)(2,1)S(1)} %get-tuple-element.34), channel_id=1, source_target_pairs={{0,224},{2,226},{4,228},{6,230},{8,232},{10,234},{12,236},{14,238}... | collective-permute-start | bytes 786440 | tf_op jit(solution)/shard_map/ppermute | solution.py:360
  12.3 3.9 %collective-permute-start.2 = (bf16[512,256]{1,0:T(8,128)(2,1)S(1)}, bf16[512,256]{1,0:T(8,128)(2,1)S(1)}, u32[]{:S(2)}, u32[]{:S(2)}) collective-permute-start(bf16[512,256]{1,0:T(8,128)(2,1)S(1)} %get-tuple-element.35), channel_id=1, source_target_pairs={{0,128},{2,130},{4,132},{6,134},{8,136},{10,138},{12,140},{14,142}... | collective-permute-start | bytes 786440 | tf_op jit(solution)/shard_map/ppermute | solution.py:360
  16.2 14.7 %all_to_all.29.ids_ref = s32[8,2,128]{2,1,0:T(2,128)S(1)} all-to-all(s32[8,2,128]{2,1,0:T(2,128)S(1)} %bitcast.6), channel_id=1, replica_groups={{0,32,64,96,128,160,192,224},{2,34,66,98,130,162,194,226},{4,36,68,100,..., dimensions={0} | all-to-all | bytes 16384 | tf_op jit(solution)/shard_map/all_to_all | solution.py:335
  30.9 0.8 shard_map.84
  31.7 2.2 %shard_map.86 = bf16[16,112,512]{2,1,0:T(8,128)(2,1)S(1)} custom-call(s32[3]{0:T(128)S(1)} %pad_add_fusion.place_ref, s32[2,8,128]{2,1,0:T(8,128)S(1)} %get-tuple-element.31.code_ref, bf16[512,256]{1,0:T(8,128)(2,1)S(1)} %get-tuple-element.32.refs_0_, bf16[512,256]{1,0:T(8,128)(2,1)S(1)} %collective-permute-done.refs_1_, ...), custom_call_target="tpu_custom_call" | custom-call | flops 805306368 | bytes 2924556 | tf_op jit(solution)/shard_map/pallas_call | solution.py:53
  33.9 1.2 copy-done
  35.2 6.7 %all-to-all-start.1 = ((bf16[16,112,512]{2,1,0:T(8,128)(2,1)}), bf16[16,112,512]{2,1,0:T(8,128)(2,1)S(1)}, u32[]{:S(2)}, u32[]{:S(2)}) async-start(bf16[16,112,512]{2,1,0:T(8,128)(2,1)} %copy-done), calls=%async_computation.1 | async-start | bytes 3670016 | tf_op jit(solution)/shard_map/all_to_all | solution.py:335
  42.3 3.3 %collective-permute-start.4 = (bf16[512,256]{1,0:T(8,128)(2,1)S(1)}, bf16[512,256]{1,0:T(8,128)(2,1)S(1)}, u32[]{:S(2)}, u32[]{:S(2)}) collective-permute-start(bf16[512,256]{1,0:T(8,128)(2,1)S(1)} %get-tuple-element.40), channel_id=1, source_target_pairs={{0,192},{2,194},{4,196},{6,198},{8,200},{10,202},{12,204},{14,206}... | collective-permute-start | bytes 786440 | tf_op jit(solution)/shard_map/ppermute | solution.py:360
  45.6 1.3 collective-permute-start.5
  46.9 3.1 %collective-permute-start.6 = (bf16[512,256]{1,0:T(8,128)(2,1)S(1)}, bf16[512,256]{1,0:T(8,128)(2,1)S(1)}, u32[]{:S(2)}, u32[]{:S(2)}) collective-permute-start(bf16[512,256]{1,0:T(8,128)(2,1)S(1)} %get-tuple-element.42), channel_id=1, source_target_pairs={{0,160},{2,162},{4,164},{6,166},{8,168},{10,170},{12,172},{14,174}... | collective-permute-start | bytes 786440 | tf_op jit(solution)/shard_map/ppermute | solution.py:360
  50.1 2.3 %collective-permute-done.3.refs_0_ = bf16[512,256]{1,0:T(8,128)(2,1)S(1)} collective-permute-done((bf16[512,256]{1,0:T(8,128)(2,1)S(1)}, bf16[512,256]{1,0:T(8,128)(2,1)S(1)}, u32[]{:S(2)}, u32[]{:S(2)}) %collective-permute-start.3) | collective-permute-done | bytes 262176 | tf_op jit(solution)/shard_map/ppermute | solution.py:360
  52.3 3.9 %collective-permute-done.4.refs_1_ = bf16[512,256]{1,0:T(8,128)(2,1)S(1)} collective-permute-done((bf16[512,256]{1,0:T(8,128)(2,1)S(1)}, bf16[512,256]{1,0:T(8,128)(2,1)S(1)}, u32[]{:S(2)}, u32[]{:S(2)}) %collective-permute-start.4) | collective-permute-done | bytes 262176 | tf_op jit(solution)/shard_map/ppermute | solution.py:360
  56.3 18.7 %collective-permute-done.5.refs_2_ = bf16[512,256]{1,0:T(8,128)(2,1)S(1)} collective-permute-done((bf16[512,256]{1,0:T(8,128)(2,1)S(1)}, bf16[512,256]{1,0:T(8,128)(2,1)S(1)}, u32[]{:S(2)}, u32[]{:S(2)}) %collective-permute-start.5) | collective-permute-done | bytes 262176 | tf_op jit(solution)/shard_map/ppermute | solution.py:360
  75.0 3.4 %shard_map.88 = bf16[16,96,512]{2,1,0:T(8,128)(2,1)} custom-call(s32[3]{0:T(128)S(1)} %pad_add_fusion.place_ref, s32[2,8,128]{2,1,0:T(8,128)S(1)} %get-tuple-element.31.code_ref, bf16[512,256]{1,0:T(8,128)(2,1)S(1)} %collective-permute-done.3.refs_0_, bf16[512,256]{1,0:T(8,128)(2,1)S(1)} %collective-permute-done.4.refs_1_, ...), custom_call_target="tpu_custom_call" | custom-call | flops 805306368 | bytes 2629644 | tf_op jit(solution)/shard_map/pallas_call | solution.py:53
  78.4 6.6 %all-to-all-start.2 = ((bf16[16,96,512]{2,1,0:T(8,128)(2,1)}), bf16[16,96,512]{2,1,0:T(8,128)(2,1)S(1)}, u32[]{:S(2)}, u32[]{:S(2)}) async-start(bf16[16,96,512]{2,1,0:T(8,128)(2,1)} %shard_map.88), calls=%async_computation.2 | async-start | bytes 3145728 | tf_op jit(solution)/shard_map/all_to_all | solution.py:335
  85.0 2.6 %shard_map.87 = (s32[16,96]{1,0:T(8,128)S(1)}, s32[16,96]{1,0:T(8,128)S(1)}) custom-call(s32[3]{0:T(128)S(1)} %pad_add_fusion.place_ref, bf16[16,112,512]{2,1,0:T(8,128)(2,1)S(1)} %all-to-all-done.1.tile_ref.recv_ref), custom_call_target="tpu_custom_call" | custom-call | flops 100000000 | bytes 1847308 | tf_op jit(solution)/shard_map/pallas_call | solution.py:53
  87.8 3.4 %shard_map.89.refs_0_ = bf16[8,256,512]{2,1,0:T(8,128)(2,1)S(1)} custom-call(s32[1,1536]{1,0:T(1,128)S(1)} %reshape.18.rank_ref, bf16[16,112,512]{2,1,0:T(8,128)(2,1)S(1)} %all-to-all-done.1.tile_ref.recv_ref), custom_call_target="tpu_custom_call" | custom-call | flops 3221225472 | bytes 3938304 | tf_op jit(solution)/shard_map/pallas_call | solution.py:53
  91.2 1.4 copy-done.9
  92.6 12.9 %all-to-all-done.2.recv_ref = bf16[16,96,512]{2,1,0:T(8,128)(2,1)S(1)} async-done(((bf16[16,96,512]{2,1,0:T(8,128)(2,1)}), bf16[16,96,512]{2,1,0:T(8,128)(2,1)S(1)}, u32[]{:S(2)}, u32[]{:S(2)}) %all-to-all-start.2) | async-done | bytes 1572896 | tf_op jit(solution)/shard_map/all_to_all | solution.py:335
  105.5 1.6 copy-done.10
  107.1 3.4 %shard_map.90 = (bf16[8,256,512]{2,1,0:T(8,128)(2,1)S(1)}, bf16[256,256]{1,0:T(8,128)(2,1)S(1)}, bf16[256,512]{1,0:T(8,128)(2,1)S(1)}) custom-call(s32[1,1536]{1,0:T(1,128)S(1)} %reshape.19.rank_ref, bf16[16,96,512]{2,1,0:T(8,128)(2,1)S(1)} %all-to-all-done.2.recv_ref, bf16[8,256,512]{2,1,0:T(8,128)(2,1)S(1)} %copy-done.10), custom_call_target="tpu_custom_call" | custom-call | flops 3221225472 | bytes 6166528 | tf_op jit(solution)/shard_map/pallas_call | solution.py:53
  110.6 1.3 collective-permute-start.8
  111.9 4.0 %collective-permute-start.7 = (bf16[256,256]{1,0:T(8,128)(2,1)S(1)}, bf16[256,256]{1,0:T(8,128)(2,1)S(1)}, u32[]{:S(2)}, u32[]{:S(2)}) collective-permute-start(bf16[256,256]{1,0:T(8,128)(2,1)S(1)} %get-tuple-element.44), channel_id=1, source_target_pairs={{0,2},{2,4},{4,6},{6,8},{8,10},{10,12},{12,14},{16,18},{18,20},{20... | collective-permute-start | bytes 393224 | tf_op jit(solution)/shard_map/ppermute | solution.py:344
  115.9 7.5 %shard_map.91 = (bf16[8,256,512]{2,1,0:T(8,128)(2,1)S(1)}, f32[2,256,256]{2,1,0:T(8,128)S(1)}) custom-call(bf16[8,256,512]{2,1,0:T(8,128)(2,1)S(1)} %get-tuple-element.43.in_ref.last_ref), custom_call_target="tpu_custom_call" | custom-call | flops 1879048192 | bytes 4718592 | tf_op jit(solution)/shard_map/pallas_call | solution.py:53
  123.4 1.3 copy-done.6
  124.8 8.0 %shard_map.92 = (bf16[2048,512]{1,0:T(8,128)(2,1)S(1)}, bf16[16,96,512]{2,1,0:T(8,128)(2,1)}) custom-call(s32[3]{0:T(128)S(1)} %pad_add_fusion.place_ref, s32[1,1536]{1,0:T(1,128)S(1)} %reshape.19.rank_ref, bf16[8,256,512]{2,1,0:T(8,128)(2,1)} %copy-done.5, bf16[8,256,512]{2,1,0:T(8,128)(2,1)} %copy-done.5, ...), custom_call_target="tpu_custom_call" | custom-call | flops 3221225472 | bytes 10885132 | tf_op jit(solution)/shard_map/pallas_call | solution.py:53
  132.8 1.4 copy-done.7
  134.1 6.4 %all-to-all-start.4 = ((bf16[16,96,512]{2,1,0:T(8,128)(2,1)}), bf16[16,96,512]{2,1,0:T(8,128)(2,1)S(1)}, u32[]{:S(2)}, u32[]{:S(2)}) async-start(bf16[16,96,512]{2,1,0:T(8,128)(2,1)} %get-tuple-element.51), calls=%async_computation.4 | async-start | bytes 3145728 | tf_op jit(solution)/shard_map/all_to_all | solution.py:335
  140.6 1.6 copy-done.8
  142.2 4.9 %shard_map.93 = bf16[16,96,512]{2,1,0:T(8,128)(2,1)} custom-call(s32[1,1536]{1,0:T(1,128)S(1)} %reshape.18.rank_ref, bf16[2048,512]{1,0:T(8,128)(2,1)S(1)} %copy-done.8), custom_call_target="tpu_custom_call" | custom-call | flops 3221225472 | bytes 3676160 | tf_op jit(solution)/shard_map/pallas_call | solution.py:53
  147.1 12.5 %all-to-all-done.4.recv_ref = bf16[16,96,512]{2,1,0:T(8,128)(2,1)S(1)} async-done(((bf16[16,96,512]{2,1,0:T(8,128)(2,1)}), bf16[16,96,512]{2,1,0:T(8,128)(2,1)S(1)}, u32[]{:S(2)}, u32[]{:S(2)}) %all-to-all-start.4) | async-done | bytes 1572896 | tf_op jit(solution)/shard_map/all_to_all | solution.py:335
  159.6 6.4 %all-to-all-start.3 = ((bf16[16,96,512]{2,1,0:T(8,128)(2,1)}), bf16[16,96,512]{2,1,0:T(8,128)(2,1)S(1)}, u32[]{:S(2)}, u32[]{:S(2)}) async-start(bf16[16,96,512]{2,1,0:T(8,128)(2,1)} %shard_map.93), calls=%async_computation.3 | async-start | bytes 3145728 | tf_op jit(solution)/shard_map/all_to_all | solution.py:335
  165.9 2.6 %shard_map.95 = (bf16[512,256]{1,0:T(8,128)(2,1)}, bf16[512,256]{1,0:T(8,128)(2,1)S(1)}, bf16[512,256]{1,0:T(8,128)(2,1)}, bf16[512,256]{1,0:T(8,128)(2,1)}) custom-call(s32[3]{0:T(128)S(1)} %pad_add_fusion.place_ref, s32[2,8,128]{2,1,0:T(8,128)S(1)} %get-tuple-element.31.code_ref, bf16[16,96,512]{2,1,0:T(8,128)(2,1)S(1)} %all-to-all-done.4.recv_ref), custom_call_target="tpu_custom_call" | custom-call | flops 805306368 | bytes 2629644 | tf_op jit(solution)/shard_map/pallas_call | solution.py:53
  168.6 3.3 %collective-permute-start.13 = (bf16[512,256]{1,0:T(8,128)(2,1)}, bf16[512,256]{1,0:T(8,128)(2,1)S(1)}, u32[]{:S(2)}, u32[]{:S(2)}) collective-permute-start(bf16[512,256]{1,0:T(8,128)(2,1)} %get-tuple-element.55), channel_id=1, source_target_pairs={{0,96},{2,98},{4,100},{6,102},{8,104},{10,106},{12,108},{14,110},{... | collective-permute-start | bytes 786440 | tf_op jit(solution)/shard_map/ppermute | solution.py:446
  171.9 3.6 %collective-permute-start.14 = (bf16[512,256]{1,0:T(8,128)(2,1)S(1)}, bf16[512,256]{1,0:T(8,128)(2,1)S(1)}, u32[]{:S(2)}, u32[]{:S(2)}) collective-permute-start(bf16[512,256]{1,0:T(8,128)(2,1)S(1)} %get-tuple-element.56), channel_id=1, source_target_pairs={{0,64},{2,66},{4,68},{6,70},{8,72},{10,74},{12,76},{14,78},{16,80}... | collective-permute-start | bytes 786440 | tf_op jit(solution)/shard_map/ppermute | solution.py:446
  175.4 10.6 %all-to-all-done.3.recv_ref = bf16[16,96,512]{2,1,0:T(8,128)(2,1)S(1)} async-done(((bf16[16,96,512]{2,1,0:T(8,128)(2,1)}), bf16[16,96,512]{2,1,0:T(8,128)(2,1)S(1)}, u32[]{:S(2)}, u32[]{:S(2)}) %all-to-all-start.3) | async-done | bytes 1572896 | tf_op jit(solution)/shard_map/all_to_all | solution.py:335
  186.0 1.9 shard_map.94
  188.5 7.9 %collective-permute-start.15 = (bf16[512,256]{1,0:T(8,128)(2,1)S(1)}, bf16[512,256]{1,0:T(8,128)(2,1)S(1)}, u32[]{:S(2)}, u32[]{:S(2)}) collective-permute-start(bf16[512,256]{1,0:T(8,128)(2,1)S(1)} %get-tuple-element.57), channel_id=1, source_target_pairs={{0,32},{2,34},{4,36},{6,38},{8,40},{10,42},{12,44},{14,46},{16,48}... | collective-permute-start | bytes 786440 | tf_op jit(solution)/shard_map/ppermute | solution.py:446
  196.4 3.0 %collective-permute-done.14.refs_6_ = bf16[512,256]{1,0:T(8,128)(2,1)S(1)} collective-permute-done((bf16[512,256]{1,0:T(8,128)(2,1)S(1)}, bf16[512,256]{1,0:T(8,128)(2,1)S(1)}, u32[]{:S(2)}, u32[]{:S(2)}) %collective-permute-start.14) | collective-permute-done | bytes 262176 | tf_op jit(solution)/shard_map/ppermute | solution.py:446
  199.4 11.1 %collective-permute-done.12.refs_4_ = bf16[512,256]{1,0:T(8,128)(2,1)S(1)} collective-permute-done((bf16[512,256]{1,0:T(8,128)(2,1)S(1)}, bf16[512,256]{1,0:T(8,128)(2,1)S(1)}, u32[]{:S(2)}, u32[]{:S(2)}) %collective-permute-start.12) | collective-permute-done | bytes 262176 | tf_op jit(solution)/shard_map/ppermute | solution.py:446
  210.5 5.4 %collective-permute-done.15.refs_7_ = bf16[512,256]{1,0:T(8,128)(2,1)S(1)} collective-permute-done((bf16[512,256]{1,0:T(8,128)(2,1)S(1)}, bf16[512,256]{1,0:T(8,128)(2,1)S(1)}, u32[]{:S(2)}, u32[]{:S(2)}) %collective-permute-start.15) | collective-permute-done | bytes 262176 | tf_op jit(solution)/shard_map/ppermute | solution.py:446
  215.9 2.1 shard_map.96
  (33 shorter events, 1.3 us)
Async XLA Ops:
  0.6 15.6 %copy-start.11 = (s32[128,16]{0,1:T(8,128)S(1)}, s32[128,16]{0,1:T(8,128)}, u32[]{:S(2)}) copy-start(s32[128,16]{0,1:T(8,128)} %param.9) | copy-start | bytes 24580
  0.7 1.0 copy-start.1
  1.8 1.0 copy-start.2
  2.8 1.0 copy-start.3
  3.9 1.0 copy-start.4
  5.8 26.0 %collective-permute-start = (bf16[512,256]{1,0:T(8,128)(2,1)S(1)}, bf16[512,256]{1,0:T(8,128)(2,1)S(1)}, u32[]{:S(2)}, u32[]{:S(2)}) collective-permute-start(bf16[512,256]{1,0:T(8,128)(2,1)S(1)} %get-tuple-element.33), channel_id=1, source_target_pairs={{0,32},{2,34},{4,36},{6,38},{8,40},{10,42},{12,44},{14,46},{16,48}... | collective-permute-start | bytes 786440 | tf_op jit(solution)/shard_map/ppermute | solution.py:360
  8.3 23.4 %collective-permute-start.1 = (bf16[512,256]{1,0:T(8,128)(2,1)S(1)}, bf16[512,256]{1,0:T(8,128)(2,1)S(1)}, u32[]{:S(2)}, u32[]{:S(2)}) collective-permute-start(bf16[512,256]{1,0:T(8,128)(2,1)S(1)} %get-tuple-element.34), channel_id=1, source_target_pairs={{0,224},{2,226},{4,228},{6,230},{8,232},{10,234},{12,236},{14,238}... | collective-permute-start | bytes 786440 | tf_op jit(solution)/shard_map/ppermute | solution.py:360
  12.3 19.4 %collective-permute-start.2 = (bf16[512,256]{1,0:T(8,128)(2,1)S(1)}, bf16[512,256]{1,0:T(8,128)(2,1)S(1)}, u32[]{:S(2)}, u32[]{:S(2)}) collective-permute-start(bf16[512,256]{1,0:T(8,128)(2,1)S(1)} %get-tuple-element.35), channel_id=1, source_target_pairs={{0,128},{2,130},{4,132},{6,134},{8,136},{10,138},{12,140},{14,142}... | collective-permute-start | bytes 786440 | tf_op jit(solution)/shard_map/ppermute | solution.py:360
  33.9 1.3 copy-start
  35.2 43.2 %all-to-all-start.1 = ((bf16[16,112,512]{2,1,0:T(8,128)(2,1)}), bf16[16,112,512]{2,1,0:T(8,128)(2,1)S(1)}, u32[]{:S(2)}, u32[]{:S(2)}) async-start(bf16[16,112,512]{2,1,0:T(8,128)(2,1)} %copy-done), calls=%async_computation.1 | async-start | bytes 3670016 | tf_op jit(solution)/shard_map/all_to_all | solution.py:335
  41.9 10.4 %collective-permute-start.3 = (bf16[512,256]{1,0:T(8,128)(2,1)S(1)}, bf16[512,256]{1,0:T(8,128)(2,1)S(1)}, u32[]{:S(2)}, u32[]{:S(2)}) collective-permute-start(bf16[512,256]{1,0:T(8,128)(2,1)S(1)} %get-tuple-element.39), channel_id=1, source_target_pairs={{0,64},{2,66},{4,68},{6,70},{8,72},{10,74},{12,76},{14,78},{16,80}... | collective-permute-start | bytes 786440 | tf_op jit(solution)/shard_map/ppermute | solution.py:360
  42.3 14.0 %collective-permute-start.4 = (bf16[512,256]{1,0:T(8,128)(2,1)S(1)}, bf16[512,256]{1,0:T(8,128)(2,1)S(1)}, u32[]{:S(2)}, u32[]{:S(2)}) collective-permute-start(bf16[512,256]{1,0:T(8,128)(2,1)S(1)} %get-tuple-element.40), channel_id=1, source_target_pairs={{0,192},{2,194},{4,196},{6,198},{8,200},{10,202},{12,204},{14,206}... | collective-permute-start | bytes 786440 | tf_op jit(solution)/shard_map/ppermute | solution.py:360
  45.6 29.4 %collective-permute-start.5 = (bf16[512,256]{1,0:T(8,128)(2,1)S(1)}, bf16[512,256]{1,0:T(8,128)(2,1)S(1)}, u32[]{:S(2)}, u32[]{:S(2)}) collective-permute-start(bf16[512,256]{1,0:T(8,128)(2,1)S(1)} %get-tuple-element.41), channel_id=1, source_target_pairs={{0,96},{2,98},{4,100},{6,102},{8,104},{10,106},{12,108},{14,110},{... | collective-permute-start | bytes 786440 | tf_op jit(solution)/shard_map/ppermute | solution.py:360
  46.9 28.1 %collective-permute-start.6 = (bf16[512,256]{1,0:T(8,128)(2,1)S(1)}, bf16[512,256]{1,0:T(8,128)(2,1)S(1)}, u32[]{:S(2)}, u32[]{:S(2)}) collective-permute-start(bf16[512,256]{1,0:T(8,128)(2,1)S(1)} %get-tuple-element.42), channel_id=1, source_target_pairs={{0,160},{2,162},{4,164},{6,166},{8,168},{10,170},{12,172},{14,174}... | collective-permute-start | bytes 786440 | tf_op jit(solution)/shard_map/ppermute | solution.py:360
  78.4 27.2 %all-to-all-start.2 = ((bf16[16,96,512]{2,1,0:T(8,128)(2,1)}), bf16[16,96,512]{2,1,0:T(8,128)(2,1)S(1)}, u32[]{:S(2)}, u32[]{:S(2)}) async-start(bf16[16,96,512]{2,1,0:T(8,128)(2,1)} %shard_map.88), calls=%async_computation.2 | async-start | bytes 3145728 | tf_op jit(solution)/shard_map/all_to_all | solution.py:335
  91.2 1.4 copy-start.9
  105.5 1.6 copy-start.10
  110.6 12.9 %copy-start.5 = (bf16[8,256,512]{2,1,0:T(8,128)(2,1)}, bf16[8,256,512]{2,1,0:T(8,128)(2,1)S(1)}, u32[]{:S(2)}) copy-start(bf16[8,256,512]{2,1,0:T(8,128)(2,1)S(1)} %get-tuple-element.43.in_ref.last_ref) | copy-start | bytes 6291460
  110.6 14.2 %collective-permute-start.8 = (bf16[256,512]{1,0:T(8,128)(2,1)S(1)}, bf16[256,512]{1,0:T(8,128)(2,1)S(1)}, u32[]{:S(2)}, u32[]{:S(2)}) collective-permute-start(bf16[256,512]{1,0:T(8,128)(2,1)S(1)} %get-tuple-element.45), channel_id=1, source_target_pairs={{2,0},{4,2},{6,4},{8,6},{10,8},{12,10},{14,12},{18,16},{20,18},{22... | collective-permute-start | bytes 786440 | tf_op jit(solution)/shard_map/ppermute | solution.py:344
  111.9 12.9 %collective-permute-start.7 = (bf16[256,256]{1,0:T(8,128)(2,1)S(1)}, bf16[256,256]{1,0:T(8,128)(2,1)S(1)}, u32[]{:S(2)}, u32[]{:S(2)}) collective-permute-start(bf16[256,256]{1,0:T(8,128)(2,1)S(1)} %get-tuple-element.44), channel_id=1, source_target_pairs={{0,2},{2,4},{4,6},{6,8},{8,10},{10,12},{12,14},{16,18},{18,20},{20... | collective-permute-start | bytes 393224 | tf_op jit(solution)/shard_map/ppermute | solution.py:344
  123.4 1.3 copy-start.6
  132.8 1.4 copy-start.7
  134.1 25.4 %all-to-all-start.4 = ((bf16[16,96,512]{2,1,0:T(8,128)(2,1)}), bf16[16,96,512]{2,1,0:T(8,128)(2,1)S(1)}, u32[]{:S(2)}, u32[]{:S(2)}) async-start(bf16[16,96,512]{2,1,0:T(8,128)(2,1)} %get-tuple-element.51), calls=%async_computation.4 | async-start | bytes 3145728 | tf_op jit(solution)/shard_map/all_to_all | solution.py:335
  140.6 1.6 copy-start.8
  159.6 26.4 %all-to-all-start.3 = ((bf16[16,96,512]{2,1,0:T(8,128)(2,1)}), bf16[16,96,512]{2,1,0:T(8,128)(2,1)S(1)}, u32[]{:S(2)}, u32[]{:S(2)}) async-start(bf16[16,96,512]{2,1,0:T(8,128)(2,1)} %shard_map.93), calls=%async_computation.3 | async-start | bytes 3145728 | tf_op jit(solution)/shard_map/all_to_all | solution.py:335
  168.6 19.4 %collective-permute-start.10 = (bf16[512,256]{1,0:T(8,128)(2,1)}, bf16[512,256]{1,0:T(8,128)(2,1)S(1)}, u32[]{:S(2)}, u32[]{:S(2)}) collective-permute-start(bf16[512,256]{1,0:T(8,128)(2,1)} %get-tuple-element.52), channel_id=1, source_target_pairs={{0,192},{2,194},{4,196},{6,198},{8,200},{10,202},{12,204},{14,206}... | collective-permute-start | bytes 786440 | tf_op jit(solution)/shard_map/ppermute | solution.py:446
  168.6 19.9 %collective-permute-start.11 = (bf16[512,256]{1,0:T(8,128)(2,1)}, bf16[512,256]{1,0:T(8,128)(2,1)S(1)}, u32[]{:S(2)}, u32[]{:S(2)}) collective-permute-start(bf16[512,256]{1,0:T(8,128)(2,1)} %get-tuple-element.53), channel_id=1, source_target_pairs={{0,160},{2,162},{4,164},{6,166},{8,168},{10,170},{12,172},{14,174}... | collective-permute-start | bytes 786440 | tf_op jit(solution)/shard_map/ppermute | solution.py:446
  168.6 27.8 %collective-permute-start.13 = (bf16[512,256]{1,0:T(8,128)(2,1)}, bf16[512,256]{1,0:T(8,128)(2,1)S(1)}, u32[]{:S(2)}, u32[]{:S(2)}) collective-permute-start(bf16[512,256]{1,0:T(8,128)(2,1)} %get-tuple-element.55), channel_id=1, source_target_pairs={{0,96},{2,98},{4,100},{6,102},{8,104},{10,106},{12,108},{14,110},{... | collective-permute-start | bytes 786440 | tf_op jit(solution)/shard_map/ppermute | solution.py:446
  171.9 27.5 %collective-permute-start.14 = (bf16[512,256]{1,0:T(8,128)(2,1)S(1)}, bf16[512,256]{1,0:T(8,128)(2,1)S(1)}, u32[]{:S(2)}, u32[]{:S(2)}) collective-permute-start(bf16[512,256]{1,0:T(8,128)(2,1)S(1)} %get-tuple-element.56), channel_id=1, source_target_pairs={{0,64},{2,66},{4,68},{6,70},{8,72},{10,74},{12,76},{14,78},{16,80}... | collective-permute-start | bytes 786440 | tf_op jit(solution)/shard_map/ppermute | solution.py:446
  187.9 11.5 %collective-permute-start.9 = (bf16[512,256]{1,0:T(8,128)(2,1)S(1)}, bf16[512,256]{1,0:T(8,128)(2,1)S(1)}, u32[]{:S(2)}, u32[]{:S(2)}) collective-permute-start(bf16[512,256]{1,0:T(8,128)(2,1)S(1)} %get-tuple-element.50), channel_id=1, source_target_pairs={{0,224},{2,226},{4,228},{6,230},{8,232},{10,234},{12,236},{14,238}... | collective-permute-start | bytes 786440 | tf_op jit(solution)/shard_map/ppermute | solution.py:446
  188.0 22.5 %collective-permute-start.12 = (bf16[512,256]{1,0:T(8,128)(2,1)S(1)}, bf16[512,256]{1,0:T(8,128)(2,1)S(1)}, u32[]{:S(2)}, u32[]{:S(2)}) collective-permute-start(bf16[512,256]{1,0:T(8,128)(2,1)S(1)} %get-tuple-element.54), channel_id=1, source_target_pairs={{0,128},{2,130},{4,132},{6,134},{8,136},{10,138},{12,140},{14,142}... | collective-permute-start | bytes 786440 | tf_op jit(solution)/shard_map/ppermute | solution.py:446
  188.5 27.4 %collective-permute-start.15 = (bf16[512,256]{1,0:T(8,128)(2,1)S(1)}, bf16[512,256]{1,0:T(8,128)(2,1)S(1)}, u32[]{:S(2)}, u32[]{:S(2)}) collective-permute-start(bf16[512,256]{1,0:T(8,128)(2,1)S(1)} %get-tuple-element.57), channel_id=1, source_target_pairs={{0,32},{2,34},{4,36},{6,38},{8,40},{10,42},{12,44},{14,46},{16,48}... | collective-permute-start | bytes 786440 | tf_op jit(solution)/shard_map/ppermute | solution.py:446
where the time goes:
time: 219 us; the launch traced here: 218 us
  waiting for transfers between devices  80.4 us (37%)
  starting transfers between devices  65.4 us (30%)
  Pallas kernels  43.7 us (20%)
  blocking collectives  14.7 us (7%)
  local copies, waits for them, and re-layouts  12.8 us (6%)
    pallas_call x13, Pallas kernels, call(): pl.pallas_call(kernel, out_shape=tuple(outs), grid=grid, in_specs=[specs....  43.7 us
    all_to_all x4, waiting for transfers between devices, exchange(): lax.all_to_all(array, 'seq', split_axis=0, concat_axis=0, axis_index_grou...  36 us
    all_to_all x4, starting transfers between devices, exchange(): lax.all_to_all(array, 'seq', split_axis=0, concat_axis=0, axis_index_grou...  26.2 us
    ppermute x7, waiting for transfers between devices, body(): moved[d] = lax.ppermute(blocks[d], 'seq', z_pairs(d))  24.9 us
    ppermute x7, waiting for transfers between devices, body(): back[d] = lax.ppermute(piece, 'seq', z_pairs(-d)) if d else piece  19.5 us
    ppermute x7, starting transfers between devices, body(): moved[d] = lax.ppermute(blocks[d], 'seq', z_pairs(d))  18.6 us
    ppermute x7, starting transfers between devices, body(): back[d] = lax.ppermute(piece, 'seq', z_pairs(-d)) if d else piece  15.4 us
    all_to_all x1, blocking collectives, exchange(): lax.all_to_all(array, 'seq', split_axis=0, concat_axis=0, axis_index_grou...  14.7 us
  transfers between devices with their start and end apart: 20, of which 9 were waited for; matrix products, arithmetic and copies ran while one was open for 0% of the time, Pallas kernels for 12%

commit v1 on v0

v1 whole, which is shorter than its diff:
```python
import functools
import math

import jax
import jax.numpy as jnp
from jax import lax
from jax.experimental import pallas as pl
from jax.experimental.pallas import tpu as pltpu
from jax.sharding import PartitionSpec as P

WIDTH = 128
SPAN = 256
CLUSTER_GROUP = 16
RANGES = 8
TOK = 128
MOST = 24
ZN = 8
PLANE = 16
HPZ = 2
ALL = 4 * WIDTH
PAIR = HPZ * WIDTH
STRIDE = 32
SLOTS = PLANE * ZN * MOST
BLOCK = 2048
SPANS = BLOCK // SPAN
TILE = 16
PICKS = 2
NONE = 4095
SCALING = 1.0 / math.sqrt(WIDTH)
BF = jnp.bfloat16
F32 = jnp.float32
I32 = jnp.int32

CHUNKS = ((0, 1, 7, 4), (2, 6, 3, 5))
PACK_HINT = (10**6, 10**11)
PLANES = [[z * PLANE + i for i in range(PLANE)] for z in range(ZN)]


def z_pairs(step):
    return [
        (z * PLANE + i, ((z + step) % ZN) * PLANE + i)
        for z in range(ZN)
        for i in range(PLANE)
    ]


def whole():
    return pl.BlockSpec(memory_space=pltpu.VMEM)


def call(kernel, ins, outs, scratch=(), flops=0, specs=None, out_specs=None, limit=28):
    size = sum(math.prod(o.shape) * o.dtype.itemsize for o in outs)
    size += sum(math.prod(a.shape) * a.dtype.itemsize for a in ins)
    specs = specs or {}
    return pl.pallas_call(
        kernel,
        out_shape=tuple(
            pltpu.HBM(o.shape, o.dtype) if i in (out_specs or {}) else o
            for i, o in enumerate(outs)
        ),
        in_specs=[specs.get(i) or whole() for i in range(len(ins))],
        out_specs=tuple((out_specs or {}).get(i) or whole() for i in range(len(outs))),
        scratch_shapes=list(scratch),
        cost_estimate=pl.CostEstimate(flops=flops, bytes_accessed=size, transcendentals=0),
        compiler_params=pltpu.CompilerParams(vmem_limit_bytes=limit * 1024 * 1024),
    )(*ins)


SMEM = {0: pl.BlockSpec(memory_space=pltpu.SMEM)}


def out(shape, dtype):
    return jax.ShapeDtypeStruct(shape, dtype)


def iota(shape, dim):
    return lax.broadcasted_iota(I32, shape, dim)


def one_hot(mask):
    return mask.astype(F32).astype(BF)


def row_to_col(row):
    eye = iota((128, 128), 0) == iota((128, 128), 1)
    parts = []
    for i in range(row.shape[1] // 128):
        piece = row[:, i * 128 : (i + 1) * 128]
        parts.append(jnp.sum(jnp.where(eye, piece, 0.0), axis=1, keepdims=True))
    return jnp.concatenate(parts, axis=0)


def dot(a, b, dims=((1,), (0,))):
    return lax.dot_general(a, b, (dims, ((), ())), preferred_element_type=F32)


NT = ((1,), (1,))
TN = ((0,), (0,))


def prep_kernel(place_ref, ids_ref, *refs):
    arrays, blocks, sems = refs[:4], refs[4 : 4 + ZN], refs[4 + ZN]
    z = place_ref[0]
    copies = []
    for d in range(ZN):
        cols = pl.ds(pl.multiple_of(((z + d) & (ZN - 1)) * PAIR, PAIR), PAIR)
        for t in range(4):
            copies.append(
                pltpu.make_async_copy(
                    arrays[t].at[:, cols],
                    blocks[d].at[t * TOK : (t + 1) * TOK, :],
                    sems.at[d * 4 + t],
                )
            )
    for copy in copies:
        copy.start()
    for d in range(ZN):
        at = ((z + d) & (ZN - 1)) * HPZ
        rows = [ids_ref[pl.ds(at + hh, 1), :] for hh in range(HPZ)]
        tile = jnp.concatenate(rows + [jnp.zeros((TILE - HPZ, TOK), I32)], axis=0)
        blocks[d][4 * TOK :, 0:TOK] = tile.astype(F32).astype(BF)
        blocks[d][4 * TOK :, TOK:] = jnp.zeros((TILE, PAIR - TOK), BF)
    for copy in copies:
        copy.wait()


def leave(stage_ref, out_ref, sems, i, n):
    size = PLANE // n
    part = slice(i * size, (i + 1) * size)
    return pltpu.make_async_copy(stage_ref.at[part], out_ref.at[part], sems.at[i])


def pack_kernel(chunk, *refs):
    n = len(chunk)
    blocks, (out_ref, code_ref, x_ref, send_ref, sems) = refs[:n], refs[-5:]
    rows = n * MOST
    ids = [blocks[i][4 * TOK :, 0:TOK].astype(F32) for i in range(n)]
    ids = jnp.concatenate(
        [ids[i][hh : hh + 1] for hh in range(HPZ) for i in range(n)], axis=0
    ).astype(I32)
    group = lax.shift_right_logical(ids, 4)
    local = ((ids & (CLUSTER_GROUP - 1)) + 1).astype(F32).astype(BF)
    tri = one_hot(iota((TOK, TOK), 0) < iota((TOK, TOK), 1))
    slot = jnp.zeros(ids.shape, F32)
    for b in range(RANGES):
        hot = (group == b).astype(F32)
        slot = slot + hot * dot(hot.astype(BF), tri)
    code = group * STRIDE + slot.astype(I32)
    code_ref[...] = code
    for hh in range(HPZ):
        for i in range(n):
            for t in range(4):
                x_ref[i * TOK : (i + 1) * TOK, t * WIDTH : (t + 1) * WIDTH] = blocks[i][
                    t * TOK : (t + 1) * TOK, hh * WIDTH : (hh + 1) * WIDTH
                ]
        mine = range(hh * n, (hh + 1) * n)
        position = jnp.concatenate(
            [(code[i : i + 1] & (STRIDE - 1)) + (i - hh * n) * MOST for i in mine], axis=1
        )
        owner = jnp.concatenate([group[i : i + 1] for i in mine], axis=1)
        value = jnp.concatenate([local[i : i + 1] for i in mine], axis=1)
        value = jnp.broadcast_to(value, (TILE, n * TOK))
        x = x_ref[...]
        for b in range(RANGES):
            target = jnp.where(owner == b, position, -1)
            pick = one_hot(target == iota((rows, n * TOK), 0))
            send_ref[hh * RANGES + b, 0:rows, :] = dot(pick, x).astype(BF)
            send_ref[hh * RANGES + b, rows:, 0:rows] = dot(value, pick, NT).astype(BF)
            send_ref[hh * RANGES + b, rows:, rows:] = jnp.zeros((TILE, ALL - rows), BF)
        leave(send_ref, out_ref, sems, hh, HPZ).start()
    for hh in range(HPZ):
        leave(send_ref, out_ref, sems, hh, HPZ).wait()


def rank_rows(z, clusters):
    lanes = ZN * MOST
    dist = sum(CHUNKS, ())

    def source(shape, dim):
        segment = iota(shape, dim) // MOST
        value = jnp.zeros(shape, I32)
        for i, d in enumerate(dist):
            value = jnp.where(segment == i, (z - d) & (ZN - 1), value)
        return value

    square = (lanes, lanes)
    from_z, to_z = source(square, 0), source(square, 1)
    same = from_z == to_z
    within = one_hot(same & (iota(square, 0) < iota(square, 1)))
    segment = one_hot(same)
    earlier = one_hot(from_z < to_z)
    hot = jnp.concatenate(
        [(clusters == float(c + 1)).astype(F32) for c in range(CLUSTER_GROUP)], axis=0
    )
    low = hot.astype(BF)
    side = CLUSTER_GROUP * PLANE
    row, col = iota((side, side), 0), iota((side, side), 1)
    row_c, col_c = lax.shift_right_logical(row, 4), lax.shift_right_logical(col, 4)
    before = one_hot((row_c == col_c) & (col < row))
    together = one_hot(row_c == col_c)
    lower = one_hot(col_c < row_c)
    total = dot(low, jnp.ones(square, BF))
    rank = (
        dot(low, within)
        + dot(before, dot(low, segment).astype(BF))
        + dot(together, dot(low, earlier).astype(BF))
        + dot(lower, total.astype(BF))
    )
    rank = jnp.sum((hot * rank).reshape(CLUSTER_GROUP, PLANE, lanes), axis=0)
    rank = jnp.where(clusters > 0.5, rank, float(NONE))
    return jnp.concatenate([rank[s : s + 1, :] for s in range(PLANE)], axis=1)


def place_kernel(place_ref, *refs):
    n = len(CHUNKS)
    recvs, (sorted_ref, tail_ref, head_ref, rank_ref, x_ref) = refs[:n], refs[n:]
    clusters = []
    at = 0
    for chunk, recv_ref in zip(CHUNKS, recvs):
        rows = len(chunk) * MOST
        clusters.append(
            jnp.concatenate(
                [recv_ref[s, rows:, 0:rows].astype(F32)[0:1] for s in range(PLANE)], axis=0
            )
        )
        for s in range(PLANE):
            x_ref[s * ZN * MOST + at : s * ZN * MOST + at + rows, :] = recv_ref[s, 0:rows, :]
        at += rows
    rank = rank_rows(place_ref[0], jnp.concatenate(clusters, axis=1)).astype(I32)
    rank_ref[...] = rank
    x = x_ref[...]
    step = 2
    for c in range(0, SPANS, step):
        pick = one_hot(rank == iota((step * SPAN, SLOTS), 0) + c * SPAN)
        sorted_ref[c : c + step] = dot(pick, x).astype(BF).reshape(step, SPAN, ALL)
    tail_ref[...] = sorted_ref[SPANS - 1, :, WIDTH : 3 * WIDTH]
    head_ref[...] = sorted_ref[0]


def span_math(q, g, k0, k1, v0, v1, keep):
    s0 = dot(q, k0, NT)
    s1 = dot(q, k1, NT)
    if keep is not None:
        s0 = jnp.where(keep, s0, -1e30)
    peak = jnp.maximum(
        jnp.max(s0, axis=1, keepdims=True), jnp.max(s1, axis=1, keepdims=True)
    )
    factor = SCALING * math.log2(math.e)
    p0 = jnp.exp2((s0 - peak) * factor)
    p1 = jnp.exp2((s1 - peak) * factor)
    inverse = 1.0 / (
        jnp.sum(p0, axis=1, keepdims=True) + jnp.sum(p1, axis=1, keepdims=True)
    )
    w0 = p0 * inverse
    w1 = p1 * inverse
    l0 = w0.astype(BF)
    l1 = w1.astype(BF)
    attended = (dot(l0, v0) + dot(l1, v1)).astype(BF)
    e0 = dot(g, v0, NT)
    e1 = dot(g, v1, NT)
    inner = jnp.sum(w0 * e0, axis=1, keepdims=True) + jnp.sum(w1 * e1, axis=1, keepdims=True)
    h0 = (w0 * (e0 - inner) * SCALING).astype(BF)
    h1 = (w1 * (e1 - inner) * SCALING).astype(BF)
    dq = (dot(h0, k0) + dot(h1, k1)).astype(BF)
    return attended, dq, dot(h0, q, TN), dot(h1, q, TN), dot(l0, g, TN), dot(l1, g, TN)


Q, K, V, G = (slice(t * WIDTH, (t + 1) * WIDTH) for t in range(4))


def main_kernel(in_ref, o_ref, part_ref, d_ref):
    d_ref[0] = jnp.zeros((SPAN, PAIR), F32)

    def one(c, carry):
        att, dq, dk0, dk1, dv0, dv1 = span_math(
            in_ref[c, :, Q], in_ref[c, :, G], in_ref[c - 1, :, K], in_ref[c, :, K],
            in_ref[c - 1, :, V], in_ref[c, :, V], None,
        )
        o_ref[c, :, Q] = att
        o_ref[c, :, K] = dq
        d_ref[c - 1, :, Q] += dk0
        d_ref[c - 1, :, K] += dv0
        d_ref[c, :, Q] = dk1
        d_ref[c, :, K] = dv1
        o_ref[c - 1, :, 2 * WIDTH :] = d_ref[c - 1].astype(BF)
        return carry

    lax.fori_loop(1, SPANS, one, 0)
    part_ref[0] = d_ref[0]
    part_ref[1] = d_ref[SPANS - 1]
    o_ref[0, :, 0 : 2 * WIDTH] = jnp.zeros((SPAN, 2 * WIDTH), BF)
    o_ref[SPANS - 1, :, 2 * WIDTH :] = jnp.zeros((SPAN, 2 * WIDTH), BF)


def pick_out(at, rank_ref, o, out_ref, send_ref, sems):
    col = row_to_col(rank_ref[...].astype(F32)).astype(I32)
    rows = send_ref.shape[1]
    step = PLANE // PICKS
    for p in range(PICKS):
        span = range(p * step, (p + 1) * step)
        part = jnp.concatenate(
            [col[i * ZN * MOST + at : i * ZN * MOST + at + rows, :] for i in span], axis=0
        )
        pick = one_hot(part == iota((step * rows, BLOCK), 1))
        send_ref[p * step : (p + 1) * step] = dot(pick, o).astype(BF).reshape(step, rows, ALL)
        leave(send_ref, out_ref, sems, p, PICKS).start()
    for p in range(PICKS):
        leave(send_ref, out_ref, sems, p, PICKS).wait()


def edge_kernel(
    at, place_ref, rank_ref, in_ref, tail_ref, head_ref, main_ref, part_ref,
    done_ref, out_ref, o_ref, send_ref, sems, done_sem,
):
    o_ref[SPAN:BLOCK, :] = main_ref[1:].reshape(BLOCK - SPAN, ALL)
    keep = jnp.broadcast_to(place_ref[1], (SPAN, SPAN)) > 0
    att, dq, _, dk1, _, dv1 = span_math(
        in_ref[0, :, Q], in_ref[0, :, G], tail_ref[:, Q], in_ref[0, :, K],
        tail_ref[:, K], in_ref[0, :, V], keep,
    )
    o_ref[0:SPAN, Q] = att
    o_ref[0:SPAN, K] = dq
    o_ref[0:SPAN, V] = (part_ref[0, :, Q] + dk1).astype(BF)
    o_ref[0:SPAN, G] = (part_ref[0, :, K] + dv1).astype(BF)
    end = SPANS - 1
    _, _, dk0, _, dv0, _ = span_math(
        head_ref[:, Q], head_ref[:, G], in_ref[end, :, K], head_ref[:, K],
        in_ref[end, :, V], head_ref[:, V], None,
    )
    o_ref[BLOCK - SPAN :, V] = (part_ref[1, :, Q] + dk0).astype(BF)
    o_ref[BLOCK - SPAN :, G] = (part_ref[1, :, K] + dv0).astype(BF)
    done = pltpu.make_async_copy(o_ref, done_ref, done_sem.at[0])
    done.start()
    pick_out(at, rank_ref, o_ref[...], out_ref, send_ref, sems)
    done.wait()


def pick_kernel(at, rank_ref, o_ref, out_ref, send_ref, sems):
    pick_out(at, rank_ref, o_ref[...], out_ref, send_ref, sems)


def unpack_kernel(chunk, code_ref, recv_ref, *blocks):
    n = len(chunk)
    rows = n * MOST
    code = code_ref[...]
    for hh in range(HPZ):
        cols = []
        for i in range(n):
            mine = code[hh * n + i : hh * n + i + 1]
            target = lax.shift_right_logical(mine, 5) * rows + (mine & (STRIDE - 1)) + i * MOST
            cols.append(row_to_col(target.astype(F32)).astype(I32))
        col = jnp.concatenate(cols, axis=0)
        pick = one_hot(col == iota((n * TOK, RANGES * rows), 1))
        x = recv_ref[hh * RANGES : (hh + 1) * RANGES].reshape(RANGES * rows, ALL)
        got = dot(pick, x).astype(BF)
        for i in range(n):
            for t in range(4):
                blocks[i][t * TOK : (t + 1) * TOK, hh * WIDTH : (hh + 1) * WIDTH] = got[
                    i * TOK : (i + 1) * TOK, t * WIDTH : (t + 1) * WIDTH
                ]


def join_kernel(place_ref, *refs):
    blocks, outs, sems = refs[:ZN], refs[ZN : ZN + 4], refs[ZN + 4]
    z = place_ref[0]
    copies = []
    for d in range(ZN):
        cols = pl.ds(pl.multiple_of(((z + d) & (ZN - 1)) * PAIR, PAIR), PAIR)
        for t in range(4):
            copies.append(
                pltpu.make_async_copy(
                    blocks[d].at[t * TOK : (t + 1) * TOK, :],
                    outs[t].at[:, cols],
                    sems.at[d * 4 + t],
                )
            )
    for copy in copies:
        copy.start()
    for copy in copies:
        copy.wait()


def exchange(array, groups):
    return lax.all_to_all(
        array, "seq", split_axis=0, concat_axis=0, axis_index_groups=groups, tiled=True
    )


def shift_owner(value, by):
    pairs = []
    for base in range(0, ZN * PLANE, RANGES):
        pairs += [(base + i, base + i + by) for i in range(RANGES) if 0 <= i + by < RANGES]
    return lax.ppermute(value, "seq", pairs)


def body(queries, keys, values, out_grad, cluster_ids):
    index = lax.axis_index("seq")
    place = jnp.stack([index // PLANE, index % RANGES]).astype(I32)
    hbm = pl.BlockSpec(memory_space=pltpu.HBM)
    blocks = call(
        prep_kernel,
        [place, cluster_ids.T, queries, keys, values, out_grad],
        [out((4 * TOK + TILE, PAIR), BF)] * ZN,
        [pltpu.SemaphoreType.DMA((4 * ZN,))],
        specs={0: SMEM[0], 2: hbm, 3: hbm, 4: hbm, 5: hbm},
        limit=60,
    )
    moved = {0: blocks[0]}
    for d in sum(CHUNKS, ()):
        if d:
            moved[d] = lax.ppermute(blocks[d], "seq", z_pairs(d))
    codes, arrived = [], []
    for i, chunk in enumerate(CHUNKS):
        n = len(chunk)
        rows = n * MOST
        send, code = call(
            functools.partial(pack_kernel, chunk),
            [moved[d] for d in chunk] + codes[-1:],
            [out((PLANE, rows + TILE, ALL), BF), out((HPZ * n, TOK), I32)],
            [
                pltpu.VMEM((n * TOK, ALL), BF),
                pltpu.VMEM((PLANE, rows + TILE, ALL), BF),
                pltpu.SemaphoreType.DMA((HPZ,)),
            ],
            flops=PACK_HINT[i],
            out_specs={0: hbm},
        )
        codes.append(code)
        arrived.append(exchange(send, PLANES))
    rows_in, tail, head, rank = call(
        place_kernel,
        [place] + arrived,
        [
            out((SPANS, SPAN, ALL), BF),
            out((SPAN, PAIR), BF),
            out((SPAN, ALL), BF),
            out((1, SLOTS), I32),
        ],
        [pltpu.VMEM((SLOTS, ALL), BF)],
        flops=2 * BLOCK * SLOTS * ALL,
        specs=SMEM,
    )
    tail = shift_owner(tail, 1)
    head = shift_owner(head, -1)
    main, part = call(
        main_kernel,
        [rows_in],
        [out((SPANS, SPAN, ALL), BF), out((2, SPAN, PAIR), F32)],
        [pltpu.VMEM((SPANS, SPAN, PAIR), F32)],
        flops=14 * SPANS * SPAN * 2 * SPAN * WIDTH,
    )
    o = None
    back = {}
    at = ZN * MOST
    for chunk, code in reversed(list(zip(CHUNKS, codes))):
        rows = len(chunk) * MOST
        at -= rows
        send_shape = out((PLANE, rows, ALL), BF)
        flops = 2 * BLOCK * PLANE * rows * ALL
        stage = [pltpu.VMEM((PLANE, rows, ALL), BF), pltpu.SemaphoreType.DMA((PICKS,))]
        if o is None:
            o, send = call(
                functools.partial(edge_kernel, at),
                [place, rank, rows_in, tail, head, main, part],
                [out((BLOCK, ALL), BF), send_shape],
                [pltpu.VMEM((BLOCK, ALL), BF)] + stage + [pltpu.SemaphoreType.DMA((1,))],
                flops=flops,
                specs=SMEM,
                out_specs={0: hbm, 1: hbm},
            )
        else:
            (send,) = call(
                functools.partial(pick_kernel, at),
                [rank, o],
                [send_shape],
                stage,
                flops=flops,
                out_specs={0: hbm},
            )
        got = exchange(send, PLANES)
        pieces = call(
            functools.partial(unpack_kernel, chunk),
            [code, got],
            [out((4 * TOK, PAIR), BF)] * len(chunk),
            flops=4 * RANGES * rows * len(chunk) * TOK * ALL,
        )
        for d, piece in zip(chunk, pieces):
            back[d] = lax.ppermute(piece, "seq", z_pairs(-d)) if d else piece
    return call(
        join_kernel,
        [place] + [back[d] for d in range(ZN)],
        [out((TOK, ZN * PAIR), BF)] * 4,
        [pltpu.SemaphoreType.DMA((4 * ZN,))],
        specs=SMEM,
        out_specs={i: hbm for i in range(4)},
    )


def solution(mesh):
    spec = P("seq", "head")
    return jax.shard_map(
        body,
        mesh=mesh,
        in_specs=(spec,) * 5,
        out_specs=(spec,) * 4,
        check_vma=False,
    )
```

time: 219 us -> 207 us (0.945)
  waiting for transfers between devices: 80.4 us -> 60.9 us
  blocking collectives: 14.7 us -> 26.3 us
  local copies, waits for them, and re-layouts: 12.8 us -> 2.54 us
  starting transfers between devices: 65.4 us -> 72 us
    all_to_all x4 -> x3, waiting for transfers between devices: 36 us -> 8.99 us  [exchange(): lax.all_to_all(array, 'seq', split_axis=0, concat_axis=0, axis_index_grou...]
    ppermute x7, starting transfers between devices: 15.4 us -> 32.9 us  [body(): back[d] = lax.ppermute(piece, 'seq', z_pairs(-d)) if d else piece]
    all_to_all x1, blocking collectives: 14.7 us -> 26.3 us  [exchange(): lax.all_to_all(array, 'seq', split_axis=0, concat_axis=0, axis_index_grou...]
    unnamed x24 -> x6, local copies, waits for them, and re-layouts: 12.6 us -> 2.54 us
    all_to_all x4 -> x3, starting transfers between devices: 26.2 us -> 17.7 us  [exchange(): lax.all_to_all(array, 'seq', split_axis=0, concat_axis=0, axis_index_grou...]
    ppermute x7, waiting for transfers between devices: 19.5 us -> 26.2 us  [body(): back[d] = lax.ppermute(piece, 'seq', z_pairs(-d)) if d else piece]
    ppermute x7, starting transfers between devices: 18.6 us -> 16.2 us  [body(): moved[d] = lax.ppermute(blocks[d], 'seq', z_pairs(d))]
    pallas_call x13 -> x10, Pallas kernels: 43.7 us -> 42.4 us  [call(): pl.pallas_call(kernel, out_shape=tuple((pltpu.HBM(o.shape, o.dtype) if i...]
  transfers between devices with their start and end apart: 20 -> 19, of which waited for: 9 -> 10; matrix products, arithmetic and copies ran while one was open for 0% -> 0% of each run, Pallas kernels for 12% -> 11%
where the time goes in v1:
time: 207 us; the launch traced here: 206 us
  starting transfers between devices  72 us (35%)
  waiting for transfers between devices  60.9 us (29%)
  Pallas kernels  42.4 us (20%)
  blocking collectives  26.3 us (13%)
  local copies, waits for them, and re-layouts  2.54 us (1%)
    pallas_call x10, Pallas kernels, call(): pl.pallas_call(kernel, out_shape=tuple((pltpu.HBM(o.shape, o.dtype) if i...  42.4 us
    ppermute x7, starting transfers between devices, body(): back[d] = lax.ppermute(piece, 'seq', z_pairs(-d)) if d else piece  32.9 us
    all_to_all x1, blocking collectives, exchange(): lax.all_to_all(array, 'seq', split_axis=0, concat_axis=0, axis_index_grou...  26.3 us
    ppermute x7, waiting for transfers between devices, body(): back[d] = lax.ppermute(piece, 'seq', z_pairs(-d)) if d else piece  26.2 us
    ppermute x7, waiting for transfers between devices, body(): moved[d] = lax.ppermute(blocks[d], 'seq', z_pairs(d))  25.6 us
    all_to_all x3, starting transfers between devices, exchange(): lax.all_to_all(array, 'seq', split_axis=0, concat_axis=0, axis_index_grou...  17.7 us
    ppermute x7, starting transfers between devices, body(): moved[d] = lax.ppermute(blocks[d], 'seq', z_pairs(d))  16.2 us
    all_to_all x3, waiting for transfers between devices, exchange(): lax.all_to_all(array, 'seq', split_axis=0, concat_axis=0, axis_index_grou...  8.99 us
  transfers between devices with their start and end apart: 19, of which 10 were waited for; matrix products, arithmetic and copies ran while one was open for 0% of the time, Pallas kernels for 11%

profile of v1, /device:TPU:1, one launch (start us, length us, event | category | flops | bytes accessed | tf_op | source)
XLA Modules:
  0.0 205.7 jit_solution(7463627949967875592)
XLA Ops:
  0.7 0.6 pad_add_fusion.place_ref
  1.3 3.9 %shard_map.84 = (bf16[528,256]{1,0:T(8,128)(2,1)}, bf16[528,256]{1,0:T(8,128)(2,1)}, bf16[528,256]{1,0:T(8,128)(2,1)}, bf16[528,256]{1,0:T(8,128)(2,1)}, bf16[52...) custom-call(s32[2]{0:T(128)} %pad_add_fusion.place_ref, ...), custom_call_target="tpu_custom_call" | custom-call | bytes 4268040 | tf_op jit(solution)/shard_map/pallas_call | solution.py:55
  5.2 2.5 %collective-permute-start = (bf16[528,256]{1,0:T(8,128)(2,1)}, bf16[528,256]{1,0:T(8,128)(2,1)S(1)}, u32[]{:S(2)}, u32[]{:S(2)}) collective-permute-start(bf16[528,256]{1,0:T(8,128)(2,1)} %get-tuple-element.33), channel_id=1, source_target_pairs={{0,32},{2,34},{4,36},{6,38},{8,40},{10,42},{12,44},{14,46},{16,48}... | collective-permute-start | bytes 811016 | tf_op jit(solution)/shard_map/ppermute | solution.py:411
  7.7 4.0 %collective-permute-start.1 = (bf16[528,256]{1,0:T(8,128)(2,1)}, bf16[528,256]{1,0:T(8,128)(2,1)S(1)}, u32[]{:S(2)}, u32[]{:S(2)}) collective-permute-start(bf16[528,256]{1,0:T(8,128)(2,1)} %get-tuple-element.34), channel_id=1, source_target_pairs={{0,224},{2,226},{4,228},{6,230},{8,232},{10,234},{12,236},{14,238}... | collective-permute-start | bytes 811016 | tf_op jit(solution)/shard_map/ppermute | solution.py:411
  11.8 3.9 %collective-permute-start.2 = (bf16[528,256]{1,0:T(8,128)(2,1)}, bf16[528,256]{1,0:T(8,128)(2,1)S(1)}, u32[]{:S(2)}, u32[]{:S(2)}) collective-permute-start(bf16[528,256]{1,0:T(8,128)(2,1)} %get-tuple-element.35), channel_id=1, source_target_pairs={{0,128},{2,130},{4,132},{6,134},{8,136},{10,138},{12,140},{14,142}... | collective-permute-start | bytes 811016 | tf_op jit(solution)/shard_map/ppermute | solution.py:411
  15.7 3.6 %collective-permute-start.4 = (bf16[528,256]{1,0:T(8,128)(2,1)}, bf16[528,256]{1,0:T(8,128)(2,1)S(1)}, u32[]{:S(2)}, u32[]{:S(2)}) collective-permute-start(bf16[528,256]{1,0:T(8,128)(2,1)} %get-tuple-element.39), channel_id=1, source_target_pairs={{0,192},{2,194},{4,196},{6,198},{8,200},{10,202},{12,204},{14,206}... | collective-permute-start | bytes 811016 | tf_op jit(solution)/shard_map/ppermute | solution.py:411
  19.3 0.2 collective-permute-start.5
  19.5 2.4 %collective-permute-done.1.refs_2_ = bf16[528,256]{1,0:T(8,128)(2,1)S(1)} collective-permute-done((bf16[528,256]{1,0:T(8,128)(2,1)}, bf16[528,256]{1,0:T(8,128)(2,1)S(1)}, u32[]{:S(2)}, u32[]{:S(2)}) %collective-permute-start.1) | collective-permute-done | bytes 270368 | tf_op jit(solution)/shard_map/ppermute | solution.py:411
  21.9 1.9 collective-permute-start.6
  23.7 4.7 %collective-permute-done.2.refs_3_ = bf16[528,256]{1,0:T(8,128)(2,1)S(1)} collective-permute-done((bf16[528,256]{1,0:T(8,128)(2,1)}, bf16[528,256]{1,0:T(8,128)(2,1)S(1)}, u32[]{:S(2)}, u32[]{:S(2)}) %collective-permute-start.2) | collective-permute-done | bytes 270368 | tf_op jit(solution)/shard_map/ppermute | solution.py:411
  28.4 1.0 copy-done
  29.4 3.1 %shard_map.85 = (bf16[16,112,512]{2,1,0:T(8,128)(2,1)}, s32[8,128]{1,0:T(8,128)S(1)}) custom-call(bf16[528,256]{1,0:T(8,128)(2,1)S(1)} %copy-done, bf16[528,256]{1,0:T(8,128)(2,1)S(1)} %collective-permute-done.refs_1_, bf16[528,256]{1,0:T(8,128)(2,1)S(1)} %collective-permute-done.1.refs_2_, bf16[528,256]{1,0:T(8,128)(2,1)S(1)} %collective-permute-done.2.refs_3_), custom_call_target="tpu_custom_call" | custom-call | flops 1000000 | bytes 2920448 | tf_op jit(solution)/shard_map/pallas_call | solution.py:55
  32.5 6.8 %all-to-all-start = ((bf16[16,112,512]{2,1,0:T(8,128)(2,1)}), bf16[16,112,512]{2,1,0:T(8,128)(2,1)S(1)}, u32[]{:S(2)}, u32[]{:S(2)}) async-start(bf16[16,112,512]{2,1,0:T(8,128)(2,1)} %get-tuple-element.37), calls=%async_computation | async-start | bytes 3670016 | tf_op jit(solution)/shard_map/all_to_all | solution.py:384
  39.2 0.0 collective-permute-done.3.refs_0_
  39.2 4.1 %collective-permute-done.4.refs_1_ = bf16[528,256]{1,0:T(8,128)(2,1)S(1)} collective-permute-done((bf16[528,256]{1,0:T(8,128)(2,1)}, bf16[528,256]{1,0:T(8,128)(2,1)S(1)}, u32[]{:S(2)}, u32[]{:S(2)}) %collective-permute-start.4) | collective-permute-done | bytes 270368 | tf_op jit(solution)/shard_map/ppermute | solution.py:411
  43.4 9.1 %collective-permute-done.5.refs_2_ = bf16[528,256]{1,0:T(8,128)(2,1)S(1)} collective-permute-done((bf16[528,256]{1,0:T(8,128)(2,1)}, bf16[528,256]{1,0:T(8,128)(2,1)S(1)}, u32[]{:S(2)}, u32[]{:S(2)}) %collective-permute-start.5) | collective-permute-done | bytes 270368 | tf_op jit(solution)/shard_map/ppermute | solution.py:411
  52.5 5.3 %collective-permute-done.6.refs_3_ = bf16[528,256]{1,0:T(8,128)(2,1)S(1)} collective-permute-done((bf16[528,256]{1,0:T(8,128)(2,1)}, bf16[528,256]{1,0:T(8,128)(2,1)S(1)}, u32[]{:S(2)}, u32[]{:S(2)}) %collective-permute-start.6) | collective-permute-done | bytes 270368 | tf_op jit(solution)/shard_map/ppermute | solution.py:411
  57.8 3.1 %shard_map.86 = (bf16[16,112,512]{2,1,0:T(8,128)(2,1)}, s32[8,128]{1,0:T(8,128)S(1)}) custom-call(bf16[528,256]{1,0:T(8,128)(2,1)S(1)} %collective-permute-done.3.refs_0_, bf16[528,256]{1,0:T(8,128)(2,1)S(1)} %collective-permute-done.4.refs_1_, bf16[528,256]{1,0:T(8,128)(2,1)S(1)} %collective-permute-done.5.refs_2_, ...), custom_call_target="tpu_custom_call" | custom-call | flops 99999997952 | bytes 2924544 | tf_op jit(solution)/shard_map/pallas_call | solution.py:55
  60.8 0.0 all-to-all-done.refs_0_
  60.9 26.3 %all_to_all.20.refs_1_ = bf16[16,112,512]{2,1,0:T(8,128)(2,1)S(1)} all-to-all(bf16[16,112,512]{2,1,0:T(8,128)(2,1)} %get-tuple-element.42), channel_id=1, replica_groups={{0,2,4,6,8,10,12,14,16,18,20,22,24,26,28,30},{32,34,36,38,40,42,44,46,4..., dimensions={0} | all-to-all | bytes 3670016 | tf_op jit(solution)/shard_map/all_to_all | solution.py:384
  87.1 8.1 %shard_map.87 = (bf16[8,256,512]{2,1,0:T(8,128)(2,1)S(1)}, bf16[256,256]{1,0:T(8,128)(2,1)S(1)}, bf16[256,512]{1,0:T(8,128)(2,1)S(1)}, s32[1,3072]{1,0:T(1,128)S(1)}) custom-call(s32[2]{0:T(128)S(1)} %copy-done.1, bf16[16,112,512]{2,1,0:T(8,128)(2,1)S(1)} %all-to-all-done.refs_0_, bf16[16,112,512]{2,1,0:T(8,128)(2,1)S(1)} %all_to_all.20.refs_1_), custom_call_target="tpu_custom_call" | custom-call | flops 6442450944 | bytes 6172680 | tf_op jit(solution)/shard_map/pallas_call | solution.py:55
  95.3 1.3 collective-permute-start.8
  96.6 4.0 %collective-permute-start.7 = (bf16[256,256]{1,0:T(8,128)(2,1)S(1)}, bf16[256,256]{1,0:T(8,128)(2,1)S(1)}, u32[]{:S(2)}, u32[]{:S(2)}) collective-permute-start(bf16[256,256]{1,0:T(8,128)(2,1)S(1)} %get-tuple-element.45), channel_id=1, source_target_pairs={{0,2},{2,4},{4,6},{6,8},{8,10},{10,12},{12,14},{16,18},{18,20},{20... | collective-permute-start | bytes 393224 | tf_op jit(solution)/shard_map/ppermute | solution.py:393
  100.6 7.5 %shard_map.88 = (bf16[8,256,512]{2,1,0:T(8,128)(2,1)S(1)}, f32[2,256,256]{2,1,0:T(8,128)S(1)}) custom-call(bf16[8,256,512]{2,1,0:T(8,128)(2,1)S(1)} %get-tuple-element.44.in_ref), custom_call_target="tpu_custom_call" | custom-call | flops 1879048192 | bytes 4718592 | tf_op jit(solution)/shard_map/pallas_call | solution.py:55
  108.1 0.0 collective-permute-done.7.tail_ref
  108.1 0.0 collective-permute-done.8.head_ref
  108.1 6.5 %shard_map.89 = (bf16[2048,512]{1,0:T(8,128)(2,1)}, bf16[16,96,512]{2,1,0:T(8,128)(2,1)}) custom-call(s32[2]{0:T(128)S(1)} %copy-done.1, s32[1,3072]{1,0:T(1,128)S(1)} %get-tuple-element.43.rank_ref, bf16[8,256,512]{2,1,0:T(8,128)(2,1)S(1)} %get-tuple-element.44.in_ref, bf16[256,256]{1,0:T(8,128)(2,1)S(1)} %collective-permute-done.7.tail_ref, ...), custom_call_target="tpu_custom_call" | custom-call | flops 3221225472 | bytes 8794120 | tf_op jit(solution)/shard_map/pallas_call | solution.py:55
  114.7 5.6 %all-to-all-start.3 = ((bf16[16,96,512]{2,1,0:T(8,128)(2,1)}), bf16[16,96,512]{2,1,0:T(8,128)(2,1)S(1)}, u32[]{:S(2)}, u32[]{:S(2)}) async-start(bf16[16,96,512]{2,1,0:T(8,128)(2,1)} %get-tuple-element.53), calls=%async_computation.3 | async-start | bytes 3145728 | tf_op jit(solution)/shard_map/all_to_all | solution.py:384
  120.3 1.6 copy-done.2
  121.9 4.7 %shard_map.90 = bf16[16,96,512]{2,1,0:T(8,128)(2,1)} custom-call(s32[1,3072]{1,0:T(1,128)S(1)} %get-tuple-element.43.rank_ref, bf16[2048,512]{1,0:T(8,128)(2,1)S(1)} %copy-done.2), custom_call_target="tpu_custom_call" | custom-call | flops 3221225472 | bytes 3682304 | tf_op jit(solution)/shard_map/pallas_call | solution.py:55
  126.6 9.0 %all-to-all-done.3.recv_ref = bf16[16,96,512]{2,1,0:T(8,128)(2,1)S(1)} async-done(((bf16[16,96,512]{2,1,0:T(8,128)(2,1)}), bf16[16,96,512]{2,1,0:T(8,128)(2,1)S(1)}, u32[]{:S(2)}, u32[]{:S(2)}) %all-to-all-start.3) | async-done | bytes 1572896 | tf_op jit(solution)/shard_map/all_to_all | solution.py:384
  135.6 5.3 %all-to-all-start.2 = ((bf16[16,96,512]{2,1,0:T(8,128)(2,1)}), bf16[16,96,512]{2,1,0:T(8,128)(2,1)S(1)}, u32[]{:S(2)}, u32[]{:S(2)}) async-start(bf16[16,96,512]{2,1,0:T(8,128)(2,1)} %shard_map.90), calls=%async_computation.2 | async-start | bytes 3145728 | tf_op jit(solution)/shard_map/all_to_all | solution.py:384
  140.8 2.1 %shard_map.92 = (bf16[512,256]{1,0:T(8,128)(2,1)}, bf16[512,256]{1,0:T(8,128)(2,1)S(1)}, bf16[512,256]{1,0:T(8,128)(2,1)}, bf16[512,256]{1,0:T(8,128)(2,1)}) custom-call(s32[8,128]{1,0:T(8,128)S(1)} %get-tuple-element.52.code_ref, bf16[16,96,512]{2,1,0:T(8,128)(2,1)S(1)} %all-to-all-done.3.recv_ref), custom_call_target="tpu_custom_call" | custom-call | flops 805306368 | bytes 2625536 | tf_op jit(solution)/shard_map/pallas_call | solution.py:55
  143.0 5.2 %collective-permute-start.10 = (bf16[512,256]{1,0:T(8,128)(2,1)}, bf16[512,256]{1,0:T(8,128)(2,1)S(1)}, u32[]{:S(2)}, u32[]{:S(2)}) collective-permute-start(bf16[512,256]{1,0:T(8,128)(2,1)} %get-tuple-element.54), channel_id=1, source_target_pairs={{0,192},{2,194},{4,196},{6,198},{8,200},{10,202},{12,204},{14,206}... | collective-permute-start | bytes 786440 | tf_op jit(solution)/shard_map/ppermute | solution.py:488
  148.2 8.3 %collective-permute-start.11 = (bf16[512,256]{1,0:T(8,128)(2,1)}, bf16[512,256]{1,0:T(8,128)(2,1)S(1)}, u32[]{:S(2)}, u32[]{:S(2)}) collective-permute-start(bf16[512,256]{1,0:T(8,128)(2,1)} %get-tuple-element.55), channel_id=1, source_target_pairs={{0,160},{2,162},{4,164},{6,166},{8,168},{10,170},{12,172},{14,174}... | collective-permute-start | bytes 786440 | tf_op jit(solution)/shard_map/ppermute | solution.py:488
  156.5 0.0 collective-permute-start.13
  156.5 2.4 %collective-permute-start.14 = (bf16[512,256]{1,0:T(8,128)(2,1)S(1)}, bf16[512,256]{1,0:T(8,128)(2,1)S(1)}, u32[]{:S(2)}, u32[]{:S(2)}) collective-permute-start(bf16[512,256]{1,0:T(8,128)(2,1)S(1)} %get-tuple-element.58), channel_id=1, source_target_pairs={{0,64},{2,66},{4,68},{6,70},{8,72},{10,74},{12,76},{14,78},{16,80}... | collective-permute-start | bytes 786440 | tf_op jit(solution)/shard_map/ppermute | solution.py:488
  158.9 0.0 all-to-all-done.2.recv_ref
  158.9 1.3 shard_map.91
  160.3 2.5 %collective-permute-start.9 = (bf16[512,256]{1,0:T(8,128)(2,1)S(1)}, bf16[512,256]{1,0:T(8,128)(2,1)S(1)}, u32[]{:S(2)}, u32[]{:S(2)}) collective-permute-start(bf16[512,256]{1,0:T(8,128)(2,1)S(1)} %get-tuple-element.51), channel_id=1, source_target_pairs={{0,224},{2,226},{4,228},{6,230},{8,232},{10,234},{12,236},{14,238}... | collective-permute-start | bytes 786440 | tf_op jit(solution)/shard_map/ppermute | solution.py:488
  162.7 8.4 %collective-permute-start.12 = (bf16[512,256]{1,0:T(8,128)(2,1)S(1)}, bf16[512,256]{1,0:T(8,128)(2,1)S(1)}, u32[]{:S(2)}, u32[]{:S(2)}) collective-permute-start(bf16[512,256]{1,0:T(8,128)(2,1)S(1)} %get-tuple-element.56), channel_id=1, source_target_pairs={{0,128},{2,130},{4,132},{6,134},{8,136},{10,138},{12,140},{14,142}... | collective-permute-start | bytes 786440 | tf_op jit(solution)/shard_map/ppermute | solution.py:488
  171.1 6.1 %collective-permute-start.15 = (bf16[512,256]{1,0:T(8,128)(2,1)S(1)}, bf16[512,256]{1,0:T(8,128)(2,1)S(1)}, u32[]{:S(2)}, u32[]{:S(2)}) collective-permute-start(bf16[512,256]{1,0:T(8,128)(2,1)S(1)} %get-tuple-element.59), channel_id=1, source_target_pairs={{0,32},{2,34},{4,36},{6,38},{8,40},{10,42},{12,44},{14,46},{16,48}... | collective-permute-start | bytes 786440 | tf_op jit(solution)/shard_map/ppermute | solution.py:488
  177.2 0.0 collective-permute-done.13.refs_5_
  177.2 4.6 %collective-permute-done.14.refs_6_ = bf16[512,256]{1,0:T(8,128)(2,1)S(1)} collective-permute-done((bf16[512,256]{1,0:T(8,128)(2,1)S(1)}, bf16[512,256]{1,0:T(8,128)(2,1)S(1)}, u32[]{:S(2)}, u32[]{:S(2)}) %collective-permute-start.14) | collective-permute-done | bytes 262176 | tf_op jit(solution)/shard_map/ppermute | solution.py:488
  181.8 1.8 collective-permute-done.9.refs_1_
  183.5 14.4 %collective-permute-done.12.refs_4_ = bf16[512,256]{1,0:T(8,128)(2,1)S(1)} collective-permute-done((bf16[512,256]{1,0:T(8,128)(2,1)S(1)}, bf16[512,256]{1,0:T(8,128)(2,1)S(1)}, u32[]{:S(2)}, u32[]{:S(2)}) %collective-permute-start.12) | collective-permute-done | bytes 262176 | tf_op jit(solution)/shard_map/ppermute | solution.py:488
  198.0 5.5 %collective-permute-done.15.refs_7_ = bf16[512,256]{1,0:T(8,128)(2,1)S(1)} collective-permute-done((bf16[512,256]{1,0:T(8,128)(2,1)S(1)}, bf16[512,256]{1,0:T(8,128)(2,1)S(1)}, u32[]{:S(2)}, u32[]{:S(2)}) %collective-permute-start.15) | collective-permute-done | bytes 262176 | tf_op jit(solution)/shard_map/ppermute | solution.py:488
  203.4 2.1 %shard_map.93 = (bf16[128,2048]{1,0:T(8,128)(2,1)}, bf16[128,2048]{1,0:T(8,128)(2,1)}, bf16[128,2048]{1,0:T(8,128)(2,1)}, bf16[128,2048]{1,0:T(8,128)(2,1)}) custom-call(s32[2]{0:T(128)S(1)} %copy-done.1, bf16[512,256]{1,0:T(8,128)(2,1)S(1)} %get-tuple-element.50.refs_0_, bf16[512,256]{1,0:T(8,128)(2,1)S(1)} %collective-permute-done.9.refs_1_, ...), custom_call_target="tpu_custom_call" | custom-call | bytes 4194312 | tf_op jit(solution)/shard_map/pallas_call | solution.py:55
  (8 shorter events, 0.0 us)
Async XLA Ops:
  5.2 14.1 %collective-permute-start = (bf16[528,256]{1,0:T(8,128)(2,1)}, bf16[528,256]{1,0:T(8,128)(2,1)S(1)}, u32[]{:S(2)}, u32[]{:S(2)}) collective-permute-start(bf16[528,256]{1,0:T(8,128)(2,1)} %get-tuple-element.33), channel_id=1, source_target_pairs={{0,32},{2,34},{4,36},{6,38},{8,40},{10,42},{12,44},{14,46},{16,48}... | collective-permute-start | bytes 811016 | tf_op jit(solution)/shard_map/ppermute | solution.py:411
  7.7 14.1 %collective-permute-start.1 = (bf16[528,256]{1,0:T(8,128)(2,1)}, bf16[528,256]{1,0:T(8,128)(2,1)S(1)}, u32[]{:S(2)}, u32[]{:S(2)}) collective-permute-start(bf16[528,256]{1,0:T(8,128)(2,1)} %get-tuple-element.34), channel_id=1, source_target_pairs={{0,224},{2,226},{4,228},{6,230},{8,232},{10,234},{12,236},{14,238}... | collective-permute-start | bytes 811016 | tf_op jit(solution)/shard_map/ppermute | solution.py:411
  11.8 16.7 %collective-permute-start.2 = (bf16[528,256]{1,0:T(8,128)(2,1)}, bf16[528,256]{1,0:T(8,128)(2,1)S(1)}, u32[]{:S(2)}, u32[]{:S(2)}) collective-permute-start(bf16[528,256]{1,0:T(8,128)(2,1)} %get-tuple-element.35), channel_id=1, source_target_pairs={{0,128},{2,130},{4,132},{6,134},{8,136},{10,138},{12,140},{14,142}... | collective-permute-start | bytes 811016 | tf_op jit(solution)/shard_map/ppermute | solution.py:411
  15.7 23.6 %collective-permute-start.3 = (bf16[528,256]{1,0:T(8,128)(2,1)}, bf16[528,256]{1,0:T(8,128)(2,1)S(1)}, u32[]{:S(2)}, u32[]{:S(2)}) collective-permute-start(bf16[528,256]{1,0:T(8,128)(2,1)} %get-tuple-element.38), channel_id=1, source_target_pairs={{0,64},{2,66},{4,68},{6,70},{8,72},{10,74},{12,76},{14,78},{16,80}... | collective-permute-start | bytes 811016 | tf_op jit(solution)/shard_map/ppermute | solution.py:411
  15.7 27.7 %collective-permute-start.4 = (bf16[528,256]{1,0:T(8,128)(2,1)}, bf16[528,256]{1,0:T(8,128)(2,1)S(1)}, u32[]{:S(2)}, u32[]{:S(2)}) collective-permute-start(bf16[528,256]{1,0:T(8,128)(2,1)} %get-tuple-element.39), channel_id=1, source_target_pairs={{0,192},{2,194},{4,196},{6,198},{8,200},{10,202},{12,204},{14,206}... | collective-permute-start | bytes 811016 | tf_op jit(solution)/shard_map/ppermute | solution.py:411
  19.3 33.2 %collective-permute-start.5 = (bf16[528,256]{1,0:T(8,128)(2,1)}, bf16[528,256]{1,0:T(8,128)(2,1)S(1)}, u32[]{:S(2)}, u32[]{:S(2)}) collective-permute-start(bf16[528,256]{1,0:T(8,128)(2,1)} %get-tuple-element.40), channel_id=1, source_target_pairs={{0,96},{2,98},{4,100},{6,102},{8,104},{10,106},{12,108},{14,110},{... | collective-permute-start | bytes 811016 | tf_op jit(solution)/shard_map/ppermute | solution.py:411
  21.9 35.9 %collective-permute-start.6 = (bf16[528,256]{1,0:T(8,128)(2,1)}, bf16[528,256]{1,0:T(8,128)(2,1)S(1)}, u32[]{:S(2)}, u32[]{:S(2)}) collective-permute-start(bf16[528,256]{1,0:T(8,128)(2,1)} %get-tuple-element.41), channel_id=1, source_target_pairs={{0,160},{2,162},{4,164},{6,166},{8,168},{10,170},{12,172},{14,174}... | collective-permute-start | bytes 811016 | tf_op jit(solution)/shard_map/ppermute | solution.py:411
  28.4 1.0 copy-start
  32.5 28.4 %all-to-all-start = ((bf16[16,112,512]{2,1,0:T(8,128)(2,1)}), bf16[16,112,512]{2,1,0:T(8,128)(2,1)S(1)}, u32[]{:S(2)}, u32[]{:S(2)}) async-start(bf16[16,112,512]{2,1,0:T(8,128)(2,1)} %get-tuple-element.37), calls=%async_computation | async-start | bytes 3670016 | tf_op jit(solution)/shard_map/all_to_all | solution.py:384
  60.8 26.3 %copy-start.1 = (s32[2]{0:T(128)S(1)}, s32[2]{0:T(128)}, u32[]{:S(2)}) copy-start(s32[2]{0:T(128)} %pad_add_fusion.place_ref) | copy-start | bytes 28
  95.3 12.9 %collective-permute-start.8 = (bf16[256,512]{1,0:T(8,128)(2,1)S(1)}, bf16[256,512]{1,0:T(8,128)(2,1)S(1)}, u32[]{:S(2)}, u32[]{:S(2)}) collective-permute-start(bf16[256,512]{1,0:T(8,128)(2,1)S(1)} %get-tuple-element.46), channel_id=1, source_target_pairs={{2,0},{4,2},{6,4},{8,6},{10,8},{12,10},{14,12},{18,16},{20,18},{22... | collective-permute-start | bytes 786440 | tf_op jit(solution)/shard_map/ppermute | solution.py:393
  96.6 11.6 %collective-permute-start.7 = (bf16[256,256]{1,0:T(8,128)(2,1)S(1)}, bf16[256,256]{1,0:T(8,128)(2,1)S(1)}, u32[]{:S(2)}, u32[]{:S(2)}) collective-permute-start(bf16[256,256]{1,0:T(8,128)(2,1)S(1)} %get-tuple-element.45), channel_id=1, source_target_pairs={{0,2},{2,4},{4,6},{6,8},{8,10},{10,12},{12,14},{16,18},{18,20},{20... | collective-permute-start | bytes 393224 | tf_op jit(solution)/shard_map/ppermute | solution.py:393
  114.7 20.9 %all-to-all-start.3 = ((bf16[16,96,512]{2,1,0:T(8,128)(2,1)}), bf16[16,96,512]{2,1,0:T(8,128)(2,1)S(1)}, u32[]{:S(2)}, u32[]{:S(2)}) async-start(bf16[16,96,512]{2,1,0:T(8,128)(2,1)} %get-tuple-element.53), calls=%async_computation.3 | async-start | bytes 3145728 | tf_op jit(solution)/shard_map/all_to_all | solution.py:384
  120.3 1.6 copy-start.2
  135.6 23.3 %all-to-all-start.2 = ((bf16[16,96,512]{2,1,0:T(8,128)(2,1)}), bf16[16,96,512]{2,1,0:T(8,128)(2,1)S(1)}, u32[]{:S(2)}, u32[]{:S(2)}) async-start(bf16[16,96,512]{2,1,0:T(8,128)(2,1)} %shard_map.90), calls=%async_computation.2 | async-start | bytes 3145728 | tf_op jit(solution)/shard_map/all_to_all | solution.py:384
  143.0 19.8 %collective-permute-start.10 = (bf16[512,256]{1,0:T(8,128)(2,1)}, bf16[512,256]{1,0:T(8,128)(2,1)S(1)}, u32[]{:S(2)}, u32[]{:S(2)}) collective-permute-start(bf16[512,256]{1,0:T(8,128)(2,1)} %get-tuple-element.54), channel_id=1, source_target_pairs={{0,192},{2,194},{4,196},{6,198},{8,200},{10,202},{12,204},{14,206}... | collective-permute-start | bytes 786440 | tf_op jit(solution)/shard_map/ppermute | solution.py:488
  148.2 22.9 %collective-permute-start.11 = (bf16[512,256]{1,0:T(8,128)(2,1)}, bf16[512,256]{1,0:T(8,128)(2,1)S(1)}, u32[]{:S(2)}, u32[]{:S(2)}) collective-permute-start(bf16[512,256]{1,0:T(8,128)(2,1)} %get-tuple-element.55), channel_id=1, source_target_pairs={{0,160},{2,162},{4,164},{6,166},{8,168},{10,170},{12,172},{14,174}... | collective-permute-start | bytes 786440 | tf_op jit(solution)/shard_map/ppermute | solution.py:488
  156.5 20.7 %collective-permute-start.13 = (bf16[512,256]{1,0:T(8,128)(2,1)}, bf16[512,256]{1,0:T(8,128)(2,1)S(1)}, u32[]{:S(2)}, u32[]{:S(2)}) collective-permute-start(bf16[512,256]{1,0:T(8,128)(2,1)} %get-tuple-element.57), channel_id=1, source_target_pairs={{0,96},{2,98},{4,100},{6,102},{8,104},{10,106},{12,108},{14,110},{... | collective-permute-start | bytes 786440 | tf_op jit(solution)/shard_map/ppermute | solution.py:488
  156.5 25.2 %collective-permute-start.14 = (bf16[512,256]{1,0:T(8,128)(2,1)S(1)}, bf16[512,256]{1,0:T(8,128)(2,1)S(1)}, u32[]{:S(2)}, u32[]{:S(2)}) collective-permute-start(bf16[512,256]{1,0:T(8,128)(2,1)S(1)} %get-tuple-element.58), channel_id=1, source_target_pairs={{0,64},{2,66},{4,68},{6,70},{8,72},{10,74},{12,76},{14,78},{16,80}... | collective-permute-start | bytes 786440 | tf_op jit(solution)/shard_map/ppermute | solution.py:488
  160.3 23.3 %collective-permute-start.9 = (bf16[512,256]{1,0:T(8,128)(2,1)S(1)}, bf16[512,256]{1,0:T(8,128)(2,1)S(1)}, u32[]{:S(2)}, u32[]{:S(2)}) collective-permute-start(bf16[512,256]{1,0:T(8,128)(2,1)S(1)} %get-tuple-element.51), channel_id=1, source_target_pairs={{0,224},{2,226},{4,228},{6,230},{8,232},{10,234},{12,236},{14,238}... | collective-permute-start | bytes 786440 | tf_op jit(solution)/shard_map/ppermute | solution.py:488
  162.7 35.2 %collective-permute-start.12 = (bf16[512,256]{1,0:T(8,128)(2,1)S(1)}, bf16[512,256]{1,0:T(8,128)(2,1)S(1)}, u32[]{:S(2)}, u32[]{:S(2)}) collective-permute-start(bf16[512,256]{1,0:T(8,128)(2,1)S(1)} %get-tuple-element.56), channel_id=1, source_target_pairs={{0,128},{2,130},{4,132},{6,134},{8,136},{10,138},{12,140},{14,142}... | collective-permute-start | bytes 786440 | tf_op jit(solution)/shard_map/ppermute | solution.py:488
  171.1 32.3 %collective-permute-start.15 = (bf16[512,256]{1,0:T(8,128)(2,1)S(1)}, bf16[512,256]{1,0:T(8,128)(2,1)S(1)}, u32[]{:S(2)}, u32[]{:S(2)}) collective-permute-start(bf16[512,256]{1,0:T(8,128)(2,1)S(1)} %get-tuple-element.59), channel_id=1, source_target_pairs={{0,32},{2,34},{4,36},{6,38},{8,40},{10,42},{12,44},{14,46},{16,48}... | collective-permute-start | bytes 786440 | tf_op jit(solution)/shard_map/ppermute | solution.py:488

commit v2 on v1

--- a/solution.py
+++ b/solution.py
@@ -31,7 +31,11 @@
 F32 = jnp.float32
 I32 = jnp.int32
 
-CHUNKS = ((0, 1, 7, 4), (2, 6, 3, 5))
+CHUNKS = ((0, 1, 7, 2), (6, 3, 5, 4))
+PICK_HINT = (0, 10**9, 10**11)
+UNPACK_HINT = (10**9, 10**11, 10**9)
+RETURNS = ((3, 5), (4, 2, 6, 7), (0, 1))
+ORDER = sum(CHUNKS, ())
 PACK_HINT = (10**6, 10**11)
 PLANES = [[z * PLANE + i for i in range(PLANE)] for z in range(ZN)]
 
@@ -48,7 +52,7 @@
     return pl.BlockSpec(memory_space=pltpu.VMEM)
 
 
-def call(kernel, ins, outs, scratch=(), flops=0, specs=None, out_specs=None, limit=28):
+def call(kernel, ins, outs, scratch=(), flops=0, specs=None, out_specs=None, out_spec=None, limit=28, aliases=None):
     size = sum(math.prod(o.shape) * o.dtype.itemsize for o in outs)
     size += sum(math.prod(a.shape) * a.dtype.itemsize for a in ins)
     specs = specs or {}
@@ -59,8 +63,9 @@
             for i, o in enumerate(outs)
         ),
         in_specs=[specs.get(i) or whole() for i in range(len(ins))],
-        out_specs=tuple((out_specs or {}).get(i) or whole() for i in range(len(outs))),
+        out_specs=tuple((out_specs or {}).get(i) or out_spec or whole() for i in range(len(outs))),
         scratch_shapes=list(scratch),
+        input_output_aliases=aliases or {},
         cost_estimate=pl.CostEstimate(flops=flops, bytes_accessed=size, transcendentals=0),
         compiler_params=pltpu.CompilerParams(vmem_limit_bytes=limit * 1024 * 1024),
     )(*ins)
@@ -130,9 +135,12 @@
     return pltpu.make_async_copy(stage_ref.at[part], out_ref.at[part], sems.at[i])
 
 
-def pack_kernel(chunk, *refs):
+def pack_kernel(index, *refs):
+    chunk = CHUNKS[index]
     n = len(chunk)
-    blocks, (out_ref, code_ref, x_ref, send_ref, sems) = refs[:n], refs[-5:]
+    blocks, notes = refs[:n], refs[n : n + index]
+    out_ref, code_ref, note_ref, x_ref, send_ref, sems = refs[-6:]
+    last = index == len(CHUNKS) - 1
     rows = n * MOST
     ids = [blocks[i][4 * TOK :, 0:TOK].astype(F32) for i in range(n)]
     ids = jnp.concatenate(
@@ -147,26 +155,35 @@
         slot = slot + hot * dot(hot.astype(BF), tri)
     code = group * STRIDE + slot.astype(I32)
     code_ref[...] = code
+    zeros = jnp.zeros((TILE, WIDTH), BF)
     for hh in range(HPZ):
         for i in range(n):
             for t in range(4):
                 x_ref[i * TOK : (i + 1) * TOK, t * WIDTH : (t + 1) * WIDTH] = blocks[i][
                     t * TOK : (t + 1) * TOK, hh * WIDTH : (hh + 1) * WIDTH
                 ]
-        mine = range(hh * n, (hh + 1) * n)
-        position = jnp.concatenate(
-            [(code[i : i + 1] & (STRIDE - 1)) + (i - hh * n) * MOST for i in mine], axis=1
-        )
-        owner = jnp.concatenate([group[i : i + 1] for i in mine], axis=1)
-        value = jnp.concatenate([local[i : i + 1] for i in mine], axis=1)
-        value = jnp.broadcast_to(value, (TILE, n * TOK))
-        x = x_ref[...]
+        found = [[] for _ in range(RANGES)]
+        for p in range(0, n, 2):
+            mine = [hh * n + p, hh * n + p + 1]
+            position = jnp.concatenate(
+                [(code[i : i + 1] & (STRIDE - 1)) + j * MOST for j, i in enumerate(mine)], axis=1
+            )
+            owner = jnp.concatenate([group[i : i + 1] for i in mine], axis=1)
+            value = jnp.concatenate([local[i : i + 1] for i in mine], axis=1)
+            value = jnp.broadcast_to(value, (TILE, 2 * TOK))
+            x = x_ref[p * TOK : (p + 2) * TOK, :]
+            for b in range(RANGES):
+                target = jnp.where(owner == b, position, -1)
+                pick = one_hot(target == iota((2 * MOST, 2 * TOK), 0))
+                send_ref[hh * RANGES + b, p * MOST : (p + 2) * MOST, :] = dot(pick, x).astype(BF)
+                found[b].append(dot(value, pick, NT).astype(BF))
         for b in range(RANGES):
-            target = jnp.where(owner == b, position, -1)
-            pick = one_hot(target == iota((rows, n * TOK), 0))
-            send_ref[hh * RANGES + b, 0:rows, :] = dot(pick, x).astype(BF)
-            send_ref[hh * RANGES + b, rows:, 0:rows] = dot(value, pick, NT).astype(BF)
-            send_ref[hh * RANGES + b, rows:, rows:] = jnp.zeros((TILE, ALL - rows), BF)
+            note = jnp.concatenate(found[b] + [zeros[:, n * MOST :]], axis=1)
+            note_ref[hh * RANGES + b] = note
+            if last:
+                tile = [a[hh * RANGES + b] for a in notes] + [note]
+                tile = tile + [zeros] * (4 - len(tile))
+                send_ref[hh * RANGES + b, rows:, :] = jnp.concatenate(tile, axis=1)
         leave(send_ref, out_ref, sems, hh, HPZ).start()
     for hh in range(HPZ):
         leave(send_ref, out_ref, sems, hh, HPZ).wait()
@@ -174,12 +191,11 @@
 
 def rank_rows(z, clusters):
     lanes = ZN * MOST
-    dist = sum(CHUNKS, ())
 
     def source(shape, dim):
         segment = iota(shape, dim) // MOST
         value = jnp.zeros(shape, I32)
-        for i, d in enumerate(dist):
+        for i, d in enumerate(ORDER):
             value = jnp.where(segment == i, (z - d) & (ZN - 1), value)
         return value
 
@@ -216,11 +232,16 @@
     recvs, (sorted_ref, tail_ref, head_ref, rank_ref, x_ref) = refs[:n], refs[n:]
     clusters = []
     at = 0
-    for chunk, recv_ref in zip(CHUNKS, recvs):
+    for i, (chunk, recv_ref) in enumerate(zip(CHUNKS, recvs)):
         rows = len(chunk) * MOST
+        tail = len(CHUNKS[-1]) * MOST
         clusters.append(
             jnp.concatenate(
-                [recv_ref[s, rows:, 0:rows].astype(F32)[0:1] for s in range(PLANE)], axis=0
+                [
+                    recvs[-1][s, tail:, i * WIDTH : i * WIDTH + rows].astype(F32)[0:1]
+                    for s in range(PLANE)
+                ],
+                axis=0,
             )
         )
         for s in range(PLANE):
@@ -238,31 +259,31 @@
 
 
 def span_math(q, g, k0, k1, v0, v1, keep):
-    s0 = dot(q, k0, NT)
-    s1 = dot(q, k1, NT)
+    s0 = dot(k0, q, NT)
+    s1 = dot(k1, q, NT)
     if keep is not None:
         s0 = jnp.where(keep, s0, -1e30)
     peak = jnp.maximum(
-        jnp.max(s0, axis=1, keepdims=True), jnp.max(s1, axis=1, keepdims=True)
+        jnp.max(s0, axis=0, keepdims=True), jnp.max(s1, axis=0, keepdims=True)
     )
     factor = SCALING * math.log2(math.e)
     p0 = jnp.exp2((s0 - peak) * factor)
     p1 = jnp.exp2((s1 - peak) * factor)
     inverse = 1.0 / (
-        jnp.sum(p0, axis=1, keepdims=True) + jnp.sum(p1, axis=1, keepdims=True)
+        jnp.sum(p0, axis=0, keepdims=True) + jnp.sum(p1, axis=0, keepdims=True)
     )
     w0 = p0 * inverse
     w1 = p1 * inverse
     l0 = w0.astype(BF)
     l1 = w1.astype(BF)
-    attended = (dot(l0, v0) + dot(l1, v1)).astype(BF)
-    e0 = dot(g, v0, NT)
-    e1 = dot(g, v1, NT)
-    inner = jnp.sum(w0 * e0, axis=1, keepdims=True) + jnp.sum(w1 * e1, axis=1, keepdims=True)
+    attended = (dot(v0, l0, TN) + dot(v1, l1, TN)).T.astype(BF)
+    e0 = dot(v0, g, NT)
+    e1 = dot(v1, g, NT)
+    inner = jnp.sum(w0 * e0, axis=0, keepdims=True) + jnp.sum(w1 * e1, axis=0, keepdims=True)
     h0 = (w0 * (e0 - inner) * SCALING).astype(BF)
     h1 = (w1 * (e1 - inner) * SCALING).astype(BF)
-    dq = (dot(h0, k0) + dot(h1, k1)).astype(BF)
-    return attended, dq, dot(h0, q, TN), dot(h1, q, TN), dot(l0, g, TN), dot(l1, g, TN)
+    dq = (dot(k0, h0, TN) + dot(k1, h1, TN)).T.astype(BF)
+    return attended, dq, dot(h0, q), dot(h1, q), dot(l0, g), dot(l1, g)
 
 
 Q, K, V, G = (slice(t * WIDTH, (t + 1) * WIDTH) for t in range(4))
@@ -285,7 +306,8 @@
         o_ref[c - 1, :, 2 * WIDTH :] = d_ref[c - 1].astype(BF)
         return carry
 
-    lax.fori_loop(1, SPANS, one, 0)
+    for c in range(1, SPANS):
+        one(c, 0)
     part_ref[0] = d_ref[0]
     part_ref[1] = d_ref[SPANS - 1]
     o_ref[0, :, 0 : 2 * WIDTH] = jnp.zeros((SPAN, 2 * WIDTH), BF)
@@ -299,7 +321,12 @@
     for p in range(PICKS):
         span = range(p * step, (p + 1) * step)
         part = jnp.concatenate(
-            [col[i * ZN * MOST + at : i * ZN * MOST + at + rows, :] for i in span], axis=0
+            [
+                col[i * ZN * MOST + j * MOST : i * ZN * MOST + (j + 1) * MOST, :]
+                for i in span
+                for j in at
+            ],
+            axis=0,
         )
         pick = one_hot(part == iota((step * rows, BLOCK), 1))
         send_ref[p * step : (p + 1) * step] = dot(pick, o).astype(BF).reshape(step, rows, ALL)
@@ -335,29 +362,29 @@
     done.wait()
 
 
-def pick_kernel(at, rank_ref, o_ref, out_ref, send_ref, sems):
-    pick_out(at, rank_ref, o_ref[...], out_ref, send_ref, sems)
-
-
-def unpack_kernel(chunk, code_ref, recv_ref, *blocks):
-    n = len(chunk)
-    rows = n * MOST
-    code = code_ref[...]
+def pick_kernel(at, rank_ref, o_ref, *refs):
+    pick_out(at, rank_ref, o_ref[...], *refs[-3:])
+
+
+def unpack_kernel(places, *refs):
+    codes, recv_ref, blocks = refs[: len(CHUNKS)], refs[len(CHUNKS)], refs[-len(places) :]
     for hh in range(HPZ):
-        cols = []
-        for i in range(n):
-            mine = code[hh * n + i : hh * n + i + 1]
-            target = lax.shift_right_logical(mine, 5) * rows + (mine & (STRIDE - 1)) + i * MOST
-            cols.append(row_to_col(target.astype(F32)).astype(I32))
-        col = jnp.concatenate(cols, axis=0)
-        pick = one_hot(col == iota((n * TOK, RANGES * rows), 1))
-        x = recv_ref[hh * RANGES : (hh + 1) * RANGES].reshape(RANGES * rows, ALL)
-        got = dot(pick, x).astype(BF)
-        for i in range(n):
-            for t in range(4):
-                blocks[i][t * TOK : (t + 1) * TOK, hh * WIDTH : (hh + 1) * WIDTH] = got[
-                    i * TOK : (i + 1) * TOK, t * WIDTH : (t + 1) * WIDTH
-                ]
+        for p in range(0, len(places), 2):
+            cols = []
+            for j, (chunk, at) in enumerate(places[p : p + 2]):
+                row = hh * len(CHUNKS[chunk]) + at
+                mine = codes[chunk][row : row + 1, :]
+                target = lax.shift_right_logical(mine, 5) * (2 * MOST) + (mine & (STRIDE - 1))
+                cols.append(row_to_col((target + j * MOST).astype(F32)).astype(I32))
+            col = jnp.concatenate(cols, axis=0)
+            pick = one_hot(col == iota((2 * TOK, RANGES * 2 * MOST), 1))
+            x = recv_ref[hh * RANGES : (hh + 1) * RANGES, p * MOST : (p + 2) * MOST, :]
+            got = dot(pick, x.reshape(RANGES * 2 * MOST, ALL)).astype(BF)
+            for j in range(2):
+                for t in range(4):
+                    blocks[p + j][t * TOK : (t + 1) * TOK, hh * WIDTH : (hh + 1) * WIDTH] = got[
+                        j * TOK : (j + 1) * TOK, t * WIDTH : (t + 1) * WIDTH
+                    ]
 
 
 def join_kernel(place_ref, *refs):
@@ -397,6 +424,7 @@
     index = lax.axis_index("seq")
     place = jnp.stack([index // PLANE, index % RANGES]).astype(I32)
     hbm = pl.BlockSpec(memory_space=pltpu.HBM)
+    anywhere = pl.BlockSpec(memory_space=pl.ANY)
     blocks = call(
         prep_kernel,
         [place, cluster_ids.T, queries, keys, values, out_grad],
@@ -406,26 +434,32 @@
         limit=60,
     )
     moved = {0: blocks[0]}
-    for d in sum(CHUNKS, ()):
+    for d in ORDER:
         if d:
             moved[d] = lax.ppermute(blocks[d], "seq", z_pairs(d))
-    codes, arrived = [], []
+    codes, arrived, notes = [], [], []
     for i, chunk in enumerate(CHUNKS):
         n = len(chunk)
         rows = n * MOST
-        send, code = call(
-            functools.partial(pack_kernel, chunk),
-            [moved[d] for d in chunk] + codes[-1:],
-            [out((PLANE, rows + TILE, ALL), BF), out((HPZ * n, TOK), I32)],
+        extra = TILE if i == len(CHUNKS) - 1 else 0
+        send, code, note = call(
+            functools.partial(pack_kernel, i),
+            [moved[d] for d in chunk] + notes,
+            [
+                out((PLANE, rows + extra, ALL), BF),
+                out((HPZ * n, TOK), I32),
+                out((PLANE, TILE, WIDTH), BF),
+            ],
             [
                 pltpu.VMEM((n * TOK, ALL), BF),
-                pltpu.VMEM((PLANE, rows + TILE, ALL), BF),
+                pltpu.VMEM((PLANE, rows + extra, ALL), BF),
                 pltpu.SemaphoreType.DMA((HPZ,)),
             ],
             flops=PACK_HINT[i],
             out_specs={0: hbm},
         )
         codes.append(code)
+        notes.append(note)
         arrived.append(exchange(send, PLANES))
     rows_in, tail, head, rank = call(
         place_kernel,
@@ -451,10 +485,10 @@
     )
     o = None
     back = {}
-    at = ZN * MOST
-    for chunk, code in reversed(list(zip(CHUNKS, codes))):
+    waits = {}
+    for step, chunk in enumerate(RETURNS):
         rows = len(chunk) * MOST
-        at -= rows
+        at = tuple(ORDER.index(d) for d in chunk)
         send_shape = out((PLANE, rows, ALL), BF)
         flops = 2 * BLOCK * PLANE * rows * ALL
         stage = [pltpu.VMEM((PLANE, rows, ALL), BF), pltpu.SemaphoreType.DMA((PICKS,))]
@@ -471,21 +505,29 @@
         else:
             (send,) = call(
                 functools.partial(pick_kernel, at),
-                [rank, o],
+                [rank, o] + waits.get(("pick", step), []),
                 [send_shape],
                 stage,
-                flops=flops,
+                flops=PICK_HINT[step],
+                specs={2: anywhere},
                 out_specs={0: hbm},
             )
         got = exchange(send, PLANES)
+        places = tuple(
+            (i, c.index(d)) for d in chunk for i, c in enumerate(CHUNKS) if d in c
+        )
         pieces = call(
-            functools.partial(unpack_kernel, chunk),
-            [code, got],
+            functools.partial(unpack_kernel, places),
+            codes + [got] + waits.get(("unpack", step), []),
             [out((4 * TOK, PAIR), BF)] * len(chunk),
-            flops=4 * RANGES * rows * len(chunk) * TOK * ALL,
+            flops=UNPACK_HINT[step],
+            specs={j: anywhere for j in range(len(codes) + 1, len(codes) + 5)},
         )
         for d, piece in zip(chunk, pieces):
             back[d] = lax.ppermute(piece, "seq", z_pairs(-d)) if d else piece
+        waits["pick", step + 2] = [pieces[0]]
+        if step == 0:
+            waits["unpack", 1] = [back[d] for d in chunk]
     return call(
         join_kernel,
         [place] + [back[d] for d in range(ZN)],

time: 207 us -> 202 us (0.976)
  starting transfers between devices: 72 us -> 58.5 us
  waiting for transfers between devices: 60.9 us -> 66 us
  blocking collectives: 26.3 us -> 29.7 us
    ppermute x7, starting transfers between devices: 32.9 us -> 15.1 us  [body(): back[d] = lax.ppermute(piece, 'seq', z_pairs(-d)) if d else piece]
    all_to_all x3 -> x4, waiting for transfers between devices: 8.99 us -> 14.4 us  [exchange(): lax.all_to_all(array, 'seq', split_axis=0, concat_axis=0, axis_index_grou...]
    all_to_all x3 -> x4, starting transfers between devices: 17.7 us -> 21.8 us  [exchange(): lax.all_to_all(array, 'seq', split_axis=0, concat_axis=0, axis_index_grou...]
    all_to_all x1, blocking collectives: 26.3 us -> 29.7 us  [exchange(): lax.all_to_all(array, 'seq', split_axis=0, concat_axis=0, axis_index_grou...]
    pallas_call x10 -> x12, Pallas kernels: 42.4 us -> 42 us  [call(): pl.pallas_call(kernel, out_shape=tuple((pltpu.HBM(o.shape, o.dtype) if i...]
  transfers between devices with their start and end apart: 19 -> 20, of which waited for: 10 -> 10; matrix products, arithmetic and copies ran while one was open for 0% -> 0% of each run, Pallas kernels for 11% -> 12%
where the time goes in v2:
time: 202 us; the launch traced here: 200 us
  waiting for transfers between devices  66 us (33%)
  starting transfers between devices  58.5 us (29%)
  Pallas kernels  42 us (21%)
  blocking collectives  29.7 us (15%)
  local copies, waits for them, and re-layouts  2.55 us (1%)
    pallas_call x12, Pallas kernels, call(): pl.pallas_call(kernel, out_shape=tuple((pltpu.HBM(o.shape, o.dtype) if i...  42 us
    all_to_all x1, blocking collectives, exchange(): lax.all_to_all(array, 'seq', split_axis=0, concat_axis=0, axis_index_grou...  29.7 us
    ppermute x7, waiting for transfers between devices, body(): moved[d] = lax.ppermute(blocks[d], 'seq', z_pairs(d))  25.9 us
    ppermute x7, waiting for transfers between devices, body(): back[d] = lax.ppermute(piece, 'seq', z_pairs(-d)) if d else piece  25.7 us
    all_to_all x4, starting transfers between devices, exchange(): lax.all_to_all(array, 'seq', split_axis=0, concat_axis=0, axis_index_grou...  21.8 us
    ppermute x7, starting transfers between devices, body(): moved[d] = lax.ppermute(blocks[d], 'seq', z_pairs(d))  16.1 us
    ppermute x7, starting transfers between devices, body(): back[d] = lax.ppermute(piece, 'seq', z_pairs(-d)) if d else piece  15.1 us
    all_to_all x4, waiting for transfers between devices, exchange(): lax.all_to_all(array, 'seq', split_axis=0, concat_axis=0, axis_index_grou...  14.4 us
  transfers between devices with their start and end apart: 20, of which 10 were waited for; matrix products, arithmetic and copies ran while one was open for 0% of the time, Pallas kernels for 12%

profile of v2, /device:TPU:1, one launch (start us, length us, event | category | flops | bytes accessed | tf_op | source)
XLA Modules:
  0.0 200.5 jit_solution(1862040989167849451)
XLA Ops:
  0.7 0.6 pad_add_fusion.place_ref
  1.3 3.9 %shard_map.84 = (bf16[528,256]{1,0:T(8,128)(2,1)}, bf16[528,256]{1,0:T(8,128)(2,1)}, bf16[528,256]{1,0:T(8,128)(2,1)}, bf16[528,256]{1,0:T(8,128)(2,1)}, bf16[52...) custom-call(s32[2]{0:T(128)} %pad_add_fusion.place_ref, ...), custom_call_target="tpu_custom_call" | custom-call | bytes 4268040 | tf_op jit(solution)/shard_map/pallas_call | solution.py:59
  5.2 2.5 %collective-permute-start = (bf16[528,256]{1,0:T(8,128)(2,1)}, bf16[528,256]{1,0:T(8,128)(2,1)S(1)}, u32[]{:S(2)}, u32[]{:S(2)}) collective-permute-start(bf16[528,256]{1,0:T(8,128)(2,1)} %get-tuple-element.34), channel_id=1, source_target_pairs={{0,32},{2,34},{4,36},{6,38},{8,40},{10,42},{12,44},{14,46},{16,48}... | collective-permute-start | bytes 811016 | tf_op jit(solution)/shard_map/ppermute | solution.py:439
  7.7 4.0 %collective-permute-start.1 = (bf16[528,256]{1,0:T(8,128)(2,1)}, bf16[528,256]{1,0:T(8,128)(2,1)S(1)}, u32[]{:S(2)}, u32[]{:S(2)}) collective-permute-start(bf16[528,256]{1,0:T(8,128)(2,1)} %get-tuple-element.35), channel_id=1, source_target_pairs={{0,224},{2,226},{4,228},{6,230},{8,232},{10,234},{12,236},{14,238}... | collective-permute-start | bytes 811016 | tf_op jit(solution)/shard_map/ppermute | solution.py:439
  11.8 0.0 collective-permute-start.2
  11.8 3.6 %collective-permute-start.3 = (bf16[528,256]{1,0:T(8,128)(2,1)}, bf16[528,256]{1,0:T(8,128)(2,1)S(1)}, u32[]{:S(2)}, u32[]{:S(2)}) collective-permute-start(bf16[528,256]{1,0:T(8,128)(2,1)} %get-tuple-element.38), channel_id=1, source_target_pairs={{0,192},{2,194},{4,196},{6,198},{8,200},{10,202},{12,204},{14,206}... | collective-permute-start | bytes 811016 | tf_op jit(solution)/shard_map/ppermute | solution.py:439
  15.3 0.3 collective-permute-start.4
  15.7 2.4 %collective-permute-done.refs_1_ = bf16[528,256]{1,0:T(8,128)(2,1)S(1)} collective-permute-done((bf16[528,256]{1,0:T(8,128)(2,1)}, bf16[528,256]{1,0:T(8,128)(2,1)S(1)}, u32[]{:S(2)}, u32[]{:S(2)}) %collective-permute-start) | collective-permute-done | bytes 270368 | tf_op jit(solution)/shard_map/ppermute | solution.py:439
  18.1 2.0 %collective-permute-start.5 = (bf16[528,256]{1,0:T(8,128)(2,1)}, bf16[528,256]{1,0:T(8,128)(2,1)S(1)}, u32[]{:S(2)}, u32[]{:S(2)}) collective-permute-start(bf16[528,256]{1,0:T(8,128)(2,1)} %get-tuple-element.40), channel_id=1, source_target_pairs={{0,160},{2,162},{4,164},{6,166},{8,168},{10,170},{12,172},{14,174}... | collective-permute-start | bytes 811016 | tf_op jit(solution)/shard_map/ppermute | solution.py:439
  20.1 3.6 %collective-permute-start.6 = (bf16[528,256]{1,0:T(8,128)(2,1)}, bf16[528,256]{1,0:T(8,128)(2,1)S(1)}, u32[]{:S(2)}, u32[]{:S(2)}) collective-permute-start(bf16[528,256]{1,0:T(8,128)(2,1)} %get-tuple-element.41), channel_id=1, source_target_pairs={{0,128},{2,130},{4,132},{6,134},{8,136},{10,138},{12,140},{14,142}... | collective-permute-start | bytes 811016 | tf_op jit(solution)/shard_map/ppermute | solution.py:439
  23.8 1.9 collective-permute-done.2.refs_3_
  25.7 1.0 copy-done
  26.7 2.8 %shard_map.85 = (bf16[16,96,512]{2,1,0:T(8,128)(2,1)}, s32[8,128]{1,0:T(8,128)S(1)}, bf16[16,16,128]{2,1,0:T(8,128)(2,1)S(1)}) custom-call(bf16[528,256]{1,0:T(8,128)(2,1)S(1)} %copy-done, bf16[528,256]{1,0:T(8,128)(2,1)S(1)} %collective-permute-done.refs_1_, bf16[528,256]{1,0:T(8,128)(2,1)S(1)} %collective-permute-done.1.refs_2_, ...), custom_call_target="tpu_custom_call" | custom-call | flops 1000000 | bytes 2723840 | tf_op jit(solution)/shard_map/pallas_call | solution.py:59
  29.5 6.8 %all-to-all-start = ((bf16[16,96,512]{2,1,0:T(8,128)(2,1)}), bf16[16,96,512]{2,1,0:T(8,128)(2,1)S(1)}, u32[]{:S(2)}, u32[]{:S(2)}) async-start(bf16[16,96,512]{2,1,0:T(8,128)(2,1)} %get-tuple-element.44), calls=%async_computation | async-start | bytes 3145728 | tf_op jit(solution)/shard_map/all_to_all | solution.py:411
  36.3 0.0 collective-permute-done.3.refs_0_
  36.3 11.0 %collective-permute-done.4.refs_1_ = bf16[528,256]{1,0:T(8,128)(2,1)S(1)} collective-permute-done((bf16[528,256]{1,0:T(8,128)(2,1)}, bf16[528,256]{1,0:T(8,128)(2,1)S(1)}, u32[]{:S(2)}, u32[]{:S(2)}) %collective-permute-start.4) | collective-permute-done | bytes 270368 | tf_op jit(solution)/shard_map/ppermute | solution.py:439
  47.2 10.5 %collective-permute-done.5.refs_2_ = bf16[528,256]{1,0:T(8,128)(2,1)S(1)} collective-permute-done((bf16[528,256]{1,0:T(8,128)(2,1)}, bf16[528,256]{1,0:T(8,128)(2,1)S(1)}, u32[]{:S(2)}, u32[]{:S(2)}) %collective-permute-start.5) | collective-permute-done | bytes 270368 | tf_op jit(solution)/shard_map/ppermute | solution.py:439
  57.8 0.0 collective-permute-done.6.refs_3_
  57.8 3.6 %shard_map.86 = (bf16[16,112,512]{2,1,0:T(8,128)(2,1)}, s32[8,128]{1,0:T(8,128)S(1)}, bf16[16,16,128]{2,1,0:T(8,128)(2,1)}) custom-call(bf16[528,256]{1,0:T(8,128)(2,1)S(1)} %collective-permute-done.3.refs_0_, bf16[528,256]{1,0:T(8,128)(2,1)S(1)} %collective-permute-done.4.refs_1_, bf16[528,256]{1,0:T(8,128)(2,1)S(1)} %collective-permute-done.5.refs_2_, ...), custom_call_target="tpu_custom_call" | custom-call | flops 99999997952 | bytes 3051520 | tf_op jit(solution)/shard_map/pallas_call | solution.py:59
  61.4 0.0 all-to-all-done.refs_0_
  61.4 29.7 %all_to_all.25.refs_1_ = bf16[16,112,512]{2,1,0:T(8,128)(2,1)S(1)} all-to-all(bf16[16,112,512]{2,1,0:T(8,128)(2,1)} %get-tuple-element.45), channel_id=1, replica_groups={{0,2,4,6,8,10,12,14,16,18,20,22,24,26,28,30},{32,34,36,38,40,42,44,46,4..., dimensions={0} | all-to-all | bytes 3670016 | tf_op jit(solution)/shard_map/all_to_all | solution.py:411
  91.2 8.1 %shard_map.87 = (bf16[8,256,512]{2,1,0:T(8,128)(2,1)S(1)}, bf16[256,256]{1,0:T(8,128)(2,1)S(1)}, bf16[256,512]{1,0:T(8,128)(2,1)S(1)}, s32[1,3072]{1,0:T(1,128)S(1)}) custom-call(s32[2]{0:T(128)S(1)} %copy-done.1, bf16[16,96,512]{2,1,0:T(8,128)(2,1)S(1)} %all-to-all-done.refs_0_, bf16[16,112,512]{2,1,0:T(8,128)(2,1)S(1)} %all_to_all.25.refs_1_), custom_call_target="tpu_custom_call" | custom-call | flops 6442450944 | bytes 5910536 | tf_op jit(solution)/shard_map/pallas_call | solution.py:59
  99.3 1.3 collective-permute-start.8
  100.6 4.2 %collective-permute-start.7 = (bf16[256,256]{1,0:T(8,128)(2,1)S(1)}, bf16[256,256]{1,0:T(8,128)(2,1)S(1)}, u32[]{:S(2)}, u32[]{:S(2)}) collective-permute-start(bf16[256,256]{1,0:T(8,128)(2,1)S(1)} %get-tuple-element.48), channel_id=1, source_target_pairs={{0,2},{2,4},{4,6},{6,8},{8,10},{10,12},{12,14},{16,18},{18,20},{20... | collective-permute-start | bytes 393224 | tf_op jit(solution)/shard_map/ppermute | solution.py:420
  104.8 6.5 %shard_map.88 = (bf16[8,256,512]{2,1,0:T(8,128)(2,1)S(1)}, f32[2,256,256]{2,1,0:T(8,128)S(1)}) custom-call(bf16[8,256,512]{2,1,0:T(8,128)(2,1)S(1)} %get-tuple-element.47.in_ref), custom_call_target="tpu_custom_call" | custom-call | flops 1879048192 | bytes 4718592 | tf_op jit(solution)/shard_map/pallas_call | solution.py:59
  111.3 4.4 %shard_map.89 = (bf16[2048,512]{1,0:T(8,128)(2,1)}, bf16[16,48,512]{2,1,0:T(8,128)(2,1)}) custom-call(s32[2]{0:T(128)S(1)} %copy-done.1, s32[1,3072]{1,0:T(1,128)S(1)} %get-tuple-element.46.rank_ref, bf16[8,256,512]{2,1,0:T(8,128)(2,1)S(1)} %get-tuple-element.47.in_ref, bf16[256,256]{1,0:T(8,128)(2,1)S(1)} %collective-permute-done.7.tail_ref, ...), custom_call_target="tpu_custom_call" | custom-call | flops 1610612736 | bytes 8007688 | tf_op jit(solution)/shard_map/pallas_call | solution.py:59
  115.7 5.5 %all-to-all-start.2 = ((bf16[16,48,512]{2,1,0:T(8,128)(2,1)}), bf16[16,48,512]{2,1,0:T(8,128)(2,1)S(1)}, u32[]{:S(2)}, u32[]{:S(2)}) async-start(bf16[16,48,512]{2,1,0:T(8,128)(2,1)} %get-tuple-element.53), calls=%async_computation.2 | async-start | bytes 1572864 | tf_op jit(solution)/shard_map/all_to_all | solution.py:411
  121.3 1.6 copy-done.3
  122.9 4.7 %shard_map.93 = bf16[16,96,512]{2,1,0:T(8,128)(2,1)} custom-call(s32[1,3072]{1,0:T(1,128)S(1)} %get-tuple-element.46.rank_ref, bf16[2048,512]{1,0:T(8,128)(2,1)S(1)} %copy-done.3), custom_call_target="tpu_custom_call" | custom-call | flops 1000000000 | bytes 3682304 | tf_op jit(solution)/shard_map/pallas_call | solution.py:59
  127.5 4.4 %all-to-all-done.2.refs_2_ = bf16[16,48,512]{2,1,0:T(8,128)(2,1)S(1)} async-done(((bf16[16,48,512]{2,1,0:T(8,128)(2,1)}), bf16[16,48,512]{2,1,0:T(8,128)(2,1)S(1)}, u32[]{:S(2)}, u32[]{:S(2)}) %all-to-all-start.2) | async-done | bytes 786464 | tf_op jit(solution)/shard_map/all_to_all | solution.py:411
  132.0 3.7 %all-to-all-start.4 = ((bf16[16,96,512]{2,1,0:T(8,128)(2,1)}), bf16[16,96,512]{2,1,0:T(8,128)(2,1)S(1)}, u32[]{:S(2)}, u32[]{:S(2)}) async-start(bf16[16,96,512]{2,1,0:T(8,128)(2,1)} %shard_map.93), calls=%async_computation.4 | async-start | bytes 3145728 | tf_op jit(solution)/shard_map/all_to_all | solution.py:411
  135.7 0.7 shard_map.90
  136.4 1.4 collective-permute-start.11
  137.8 4.2 %collective-permute-start.10 = (bf16[512,256]{1,0:T(8,128)(2,1)S(1)}, bf16[512,256]{1,0:T(8,128)(2,1)S(1)}, u32[]{:S(2)}, u32[]{:S(2)}) collective-permute-start(bf16[512,256]{1,0:T(8,128)(2,1)S(1)} %get-tuple-element.54.refs_0_), channel_id=1, source_target_pairs={{0,160},{2,162},{4,164},{6,166},{8,168},{10,170},{12,172},{14,174}... | collective-permute-start | bytes 786440 | tf_op jit(solution)/shard_map/ppermute | solution.py:527
  141.9 2.8 %shard_map.91 = bf16[16,48,512]{2,1,0:T(8,128)(2,1)} custom-call(s32[1,3072]{1,0:T(1,128)S(1)} %get-tuple-element.46.rank_ref, bf16[2048,512]{1,0:T(8,128)(2,1)S(1)} %copy-done.4, bf16[512,256]{1,0:T(8,128)(2,1)S(1)} %get-tuple-element.54.refs_0_), custom_call_target="tpu_custom_call" | custom-call | flops 99999997952 | bytes 3158016 | tf_op jit(solution)/shard_map/pallas_call | solution.py:59
  144.7 9.7 %all-to-all-done.4.refs_2_ = bf16[16,96,512]{2,1,0:T(8,128)(2,1)S(1)} async-done(((bf16[16,96,512]{2,1,0:T(8,128)(2,1)}), bf16[16,96,512]{2,1,0:T(8,128)(2,1)S(1)}, u32[]{:S(2)}, u32[]{:S(2)}) %all-to-all-start.4) | async-done | bytes 1572896 | tf_op jit(solution)/shard_map/all_to_all | solution.py:411
  154.4 5.8 %all-to-all-start.3 = ((bf16[16,48,512]{2,1,0:T(8,128)(2,1)}), bf16[16,48,512]{2,1,0:T(8,128)(2,1)S(1)}, u32[]{:S(2)}, u32[]{:S(2)}) async-start(bf16[16,48,512]{2,1,0:T(8,128)(2,1)} %shard_map.91), calls=%async_computation.3 | async-start | bytes 1572864 | tf_op jit(solution)/shard_map/all_to_all | solution.py:411
  160.2 1.7 shard_map.94
  161.9 4.6 %collective-permute-start.12 = (bf16[512,256]{1,0:T(8,128)(2,1)}, bf16[512,256]{1,0:T(8,128)(2,1)S(1)}, u32[]{:S(2)}, u32[]{:S(2)}) collective-permute-start(bf16[512,256]{1,0:T(8,128)(2,1)} %get-tuple-element.58), channel_id=1, source_target_pairs={{0,192},{2,194},{4,196},{6,198},{8,200},{10,202},{12,204},{14,206}... | collective-permute-start | bytes 786440 | tf_op jit(solution)/shard_map/ppermute | solution.py:527
  166.5 2.5 %collective-permute-start.13 = (bf16[512,256]{1,0:T(8,128)(2,1)}, bf16[512,256]{1,0:T(8,128)(2,1)S(1)}, u32[]{:S(2)}, u32[]{:S(2)}) collective-permute-start(bf16[512,256]{1,0:T(8,128)(2,1)} %get-tuple-element.59), channel_id=1, source_target_pairs={{0,128},{2,130},{4,132},{6,134},{8,136},{10,138},{12,140},{14,142}... | collective-permute-start | bytes 786440 | tf_op jit(solution)/shard_map/ppermute | solution.py:527
  169.0 1.6 collective-permute-start.15
  170.6 0.3 all-to-all-done.3.refs_2_
  170.9 0.7 shard_map.92
  171.6 0.9 collective-permute-start.9
  172.5 11.8 %collective-permute-done.13.refs_4_ = bf16[512,256]{1,0:T(8,128)(2,1)S(1)} collective-permute-done((bf16[512,256]{1,0:T(8,128)(2,1)}, bf16[512,256]{1,0:T(8,128)(2,1)S(1)}, u32[]{:S(2)}, u32[]{:S(2)}) %collective-permute-start.13) | collective-permute-done | bytes 262176 | tf_op jit(solution)/shard_map/ppermute | solution.py:527
  184.3 5.8 %collective-permute-done.14.refs_6_ = bf16[512,256]{1,0:T(8,128)(2,1)S(1)} collective-permute-done((bf16[512,256]{1,0:T(8,128)(2,1)S(1)}, bf16[512,256]{1,0:T(8,128)(2,1)S(1)}, u32[]{:S(2)}, u32[]{:S(2)}) %collective-permute-start.14) | collective-permute-done | bytes 262176 | tf_op jit(solution)/shard_map/ppermute | solution.py:527
  190.1 8.1 %collective-permute-done.15.refs_7_ = bf16[512,256]{1,0:T(8,128)(2,1)S(1)} collective-permute-done((bf16[512,256]{1,0:T(8,128)(2,1)S(1)}, bf16[512,256]{1,0:T(8,128)(2,1)S(1)}, u32[]{:S(2)}, u32[]{:S(2)}) %collective-permute-start.15) | collective-permute-done | bytes 262176 | tf_op jit(solution)/shard_map/ppermute | solution.py:527
  198.2 2.1 %shard_map.95 = (bf16[128,2048]{1,0:T(8,128)(2,1)}, bf16[128,2048]{1,0:T(8,128)(2,1)}, bf16[128,2048]{1,0:T(8,128)(2,1)}, bf16[128,2048]{1,0:T(8,128)(2,1)}) custom-call(s32[2]{0:T(128)S(1)} %copy-done.2, bf16[512,256]{1,0:T(8,128)(2,1)S(1)} %get-tuple-element.55.refs_0_, bf16[512,256]{1,0:T(8,128)(2,1)S(1)} %collective-permute-done.9.refs_1_, ...), custom_call_target="tpu_custom_call" | custom-call | bytes 4194312 | tf_op jit(solution)/shard_map/pallas_call | solution.py:59
  (16 shorter events, 0.0 us)
Async XLA Ops:
  5.2 12.9 %collective-permute-start = (bf16[528,256]{1,0:T(8,128)(2,1)}, bf16[528,256]{1,0:T(8,128)(2,1)S(1)}, u32[]{:S(2)}, u32[]{:S(2)}) collective-permute-start(bf16[528,256]{1,0:T(8,128)(2,1)} %get-tuple-element.34), channel_id=1, source_target_pairs={{0,32},{2,34},{4,36},{6,38},{8,40},{10,42},{12,44},{14,46},{16,48}... | collective-permute-start | bytes 811016 | tf_op jit(solution)/shard_map/ppermute | solution.py:439
  7.7 12.4 %collective-permute-start.1 = (bf16[528,256]{1,0:T(8,128)(2,1)}, bf16[528,256]{1,0:T(8,128)(2,1)S(1)}, u32[]{:S(2)}, u32[]{:S(2)}) collective-permute-start(bf16[528,256]{1,0:T(8,128)(2,1)} %get-tuple-element.35), channel_id=1, source_target_pairs={{0,224},{2,226},{4,228},{6,230},{8,232},{10,234},{12,236},{14,238}... | collective-permute-start | bytes 811016 | tf_op jit(solution)/shard_map/ppermute | solution.py:439
  11.8 13.9 %collective-permute-start.2 = (bf16[528,256]{1,0:T(8,128)(2,1)}, bf16[528,256]{1,0:T(8,128)(2,1)S(1)}, u32[]{:S(2)}, u32[]{:S(2)}) collective-permute-start(bf16[528,256]{1,0:T(8,128)(2,1)} %get-tuple-element.36), channel_id=1, source_target_pairs={{0,64},{2,66},{4,68},{6,70},{8,72},{10,74},{12,76},{14,78},{16,80}... | collective-permute-start | bytes 811016 | tf_op jit(solution)/shard_map/ppermute | solution.py:439
  11.8 24.5 %collective-permute-start.3 = (bf16[528,256]{1,0:T(8,128)(2,1)}, bf16[528,256]{1,0:T(8,128)(2,1)S(1)}, u32[]{:S(2)}, u32[]{:S(2)}) collective-permute-start(bf16[528,256]{1,0:T(8,128)(2,1)} %get-tuple-element.38), channel_id=1, source_target_pairs={{0,192},{2,194},{4,196},{6,198},{8,200},{10,202},{12,204},{14,206}... | collective-permute-start | bytes 811016 | tf_op jit(solution)/shard_map/ppermute | solution.py:439
  15.3 31.9 %collective-permute-start.4 = (bf16[528,256]{1,0:T(8,128)(2,1)}, bf16[528,256]{1,0:T(8,128)(2,1)S(1)}, u32[]{:S(2)}, u32[]{:S(2)}) collective-permute-start(bf16[528,256]{1,0:T(8,128)(2,1)} %get-tuple-element.39), channel_id=1, source_target_pairs={{0,96},{2,98},{4,100},{6,102},{8,104},{10,106},{12,108},{14,110},{... | collective-permute-start | bytes 811016 | tf_op jit(solution)/shard_map/ppermute | solution.py:439
  18.1 39.7 %collective-permute-start.5 = (bf16[528,256]{1,0:T(8,128)(2,1)}, bf16[528,256]{1,0:T(8,128)(2,1)S(1)}, u32[]{:S(2)}, u32[]{:S(2)}) collective-permute-start(bf16[528,256]{1,0:T(8,128)(2,1)} %get-tuple-element.40), channel_id=1, source_target_pairs={{0,160},{2,162},{4,164},{6,166},{8,168},{10,170},{12,172},{14,174}... | collective-permute-start | bytes 811016 | tf_op jit(solution)/shard_map/ppermute | solution.py:439
  20.1 37.7 %collective-permute-start.6 = (bf16[528,256]{1,0:T(8,128)(2,1)}, bf16[528,256]{1,0:T(8,128)(2,1)S(1)}, u32[]{:S(2)}, u32[]{:S(2)}) collective-permute-start(bf16[528,256]{1,0:T(8,128)(2,1)} %get-tuple-element.41), channel_id=1, source_target_pairs={{0,128},{2,130},{4,132},{6,134},{8,136},{10,138},{12,140},{14,142}... | collective-permute-start | bytes 811016 | tf_op jit(solution)/shard_map/ppermute | solution.py:439
  25.7 1.0 copy-start
  29.5 31.9 %all-to-all-start = ((bf16[16,96,512]{2,1,0:T(8,128)(2,1)}), bf16[16,96,512]{2,1,0:T(8,128)(2,1)S(1)}, u32[]{:S(2)}, u32[]{:S(2)}) async-start(bf16[16,96,512]{2,1,0:T(8,128)(2,1)} %get-tuple-element.44), calls=%async_computation | async-start | bytes 3145728 | tf_op jit(solution)/shard_map/all_to_all | solution.py:411
  61.4 29.7 %copy-start.1 = (s32[2]{0:T(128)S(1)}, s32[2]{0:T(128)}, u32[]{:S(2)}) copy-start(s32[2]{0:T(128)} %pad_add_fusion.place_ref) | copy-start | bytes 28
  99.3 12.0 %collective-permute-start.8 = (bf16[256,512]{1,0:T(8,128)(2,1)S(1)}, bf16[256,512]{1,0:T(8,128)(2,1)S(1)}, u32[]{:S(2)}, u32[]{:S(2)}) collective-permute-start(bf16[256,512]{1,0:T(8,128)(2,1)S(1)} %get-tuple-element.49), channel_id=1, source_target_pairs={{2,0},{4,2},{6,4},{8,6},{10,8},{12,10},{14,12},{18,16},{20,18},{22... | collective-permute-start | bytes 786440 | tf_op jit(solution)/shard_map/ppermute | solution.py:420
  100.6 10.7 %collective-permute-start.7 = (bf16[256,256]{1,0:T(8,128)(2,1)S(1)}, bf16[256,256]{1,0:T(8,128)(2,1)S(1)}, u32[]{:S(2)}, u32[]{:S(2)}) collective-permute-start(bf16[256,256]{1,0:T(8,128)(2,1)S(1)} %get-tuple-element.48), channel_id=1, source_target_pairs={{0,2},{2,4},{4,6},{6,8},{8,10},{10,12},{12,14},{16,18},{18,20},{20... | collective-permute-start | bytes 393224 | tf_op jit(solution)/shard_map/ppermute | solution.py:420
  115.7 16.2 %all-to-all-start.2 = ((bf16[16,48,512]{2,1,0:T(8,128)(2,1)}), bf16[16,48,512]{2,1,0:T(8,128)(2,1)S(1)}, u32[]{:S(2)}, u32[]{:S(2)}) async-start(bf16[16,48,512]{2,1,0:T(8,128)(2,1)} %get-tuple-element.53), calls=%async_computation.2 | async-start | bytes 1572864 | tf_op jit(solution)/shard_map/all_to_all | solution.py:411
  121.3 1.6 copy-start.3
  132.0 22.4 %all-to-all-start.4 = ((bf16[16,96,512]{2,1,0:T(8,128)(2,1)}), bf16[16,96,512]{2,1,0:T(8,128)(2,1)S(1)}, u32[]{:S(2)}, u32[]{:S(2)}) async-start(bf16[16,96,512]{2,1,0:T(8,128)(2,1)} %shard_map.93), calls=%async_computation.4 | async-start | bytes 3145728 | tf_op jit(solution)/shard_map/all_to_all | solution.py:411
  135.7 6.3 %copy-start.4 = (bf16[2048,512]{1,0:T(8,128)(2,1)S(1)}, bf16[2048,512]{1,0:T(8,128)(2,1)}, u32[]{:S(2)}) copy-start(bf16[2048,512]{1,0:T(8,128)(2,1)} %get-tuple-element.52.o_ref) | copy-start | bytes 6291460
  136.4 23.8 %collective-permute-start.11 = (bf16[512,256]{1,0:T(8,128)(2,1)S(1)}, bf16[512,256]{1,0:T(8,128)(2,1)S(1)}, u32[]{:S(2)}, u32[]{:S(2)}) collective-permute-start(bf16[512,256]{1,0:T(8,128)(2,1)S(1)} %get-tuple-element.57), channel_id=1, source_target_pairs={{0,96},{2,98},{4,100},{6,102},{8,104},{10,106},{12,108},{14,110},{... | collective-permute-start | bytes 786440 | tf_op jit(solution)/shard_map/ppermute | solution.py:527
  137.8 22.5 %collective-permute-start.10 = (bf16[512,256]{1,0:T(8,128)(2,1)S(1)}, bf16[512,256]{1,0:T(8,128)(2,1)S(1)}, u32[]{:S(2)}, u32[]{:S(2)}) collective-permute-start(bf16[512,256]{1,0:T(8,128)(2,1)S(1)} %get-tuple-element.54.refs_0_), channel_id=1, source_target_pairs={{0,160},{2,162},{4,164},{6,166},{8,168},{10,170},{12,172},{14,174}... | collective-permute-start | bytes 786440 | tf_op jit(solution)/shard_map/ppermute | solution.py:527
  154.4 16.5 %all-to-all-start.3 = ((bf16[16,48,512]{2,1,0:T(8,128)(2,1)}), bf16[16,48,512]{2,1,0:T(8,128)(2,1)S(1)}, u32[]{:S(2)}, u32[]{:S(2)}) async-start(bf16[16,48,512]{2,1,0:T(8,128)(2,1)} %shard_map.91), calls=%async_computation.3 | async-start | bytes 1572864 | tf_op jit(solution)/shard_map/all_to_all | solution.py:411
  161.9 10.6 %collective-permute-start.12 = (bf16[512,256]{1,0:T(8,128)(2,1)}, bf16[512,256]{1,0:T(8,128)(2,1)S(1)}, u32[]{:S(2)}, u32[]{:S(2)}) collective-permute-start(bf16[512,256]{1,0:T(8,128)(2,1)} %get-tuple-element.58), channel_id=1, source_target_pairs={{0,192},{2,194},{4,196},{6,198},{8,200},{10,202},{12,204},{14,206}... | collective-permute-start | bytes 786440 | tf_op jit(solution)/shard_map/ppermute | solution.py:527
  166.5 17.8 %collective-permute-start.13 = (bf16[512,256]{1,0:T(8,128)(2,1)}, bf16[512,256]{1,0:T(8,128)(2,1)S(1)}, u32[]{:S(2)}, u32[]{:S(2)}) collective-permute-start(bf16[512,256]{1,0:T(8,128)(2,1)} %get-tuple-element.59), channel_id=1, source_target_pairs={{0,128},{2,130},{4,132},{6,134},{8,136},{10,138},{12,140},{14,142}... | collective-permute-start | bytes 786440 | tf_op jit(solution)/shard_map/ppermute | solution.py:527
  169.0 21.1 %collective-permute-start.14 = (bf16[512,256]{1,0:T(8,128)(2,1)S(1)}, bf16[512,256]{1,0:T(8,128)(2,1)S(1)}, u32[]{:S(2)}, u32[]{:S(2)}) collective-permute-start(bf16[512,256]{1,0:T(8,128)(2,1)S(1)} %get-tuple-element.60), channel_id=1, source_target_pairs={{0,64},{2,66},{4,68},{6,70},{8,72},{10,74},{12,76},{14,78},{16,80}... | collective-permute-start | bytes 786440 | tf_op jit(solution)/shard_map/ppermute | solution.py:527
  169.0 29.2 %copy-start.2 = (s32[2]{0:T(128)S(1)}, s32[2]{0:T(128)}, u32[]{:S(2)}) copy-start(s32[2]{0:T(128)} %pad_add_fusion.place_ref) | copy-start | bytes 28
  169.0 29.1 %collective-permute-start.15 = (bf16[512,256]{1,0:T(8,128)(2,1)S(1)}, bf16[512,256]{1,0:T(8,128)(2,1)S(1)}, u32[]{:S(2)}, u32[]{:S(2)}) collective-permute-start(bf16[512,256]{1,0:T(8,128)(2,1)S(1)} %get-tuple-element.61), channel_id=1, source_target_pairs={{0,32},{2,34},{4,36},{6,38},{8,40},{10,42},{12,44},{14,46},{16,48}... | collective-permute-start | bytes 786440 | tf_op jit(solution)/shard_map/ppermute | solution.py:527
  171.6 26.6 %collective-permute-start.9 = (bf16[512,256]{1,0:T(8,128)(2,1)S(1)}, bf16[512,256]{1,0:T(8,128)(2,1)S(1)}, u32[]{:S(2)}, u32[]{:S(2)}) collective-permute-start(bf16[512,256]{1,0:T(8,128)(2,1)S(1)} %get-tuple-element.56), channel_id=1, source_target_pairs={{0,224},{2,226},{4,228},{6,230},{8,232},{10,234},{12,236},{14,238}... | collective-permute-start | bytes 786440 | tf_op jit(solution)/shard_map/ppermute | solution.py:527

commit v3 on v2

--- a/solution.py
+++ b/solution.py
@@ -32,10 +32,11 @@
 I32 = jnp.int32
 
 CHUNKS = ((0, 1, 7, 2), (6, 3, 5, 4))
-PICK_HINT = (0, 10**9, 10**11)
+PICK_HINT = (0, 10**9, 10**9)
 UNPACK_HINT = (10**9, 10**11, 10**9)
 RETURNS = ((3, 5), (4, 2, 6, 7), (0, 1))
 ORDER = sum(CHUNKS, ())
+SOON = (2, 6)
 PACK_HINT = (10**6, 10**11)
 PLANES = [[z * PLANE + i for i in range(PLANE)] for z in range(ZN)]
 
@@ -385,6 +386,11 @@
                     blocks[p + j][t * TOK : (t + 1) * TOK, hh * WIDTH : (hh + 1) * WIDTH] = got[
                         j * TOK : (j + 1) * TOK, t * WIDTH : (t + 1) * WIDTH
                     ]
+
+
+def mark_kernel(place_ref, *refs):
+    mark_ref = refs[-1]
+    mark_ref[...] = jnp.broadcast_to(place_ref[0], mark_ref.shape).astype(F32)
 
 
 def join_kernel(place_ref, *refs):
@@ -483,51 +489,61 @@
         [pltpu.VMEM((SPANS, SPAN, PAIR), F32)],
         flops=14 * SPANS * SPAN * 2 * SPAN * WIDTH,
     )
-    o = None
-    back = {}
-    waits = {}
+    sends = []
     for step, chunk in enumerate(RETURNS):
         rows = len(chunk) * MOST
         at = tuple(ORDER.index(d) for d in chunk)
         send_shape = out((PLANE, rows, ALL), BF)
-        flops = 2 * BLOCK * PLANE * rows * ALL
         stage = [pltpu.VMEM((PLANE, rows, ALL), BF), pltpu.SemaphoreType.DMA((PICKS,))]
-        if o is None:
+        if step == 0:
             o, send = call(
                 functools.partial(edge_kernel, at),
                 [place, rank, rows_in, tail, head, main, part],
                 [out((BLOCK, ALL), BF), send_shape],
                 [pltpu.VMEM((BLOCK, ALL), BF)] + stage + [pltpu.SemaphoreType.DMA((1,))],
-                flops=flops,
+                flops=2 * BLOCK * PLANE * rows * ALL,
                 specs=SMEM,
                 out_specs={0: hbm, 1: hbm},
             )
         else:
             (send,) = call(
                 functools.partial(pick_kernel, at),
-                [rank, o] + waits.get(("pick", step), []),
+                [rank, o],
                 [send_shape],
                 stage,
                 flops=PICK_HINT[step],
-                specs={2: anywhere},
                 out_specs={0: hbm},
             )
-        got = exchange(send, PLANES)
+        sends.append(send)
+    back = {}
+    waits = {}
+    for step, chunk in enumerate(RETURNS):
+        got = exchange(sends[step], PLANES)
         places = tuple(
             (i, c.index(d)) for d in chunk for i, c in enumerate(CHUNKS) if d in c
         )
+        wait = waits.get(step, [])
         pieces = call(
             functools.partial(unpack_kernel, places),
-            codes + [got] + waits.get(("unpack", step), []),
+            codes + [got] + wait,
             [out((4 * TOK, PAIR), BF)] * len(chunk),
             flops=UNPACK_HINT[step],
-            specs={j: anywhere for j in range(len(codes) + 1, len(codes) + 5)},
+            specs={len(codes) + 1 + j: anywhere for j in range(len(wait))},
         )
         for d, piece in zip(chunk, pieces):
             back[d] = lax.ppermute(piece, "seq", z_pairs(-d)) if d else piece
-        waits["pick", step + 2] = [pieces[0]]
         if step == 0:
-            waits["unpack", 1] = [back[d] for d in chunk]
+            waits[1] = [back[d] for d in chunk] + [sends[2]]
+        if step == 1:
+            waits[2] = list(
+                call(
+                    mark_kernel,
+                    [place] + [back[d] for d in SOON],
+                    [out((8, WIDTH), F32)],
+                    specs={0: SMEM[0]} | {j + 1: anywhere for j in range(len(SOON))},
+                    flops=10**11,
+                )
+            )
     return call(
         join_kernel,
         [place] + [back[d] for d in range(ZN)],

time: 202 us -> 197 us (0.975)
  waiting for transfers between devices: 66 us -> 58.1 us
  starting transfers between devices: 58.5 us -> 62 us
    all_to_all x4, waiting for transfers between devices: 14.4 us -> 7.72 us  [exchange(): lax.all_to_all(array, 'seq', split_axis=0, concat_axis=0, axis_index_grou...]
    ppermute x7, starting transfers between devices: 15.1 us -> 17.8 us  [body(): back[d] = lax.ppermute(piece, 'seq', z_pairs(-d)) if d else piece]
    pallas_call x12 -> x13, Pallas kernels: 42 us -> 42 us  [call(): pl.pallas_call(kernel, out_shape=tuple((pltpu.HBM(o.shape, o.dtype) if i...]
  transfers between devices with their start and end apart: 20 -> 20, of which waited for: 10 -> 10; matrix products, arithmetic and copies ran while one was open for 0% -> 0% of each run, Pallas kernels for 12% -> 11%
where the time goes in v3:
time: 197 us; the launch traced here: 196 us
  starting transfers between devices  62 us (31%)
  waiting for transfers between devices  58.1 us (29%)
  Pallas kernels  42 us (21%)
  blocking collectives  29.7 us (15%)
  local copies, waits for them, and re-layouts  2.55 us (1%)
    pallas_call x13, Pallas kernels, call(): pl.pallas_call(kernel, out_shape=tuple((pltpu.HBM(o.shape, o.dtype) if i...  42 us
    all_to_all x1, blocking collectives, exchange(): lax.all_to_all(array, 'seq', split_axis=0, concat_axis=0, axis_index_grou...  29.7 us
    ppermute x7, waiting for transfers between devices, body(): moved[d] = lax.ppermute(blocks[d], 'seq', z_pairs(d))  25.9 us
    ppermute x7, waiting for transfers between devices, body(): back[d] = lax.ppermute(piece, 'seq', z_pairs(-d)) if d else piece  24.5 us
    all_to_all x4, starting transfers between devices, exchange(): lax.all_to_all(array, 'seq', split_axis=0, concat_axis=0, axis_index_grou...  22.6 us
    ppermute x7, starting transfers between devices, body(): back[d] = lax.ppermute(piece, 'seq', z_pairs(-d)) if d else piece  17.8 us
    ppermute x7, starting transfers between devices, body(): moved[d] = lax.ppermute(blocks[d], 'seq', z_pairs(d))  16.1 us
    all_to_all x4, waiting for transfers between devices, exchange(): lax.all_to_all(array, 'seq', split_axis=0, concat_axis=0, axis_index_grou...  7.72 us
  transfers between devices with their start and end apart: 20, of which 10 were waited for; matrix products, arithmetic and copies ran while one was open for 0% of the time, Pallas kernels for 11%

profile of v3, /device:TPU:1, one launch (start us, length us, event | category | flops | bytes accessed | tf_op | source)
XLA Modules:
  0.0 196.1 jit_solution(9605483482969187706)
XLA Ops:
  0.7 0.6 pad_add_fusion.place_ref
  1.3 3.9 %shard_map.84 = (bf16[528,256]{1,0:T(8,128)(2,1)}, bf16[528,256]{1,0:T(8,128)(2,1)}, bf16[528,256]{1,0:T(8,128)(2,1)}, bf16[528,256]{1,0:T(8,128)(2,1)}, bf16[52...) custom-call(s32[2]{0:T(128)} %pad_add_fusion.place_ref, ...), custom_call_target="tpu_custom_call" | custom-call | bytes 4268040 | tf_op jit(solution)/shard_map/pallas_call | solution.py:60
  5.2 2.5 %collective-permute-start = (bf16[528,256]{1,0:T(8,128)(2,1)}, bf16[528,256]{1,0:T(8,128)(2,1)S(1)}, u32[]{:S(2)}, u32[]{:S(2)}) collective-permute-start(bf16[528,256]{1,0:T(8,128)(2,1)} %get-tuple-element.34), channel_id=1, source_target_pairs={{0,32},{2,34},{4,36},{6,38},{8,40},{10,42},{12,44},{14,46},{16,48}... | collective-permute-start | bytes 811016 | tf_op jit(solution)/shard_map/ppermute | solution.py:445
  7.7 4.0 %collective-permute-start.1 = (bf16[528,256]{1,0:T(8,128)(2,1)}, bf16[528,256]{1,0:T(8,128)(2,1)S(1)}, u32[]{:S(2)}, u32[]{:S(2)}) collective-permute-start(bf16[528,256]{1,0:T(8,128)(2,1)} %get-tuple-element.35), channel_id=1, source_target_pairs={{0,224},{2,226},{4,228},{6,230},{8,232},{10,234},{12,236},{14,238}... | collective-permute-start | bytes 811016 | tf_op jit(solution)/shard_map/ppermute | solution.py:445
  11.8 3.6 %collective-permute-start.3 = (bf16[528,256]{1,0:T(8,128)(2,1)}, bf16[528,256]{1,0:T(8,128)(2,1)S(1)}, u32[]{:S(2)}, u32[]{:S(2)}) collective-permute-start(bf16[528,256]{1,0:T(8,128)(2,1)} %get-tuple-element.38), channel_id=1, source_target_pairs={{0,192},{2,194},{4,196},{6,198},{8,200},{10,202},{12,204},{14,206}... | collective-permute-start | bytes 811016 | tf_op jit(solution)/shard_map/ppermute | solution.py:445
  15.3 0.3 collective-permute-start.4
  15.7 2.4 %collective-permute-done.refs_1_ = bf16[528,256]{1,0:T(8,128)(2,1)S(1)} collective-permute-done((bf16[528,256]{1,0:T(8,128)(2,1)}, bf16[528,256]{1,0:T(8,128)(2,1)S(1)}, u32[]{:S(2)}, u32[]{:S(2)}) %collective-permute-start) | collective-permute-done | bytes 270368 | tf_op jit(solution)/shard_map/ppermute | solution.py:445
  18.1 2.0 %collective-permute-start.5 = (bf16[528,256]{1,0:T(8,128)(2,1)}, bf16[528,256]{1,0:T(8,128)(2,1)S(1)}, u32[]{:S(2)}, u32[]{:S(2)}) collective-permute-start(bf16[528,256]{1,0:T(8,128)(2,1)} %get-tuple-element.40), channel_id=1, source_target_pairs={{0,160},{2,162},{4,164},{6,166},{8,168},{10,170},{12,172},{14,174}... | collective-permute-start | bytes 811016 | tf_op jit(solution)/shard_map/ppermute | solution.py:445
  20.1 0.0 collective-permute-done.1.refs_2_
  20.1 3.6 %collective-permute-start.6 = (bf16[528,256]{1,0:T(8,128)(2,1)}, bf16[528,256]{1,0:T(8,128)(2,1)S(1)}, u32[]{:S(2)}, u32[]{:S(2)}) collective-permute-start(bf16[528,256]{1,0:T(8,128)(2,1)} %get-tuple-element.41), channel_id=1, source_target_pairs={{0,128},{2,130},{4,132},{6,134},{8,136},{10,138},{12,140},{14,142}... | collective-permute-start | bytes 811016 | tf_op jit(solution)/shard_map/ppermute | solution.py:445
  23.8 1.9 collective-permute-done.2.refs_3_
  25.7 1.0 copy-done
  26.7 2.8 %shard_map.85 = (bf16[16,96,512]{2,1,0:T(8,128)(2,1)}, s32[8,128]{1,0:T(8,128)S(1)}, bf16[16,16,128]{2,1,0:T(8,128)(2,1)S(1)}) custom-call(bf16[528,256]{1,0:T(8,128)(2,1)S(1)} %copy-done, bf16[528,256]{1,0:T(8,128)(2,1)S(1)} %collective-permute-done.refs_1_, bf16[528,256]{1,0:T(8,128)(2,1)S(1)} %collective-permute-done.1.refs_2_, ...), custom_call_target="tpu_custom_call" | custom-call | flops 1000000 | bytes 2723840 | tf_op jit(solution)/shard_map/pallas_call | solution.py:60
  29.5 6.8 %all-to-all-start = ((bf16[16,96,512]{2,1,0:T(8,128)(2,1)}), bf16[16,96,512]{2,1,0:T(8,128)(2,1)S(1)}, u32[]{:S(2)}, u32[]{:S(2)}) async-start(bf16[16,96,512]{2,1,0:T(8,128)(2,1)} %get-tuple-element.44), calls=%async_computation | async-start | bytes 3145728 | tf_op jit(solution)/shard_map/all_to_all | solution.py:417
  36.3 10.9 %collective-permute-done.4.refs_1_ = bf16[528,256]{1,0:T(8,128)(2,1)S(1)} collective-permute-done((bf16[528,256]{1,0:T(8,128)(2,1)}, bf16[528,256]{1,0:T(8,128)(2,1)S(1)}, u32[]{:S(2)}, u32[]{:S(2)}) %collective-permute-start.4) | collective-permute-done | bytes 270368 | tf_op jit(solution)/shard_map/ppermute | solution.py:445
  47.2 10.5 %collective-permute-done.5.refs_2_ = bf16[528,256]{1,0:T(8,128)(2,1)S(1)} collective-permute-done((bf16[528,256]{1,0:T(8,128)(2,1)}, bf16[528,256]{1,0:T(8,128)(2,1)S(1)}, u32[]{:S(2)}, u32[]{:S(2)}) %collective-permute-start.5) | collective-permute-done | bytes 270368 | tf_op jit(solution)/shard_map/ppermute | solution.py:445
  57.8 3.6 %shard_map.86 = (bf16[16,112,512]{2,1,0:T(8,128)(2,1)}, s32[8,128]{1,0:T(8,128)S(1)}, bf16[16,16,128]{2,1,0:T(8,128)(2,1)}) custom-call(bf16[528,256]{1,0:T(8,128)(2,1)S(1)} %collective-permute-done.3.refs_0_, bf16[528,256]{1,0:T(8,128)(2,1)S(1)} %collective-permute-done.4.refs_1_, bf16[528,256]{1,0:T(8,128)(2,1)S(1)} %collective-permute-done.5.refs_2_, ...), custom_call_target="tpu_custom_call" | custom-call | flops 99999997952 | bytes 3051520 | tf_op jit(solution)/shard_map/pallas_call | solution.py:60
  61.4 29.7 %all_to_all.25.refs_1_ = bf16[16,112,512]{2,1,0:T(8,128)(2,1)S(1)} all-to-all(bf16[16,112,512]{2,1,0:T(8,128)(2,1)} %get-tuple-element.45), channel_id=1, replica_groups={{0,2,4,6,8,10,12,14,16,18,20,22,24,26,28,30},{32,34,36,38,40,42,44,46,4..., dimensions={0} | all-to-all | bytes 3670016 | tf_op jit(solution)/shard_map/all_to_all | solution.py:417
  91.2 8.1 %shard_map.87 = (bf16[8,256,512]{2,1,0:T(8,128)(2,1)S(1)}, bf16[256,256]{1,0:T(8,128)(2,1)S(1)}, bf16[256,512]{1,0:T(8,128)(2,1)S(1)}, s32[1,3072]{1,0:T(1,128)S(1)}) custom-call(s32[2]{0:T(128)S(1)} %copy-done.1, bf16[16,96,512]{2,1,0:T(8,128)(2,1)S(1)} %all-to-all-done.refs_0_, bf16[16,112,512]{2,1,0:T(8,128)(2,1)S(1)} %all_to_all.25.refs_1_), custom_call_target="tpu_custom_call" | custom-call | flops 6442450944 | bytes 5910536 | tf_op jit(solution)/shard_map/pallas_call | solution.py:60
  99.3 1.3 collective-permute-start.8
  100.6 4.2 %collective-permute-start.7 = (bf16[256,256]{1,0:T(8,128)(2,1)S(1)}, bf16[256,256]{1,0:T(8,128)(2,1)S(1)}, u32[]{:S(2)}, u32[]{:S(2)}) collective-permute-start(bf16[256,256]{1,0:T(8,128)(2,1)S(1)} %get-tuple-element.48), channel_id=1, source_target_pairs={{0,2},{2,4},{4,6},{6,8},{8,10},{10,12},{12,14},{16,18},{18,20},{20... | collective-permute-start | bytes 393224 | tf_op jit(solution)/shard_map/ppermute | solution.py:426
  104.8 6.5 %shard_map.88 = (bf16[8,256,512]{2,1,0:T(8,128)(2,1)S(1)}, f32[2,256,256]{2,1,0:T(8,128)S(1)}) custom-call(bf16[8,256,512]{2,1,0:T(8,128)(2,1)S(1)} %get-tuple-element.47.in_ref), custom_call_target="tpu_custom_call" | custom-call | flops 1879048192 | bytes 4718592 | tf_op jit(solution)/shard_map/pallas_call | solution.py:60
  111.3 0.0 collective-permute-done.7.tail_ref
  111.3 0.0 collective-permute-done.8.head_ref
  111.3 4.4 %shard_map.89 = (bf16[2048,512]{1,0:T(8,128)(2,1)}, bf16[16,48,512]{2,1,0:T(8,128)(2,1)}) custom-call(s32[2]{0:T(128)S(1)} %copy-done.1, s32[1,3072]{1,0:T(1,128)S(1)} %get-tuple-element.46.rank_ref, bf16[8,256,512]{2,1,0:T(8,128)(2,1)S(1)} %get-tuple-element.47.in_ref, bf16[256,256]{1,0:T(8,128)(2,1)S(1)} %collective-permute-done.7.tail_ref, ...), custom_call_target="tpu_custom_call" | custom-call | flops 1610612736 | bytes 8007688 | tf_op jit(solution)/shard_map/pallas_call | solution.py:60
  115.8 5.5 %all-to-all-start.4 = ((bf16[16,48,512]{2,1,0:T(8,128)(2,1)}), bf16[16,48,512]{2,1,0:T(8,128)(2,1)S(1)}, u32[]{:S(2)}, u32[]{:S(2)}) async-start(bf16[16,48,512]{2,1,0:T(8,128)(2,1)} %get-tuple-element.53), calls=%async_computation.4 | async-start | bytes 1572864 | tf_op jit(solution)/shard_map/all_to_all | solution.py:417
  121.3 1.6 copy-done.2
  122.9 4.7 %shard_map.91 = bf16[16,96,512]{2,1,0:T(8,128)(2,1)} custom-call(s32[1,3072]{1,0:T(1,128)S(1)} %get-tuple-element.46.rank_ref, bf16[2048,512]{1,0:T(8,128)(2,1)S(1)} %copy-done.2), custom_call_target="tpu_custom_call" | custom-call | flops 1000000000 | bytes 3682304 | tf_op jit(solution)/shard_map/pallas_call | solution.py:60
  127.6 4.4 %all-to-all-done.4.refs_2_ = bf16[16,48,512]{2,1,0:T(8,128)(2,1)S(1)} async-done(((bf16[16,48,512]{2,1,0:T(8,128)(2,1)}), bf16[16,48,512]{2,1,0:T(8,128)(2,1)S(1)}, u32[]{:S(2)}, u32[]{:S(2)}) %all-to-all-start.4) | async-done | bytes 786464 | tf_op jit(solution)/shard_map/all_to_all | solution.py:417
  132.0 3.7 %all-to-all-start.3 = ((bf16[16,96,512]{2,1,0:T(8,128)(2,1)}), bf16[16,96,512]{2,1,0:T(8,128)(2,1)S(1)}, u32[]{:S(2)}, u32[]{:S(2)}) async-start(bf16[16,96,512]{2,1,0:T(8,128)(2,1)} %shard_map.91), calls=%async_computation.3 | async-start | bytes 3145728 | tf_op jit(solution)/shard_map/all_to_all | solution.py:417
  135.7 0.7 shard_map.92
  136.4 5.5 %collective-permute-start.9 = (bf16[512,256]{1,0:T(8,128)(2,1)S(1)}, bf16[512,256]{1,0:T(8,128)(2,1)S(1)}, u32[]{:S(2)}, u32[]{:S(2)}) collective-permute-start(bf16[512,256]{1,0:T(8,128)(2,1)S(1)} %get-tuple-element.54), channel_id=1, source_target_pairs={{0,160},{2,162},{4,164},{6,166},{8,168},{10,170},{12,172},{14,174}... | collective-permute-start | bytes 786440 | tf_op jit(solution)/shard_map/ppermute | solution.py:534
  141.9 2.8 %shard_map.90.refs_5_ = bf16[16,48,512]{2,1,0:T(8,128)(2,1)} custom-call(s32[1,3072]{1,0:T(1,128)S(1)} %get-tuple-element.46.rank_ref, bf16[2048,512]{1,0:T(8,128)(2,1)S(1)} %copy-done.3), custom_call_target="tpu_custom_call" | custom-call | flops 1000000000 | bytes 2895872 | tf_op jit(solution)/shard_map/pallas_call | solution.py:60
  144.7 5.3 %collective-permute-done.9.refs_3_ = bf16[512,256]{1,0:T(8,128)(2,1)S(1)} collective-permute-done((bf16[512,256]{1,0:T(8,128)(2,1)S(1)}, bf16[512,256]{1,0:T(8,128)(2,1)S(1)}, u32[]{:S(2)}, u32[]{:S(2)}) %collective-permute-start.9) | collective-permute-done | bytes 262176 | tf_op jit(solution)/shard_map/ppermute | solution.py:534
  150.0 7.2 %collective-permute-done.10.refs_4_.refs_5_ = bf16[512,256]{1,0:T(8,128)(2,1)S(1)} collective-permute-done((bf16[512,256]{1,0:T(8,128)(2,1)S(1)}, bf16[512,256]{1,0:T(8,128)(2,1)S(1)}, u32[]{:S(2)}, u32[]{:S(2)}) %collective-permute-start.10) | collective-permute-done | bytes 262176 | tf_op jit(solution)/shard_map/ppermute | solution.py:534
  157.2 1.1 shard_map.93
  158.3 1.9 collective-permute-start.11
  160.3 0.5 collective-permute-start.12
  160.8 6.6 %all-to-all-start.2 = ((bf16[16,48,512]{2,1,0:T(8,128)(2,1)}), bf16[16,48,512]{2,1,0:T(8,128)(2,1)S(1)}, u32[]{:S(2)}, u32[]{:S(2)}) async-start(bf16[16,48,512]{2,1,0:T(8,128)(2,1)} %shard_map.90.refs_5_), calls=%async_computation.2 | async-start | bytes 1572864 | tf_op jit(solution)/shard_map/all_to_all | solution.py:417
  167.4 3.5 %collective-permute-start.14 = (bf16[512,256]{1,0:T(8,128)(2,1)S(1)}, bf16[512,256]{1,0:T(8,128)(2,1)S(1)}, u32[]{:S(2)}, u32[]{:S(2)}) collective-permute-start(bf16[512,256]{1,0:T(8,128)(2,1)S(1)} %get-tuple-element.60), channel_id=1, source_target_pairs={{0,128},{2,130},{4,132},{6,134},{8,136},{10,138},{12,140},{14,142}... | collective-permute-start | bytes 786440 | tf_op jit(solution)/shard_map/ppermute | solution.py:534
  170.8 3.1 %collective-permute-start.15 = (bf16[512,256]{1,0:T(8,128)(2,1)S(1)}, bf16[512,256]{1,0:T(8,128)(2,1)S(1)}, u32[]{:S(2)}, u32[]{:S(2)}) collective-permute-start(bf16[512,256]{1,0:T(8,128)(2,1)S(1)} %get-tuple-element.61), channel_id=1, source_target_pairs={{0,32},{2,34},{4,36},{6,38},{8,40},{10,42},{12,44},{14,46},{16,48}... | collective-permute-start | bytes 786440 | tf_op jit(solution)/shard_map/ppermute | solution.py:534
  174.0 0.5 shard_map.94.refs_3_
  174.5 3.3 %all-to-all-done.2.refs_2_ = bf16[16,48,512]{2,1,0:T(8,128)(2,1)S(1)} async-done(((bf16[16,48,512]{2,1,0:T(8,128)(2,1)}), bf16[16,48,512]{2,1,0:T(8,128)(2,1)S(1)}, u32[]{:S(2)}, u32[]{:S(2)}) %all-to-all-start.2) | async-done | bytes 786464 | tf_op jit(solution)/shard_map/all_to_all | solution.py:417
  177.8 0.7 shard_map.95
  178.5 3.3 %collective-permute-start.13 = (bf16[512,256]{1,0:T(8,128)(2,1)S(1)}, bf16[512,256]{1,0:T(8,128)(2,1)S(1)}, u32[]{:S(2)}, u32[]{:S(2)}) collective-permute-start(bf16[512,256]{1,0:T(8,128)(2,1)S(1)} %get-tuple-element.59), channel_id=1, source_target_pairs={{0,224},{2,226},{4,228},{6,230},{8,232},{10,234},{12,236},{14,238}... | collective-permute-start | bytes 786440 | tf_op jit(solution)/shard_map/ppermute | solution.py:534
  181.8 3.2 %collective-permute-done.14.refs_4_ = bf16[512,256]{1,0:T(8,128)(2,1)S(1)} collective-permute-done((bf16[512,256]{1,0:T(8,128)(2,1)S(1)}, bf16[512,256]{1,0:T(8,128)(2,1)S(1)}, u32[]{:S(2)}, u32[]{:S(2)}) %collective-permute-start.14) | collective-permute-done | bytes 262176 | tf_op jit(solution)/shard_map/ppermute | solution.py:534
  185.0 8.8 %collective-permute-done.15.refs_7_ = bf16[512,256]{1,0:T(8,128)(2,1)S(1)} collective-permute-done((bf16[512,256]{1,0:T(8,128)(2,1)S(1)}, bf16[512,256]{1,0:T(8,128)(2,1)S(1)}, u32[]{:S(2)}, u32[]{:S(2)}) %collective-permute-start.15) | collective-permute-done | bytes 262176 | tf_op jit(solution)/shard_map/ppermute | solution.py:534
  193.8 2.1 %shard_map.96 = (bf16[128,2048]{1,0:T(8,128)(2,1)}, bf16[128,2048]{1,0:T(8,128)(2,1)}, bf16[128,2048]{1,0:T(8,128)(2,1)}, bf16[128,2048]{1,0:T(8,128)(2,1)}) custom-call(s32[2]{0:T(128)S(1)} %copy-done.1, bf16[512,256]{1,0:T(8,128)(2,1)S(1)} %get-tuple-element.58.refs_0_, bf16[512,256]{1,0:T(8,128)(2,1)S(1)} %collective-permute-done.13.refs_1_, ...), custom_call_target="tpu_custom_call" | custom-call | bytes 4194312 | tf_op jit(solution)/shard_map/pallas_call | solution.py:60
  (15 shorter events, 0.0 us)
Async XLA Ops:
  5.2 12.9 %collective-permute-start = (bf16[528,256]{1,0:T(8,128)(2,1)}, bf16[528,256]{1,0:T(8,128)(2,1)S(1)}, u32[]{:S(2)}, u32[]{:S(2)}) collective-permute-start(bf16[528,256]{1,0:T(8,128)(2,1)} %get-tuple-element.34), channel_id=1, source_target_pairs={{0,32},{2,34},{4,36},{6,38},{8,40},{10,42},{12,44},{14,46},{16,48}... | collective-permute-start | bytes 811016 | tf_op jit(solution)/shard_map/ppermute | solution.py:445
  7.7 12.4 %collective-permute-start.1 = (bf16[528,256]{1,0:T(8,128)(2,1)}, bf16[528,256]{1,0:T(8,128)(2,1)S(1)}, u32[]{:S(2)}, u32[]{:S(2)}) collective-permute-start(bf16[528,256]{1,0:T(8,128)(2,1)} %get-tuple-element.35), channel_id=1, source_target_pairs={{0,224},{2,226},{4,228},{6,230},{8,232},{10,234},{12,236},{14,238}... | collective-permute-start | bytes 811016 | tf_op jit(solution)/shard_map/ppermute | solution.py:445
  11.8 13.9 %collective-permute-start.2 = (bf16[528,256]{1,0:T(8,128)(2,1)}, bf16[528,256]{1,0:T(8,128)(2,1)S(1)}, u32[]{:S(2)}, u32[]{:S(2)}) collective-permute-start(bf16[528,256]{1,0:T(8,128)(2,1)} %get-tuple-element.36), channel_id=1, source_target_pairs={{0,64},{2,66},{4,68},{6,70},{8,72},{10,74},{12,76},{14,78},{16,80}... | collective-permute-start | bytes 811016 | tf_op jit(solution)/shard_map/ppermute | solution.py:445
  11.8 24.5 %collective-permute-start.3 = (bf16[528,256]{1,0:T(8,128)(2,1)}, bf16[528,256]{1,0:T(8,128)(2,1)S(1)}, u32[]{:S(2)}, u32[]{:S(2)}) collective-permute-start(bf16[528,256]{1,0:T(8,128)(2,1)} %get-tuple-element.38), channel_id=1, source_target_pairs={{0,192},{2,194},{4,196},{6,198},{8,200},{10,202},{12,204},{14,206}... | collective-permute-start | bytes 811016 | tf_op jit(solution)/shard_map/ppermute | solution.py:445
  15.3 31.9 %collective-permute-start.4 = (bf16[528,256]{1,0:T(8,128)(2,1)}, bf16[528,256]{1,0:T(8,128)(2,1)S(1)}, u32[]{:S(2)}, u32[]{:S(2)}) collective-permute-start(bf16[528,256]{1,0:T(8,128)(2,1)} %get-tuple-element.39), channel_id=1, source_target_pairs={{0,96},{2,98},{4,100},{6,102},{8,104},{10,106},{12,108},{14,110},{... | collective-permute-start | bytes 811016 | tf_op jit(solution)/shard_map/ppermute | solution.py:445
  18.1 39.7 %collective-permute-start.5 = (bf16[528,256]{1,0:T(8,128)(2,1)}, bf16[528,256]{1,0:T(8,128)(2,1)S(1)}, u32[]{:S(2)}, u32[]{:S(2)}) collective-permute-start(bf16[528,256]{1,0:T(8,128)(2,1)} %get-tuple-element.40), channel_id=1, source_target_pairs={{0,160},{2,162},{4,164},{6,166},{8,168},{10,170},{12,172},{14,174}... | collective-permute-start | bytes 811016 | tf_op jit(solution)/shard_map/ppermute | solution.py:445
  20.1 37.7 %collective-permute-start.6 = (bf16[528,256]{1,0:T(8,128)(2,1)}, bf16[528,256]{1,0:T(8,128)(2,1)S(1)}, u32[]{:S(2)}, u32[]{:S(2)}) collective-permute-start(bf16[528,256]{1,0:T(8,128)(2,1)} %get-tuple-element.41), channel_id=1, source_target_pairs={{0,128},{2,130},{4,132},{6,134},{8,136},{10,138},{12,140},{14,142}... | collective-permute-start | bytes 811016 | tf_op jit(solution)/shard_map/ppermute | solution.py:445
  25.7 1.0 copy-start
  29.5 31.9 %all-to-all-start = ((bf16[16,96,512]{2,1,0:T(8,128)(2,1)}), bf16[16,96,512]{2,1,0:T(8,128)(2,1)S(1)}, u32[]{:S(2)}, u32[]{:S(2)}) async-start(bf16[16,96,512]{2,1,0:T(8,128)(2,1)} %get-tuple-element.44), calls=%async_computation | async-start | bytes 3145728 | tf_op jit(solution)/shard_map/all_to_all | solution.py:417
  61.4 29.7 %copy-start.1 = (s32[2]{0:T(128)S(1)}, s32[2]{0:T(128)}, u32[]{:S(2)}) copy-start(s32[2]{0:T(128)} %pad_add_fusion.place_ref) | copy-start | bytes 28
  99.3 12.0 %collective-permute-start.8 = (bf16[256,512]{1,0:T(8,128)(2,1)S(1)}, bf16[256,512]{1,0:T(8,128)(2,1)S(1)}, u32[]{:S(2)}, u32[]{:S(2)}) collective-permute-start(bf16[256,512]{1,0:T(8,128)(2,1)S(1)} %get-tuple-element.49), channel_id=1, source_target_pairs={{2,0},{4,2},{6,4},{8,6},{10,8},{12,10},{14,12},{18,16},{20,18},{22... | collective-permute-start | bytes 786440 | tf_op jit(solution)/shard_map/ppermute | solution.py:426
  100.6 10.7 %collective-permute-start.7 = (bf16[256,256]{1,0:T(8,128)(2,1)S(1)}, bf16[256,256]{1,0:T(8,128)(2,1)S(1)}, u32[]{:S(2)}, u32[]{:S(2)}) collective-permute-start(bf16[256,256]{1,0:T(8,128)(2,1)S(1)} %get-tuple-element.48), channel_id=1, source_target_pairs={{0,2},{2,4},{4,6},{6,8},{8,10},{10,12},{12,14},{16,18},{18,20},{20... | collective-permute-start | bytes 393224 | tf_op jit(solution)/shard_map/ppermute | solution.py:426
  115.8 16.2 %all-to-all-start.4 = ((bf16[16,48,512]{2,1,0:T(8,128)(2,1)}), bf16[16,48,512]{2,1,0:T(8,128)(2,1)S(1)}, u32[]{:S(2)}, u32[]{:S(2)}) async-start(bf16[16,48,512]{2,1,0:T(8,128)(2,1)} %get-tuple-element.53), calls=%async_computation.4 | async-start | bytes 1572864 | tf_op jit(solution)/shard_map/all_to_all | solution.py:417
  121.3 1.6 copy-start.2
  132.0 25.2 %all-to-all-start.3 = ((bf16[16,96,512]{2,1,0:T(8,128)(2,1)}), bf16[16,96,512]{2,1,0:T(8,128)(2,1)S(1)}, u32[]{:S(2)}, u32[]{:S(2)}) async-start(bf16[16,96,512]{2,1,0:T(8,128)(2,1)} %shard_map.91), calls=%async_computation.3 | async-start | bytes 3145728 | tf_op jit(solution)/shard_map/all_to_all | solution.py:417
  135.7 6.2 %copy-start.3 = (bf16[2048,512]{1,0:T(8,128)(2,1)S(1)}, bf16[2048,512]{1,0:T(8,128)(2,1)}, u32[]{:S(2)}) copy-start(bf16[2048,512]{1,0:T(8,128)(2,1)} %get-tuple-element.52.o_ref) | copy-start | bytes 6291460
  136.4 13.6 %collective-permute-start.9 = (bf16[512,256]{1,0:T(8,128)(2,1)S(1)}, bf16[512,256]{1,0:T(8,128)(2,1)S(1)}, u32[]{:S(2)}, u32[]{:S(2)}) collective-permute-start(bf16[512,256]{1,0:T(8,128)(2,1)S(1)} %get-tuple-element.54), channel_id=1, source_target_pairs={{0,160},{2,162},{4,164},{6,166},{8,168},{10,170},{12,172},{14,174}... | collective-permute-start | bytes 786440 | tf_op jit(solution)/shard_map/ppermute | solution.py:534
  141.9 15.3 %collective-permute-start.10 = (bf16[512,256]{1,0:T(8,128)(2,1)S(1)}, bf16[512,256]{1,0:T(8,128)(2,1)S(1)}, u32[]{:S(2)}, u32[]{:S(2)}) collective-permute-start(bf16[512,256]{1,0:T(8,128)(2,1)S(1)} %get-tuple-element.55), channel_id=1, source_target_pairs={{0,96},{2,98},{4,100},{6,102},{8,104},{10,106},{12,108},{14,110},{... | collective-permute-start | bytes 786440 | tf_op jit(solution)/shard_map/ppermute | solution.py:534
  158.3 15.6 %collective-permute-start.11 = (bf16[512,256]{1,0:T(8,128)(2,1)S(1)}, bf16[512,256]{1,0:T(8,128)(2,1)S(1)}, u32[]{:S(2)}, u32[]{:S(2)}) collective-permute-start(bf16[512,256]{1,0:T(8,128)(2,1)S(1)} %get-tuple-element.56), channel_id=1, source_target_pairs={{0,192},{2,194},{4,196},{6,198},{8,200},{10,202},{12,204},{14,206}... | collective-permute-start | bytes 786440 | tf_op jit(solution)/shard_map/ppermute | solution.py:534
  160.3 13.7 %collective-permute-start.12 = (bf16[512,256]{1,0:T(8,128)(2,1)S(1)}, bf16[512,256]{1,0:T(8,128)(2,1)S(1)}, u32[]{:S(2)}, u32[]{:S(2)}) collective-permute-start(bf16[512,256]{1,0:T(8,128)(2,1)S(1)} %get-tuple-element.57), channel_id=1, source_target_pairs={{0,64},{2,66},{4,68},{6,70},{8,72},{10,74},{12,76},{14,78},{16,80}... | collective-permute-start | bytes 786440 | tf_op jit(solution)/shard_map/ppermute | solution.py:534
  160.8 17.0 %all-to-all-start.2 = ((bf16[16,48,512]{2,1,0:T(8,128)(2,1)}), bf16[16,48,512]{2,1,0:T(8,128)(2,1)S(1)}, u32[]{:S(2)}, u32[]{:S(2)}) async-start(bf16[16,48,512]{2,1,0:T(8,128)(2,1)} %shard_map.90.refs_5_), calls=%async_computation.2 | async-start | bytes 1572864 | tf_op jit(solution)/shard_map/all_to_all | solution.py:417
  167.4 17.6 %collective-permute-start.14 = (bf16[512,256]{1,0:T(8,128)(2,1)S(1)}, bf16[512,256]{1,0:T(8,128)(2,1)S(1)}, u32[]{:S(2)}, u32[]{:S(2)}) collective-permute-start(bf16[512,256]{1,0:T(8,128)(2,1)S(1)} %get-tuple-element.60), channel_id=1, source_target_pairs={{0,128},{2,130},{4,132},{6,134},{8,136},{10,138},{12,140},{14,142}... | collective-permute-start | bytes 786440 | tf_op jit(solution)/shard_map/ppermute | solution.py:534
  170.8 23.0 %collective-permute-start.15 = (bf16[512,256]{1,0:T(8,128)(2,1)S(1)}, bf16[512,256]{1,0:T(8,128)(2,1)S(1)}, u32[]{:S(2)}, u32[]{:S(2)}) collective-permute-start(bf16[512,256]{1,0:T(8,128)(2,1)S(1)} %get-tuple-element.61), channel_id=1, source_target_pairs={{0,32},{2,34},{4,36},{6,38},{8,40},{10,42},{12,44},{14,46},{16,48}... | collective-permute-start | bytes 786440 | tf_op jit(solution)/shard_map/ppermute | solution.py:534
  178.5 15.3 %collective-permute-start.13 = (bf16[512,256]{1,0:T(8,128)(2,1)S(1)}, bf16[512,256]{1,0:T(8,128)(2,1)S(1)}, u32[]{:S(2)}, u32[]{:S(2)}) collective-permute-start(bf16[512,256]{1,0:T(8,128)(2,1)S(1)} %get-tuple-element.59), channel_id=1, source_target_pairs={{0,224},{2,226},{4,228},{6,230},{8,232},{10,234},{12,236},{14,238}... | collective-permute-start | bytes 786440 | tf_op jit(solution)/shard_map/ppermute | solution.py:534

commit v4 on v3

--- a/solution.py
+++ b/solution.py
@@ -104,20 +104,10 @@
 TN = ((0,), (0,))
 
 
-def prep_kernel(place_ref, ids_ref, *refs):
-    arrays, blocks, sems = refs[:4], refs[4 : 4 + ZN], refs[4 + ZN]
-    z = place_ref[0]
-    copies = []
-    for d in range(ZN):
-        cols = pl.ds(pl.multiple_of(((z + d) & (ZN - 1)) * PAIR, PAIR), PAIR)
-        for t in range(4):
-            copies.append(
-                pltpu.make_async_copy(
-                    arrays[t].at[:, cols],
-                    blocks[d].at[t * TOK : (t + 1) * TOK, :],
-                    sems.at[d * 4 + t],
-                )
-            )
+def prep_kernel(ids_ref, *refs):
+    arrays, blocks, stages, sems = refs[:4], refs[4 : 4 + ZN], refs[4 + ZN : 8 + ZN], refs[8 + ZN]
+    z = lax.axis_index("seq") // PLANE
+    copies = [pltpu.make_async_copy(arrays[t], stages[t], sems.at[t]) for t in range(4)]
     for copy in copies:
         copy.start()
     for d in range(ZN):
@@ -126,8 +116,11 @@
         tile = jnp.concatenate(rows + [jnp.zeros((TILE - HPZ, TOK), I32)], axis=0)
         blocks[d][4 * TOK :, 0:TOK] = tile.astype(F32).astype(BF)
         blocks[d][4 * TOK :, TOK:] = jnp.zeros((TILE, PAIR - TOK), BF)
-    for copy in copies:
-        copy.wait()
+    for t in range(4):
+        copies[t].wait()
+        for d in range(ZN):
+            cols = pl.ds(pl.multiple_of(((z + d) & (ZN - 1)) * PAIR, PAIR), PAIR)
+            blocks[d][t * TOK : (t + 1) * TOK, :] = stages[t][:, cols]
 
 
 def leave(stage_ref, out_ref, sems, i, n):
@@ -163,7 +156,7 @@
                 x_ref[i * TOK : (i + 1) * TOK, t * WIDTH : (t + 1) * WIDTH] = blocks[i][
                     t * TOK : (t + 1) * TOK, hh * WIDTH : (hh + 1) * WIDTH
                 ]
-        found = [[] for _ in range(RANGES)]
+        pairs = []
         for p in range(0, n, 2):
             mine = [hh * n + p, hh * n + p + 1]
             position = jnp.concatenate(
@@ -171,23 +164,26 @@
             )
             owner = jnp.concatenate([group[i : i + 1] for i in mine], axis=1)
             value = jnp.concatenate([local[i : i + 1] for i in mine], axis=1)
-            value = jnp.broadcast_to(value, (TILE, 2 * TOK))
-            x = x_ref[p * TOK : (p + 2) * TOK, :]
-            for b in range(RANGES):
+            pairs.append((position, owner, jnp.broadcast_to(value, (TILE, 2 * TOK))))
+        for b in range(RANGES):
+            to = hh * RANGES + b
+            found = []
+            for p, (position, owner, value) in enumerate(pairs):
                 target = jnp.where(owner == b, position, -1)
                 pick = one_hot(target == iota((2 * MOST, 2 * TOK), 0))
-                send_ref[hh * RANGES + b, p * MOST : (p + 2) * MOST, :] = dot(pick, x).astype(BF)
-                found[b].append(dot(value, pick, NT).astype(BF))
-        for b in range(RANGES):
-            note = jnp.concatenate(found[b] + [zeros[:, n * MOST :]], axis=1)
-            note_ref[hh * RANGES + b] = note
+                x = x_ref[p * 2 * TOK : (p + 1) * 2 * TOK, :]
+                send_ref[to, p * 2 * MOST : (p + 1) * 2 * MOST, :] = dot(pick, x).astype(BF)
+                found.append(dot(value, pick, NT).astype(BF))
+            note = jnp.concatenate(found + [zeros[:, n * MOST :]], axis=1)
+            note_ref[to] = note
             if last:
-                tile = [a[hh * RANGES + b] for a in notes] + [note]
+                tile = [a[to] for a in notes] + [note]
                 tile = tile + [zeros] * (4 - len(tile))
-                send_ref[hh * RANGES + b, rows:, :] = jnp.concatenate(tile, axis=1)
-        leave(send_ref, out_ref, sems, hh, HPZ).start()
-    for hh in range(HPZ):
-        leave(send_ref, out_ref, sems, hh, HPZ).wait()
+                send_ref[to, rows:, :] = jnp.concatenate(tile, axis=1)
+            if b % 2:
+                leave(send_ref, out_ref, sems, to // 2, RANGES).start()
+    for i in range(RANGES):
+        leave(send_ref, out_ref, sems, i, RANGES).wait()
 
 
 def rank_rows(z, clusters):
@@ -225,36 +221,43 @@
     )
     rank = jnp.sum((hot * rank).reshape(CLUSTER_GROUP, PLANE, lanes), axis=0)
     rank = jnp.where(clusters > 0.5, rank, float(NONE))
-    return jnp.concatenate([rank[s : s + 1, :] for s in range(PLANE)], axis=1)
+    return rank
 
 
 def place_kernel(place_ref, *refs):
     n = len(CHUNKS)
-    recvs, (sorted_ref, tail_ref, head_ref, rank_ref, x_ref) = refs[:n], refs[n:]
+    recvs, (sorted_ref, tail_ref, head_ref, rank_ref) = refs[:n], refs[n:]
     clusters = []
-    at = 0
-    for i, (chunk, recv_ref) in enumerate(zip(CHUNKS, recvs)):
+    end = len(CHUNKS[-1]) * MOST
+    for i, chunk in enumerate(CHUNKS):
         rows = len(chunk) * MOST
-        tail = len(CHUNKS[-1]) * MOST
         clusters.append(
             jnp.concatenate(
                 [
-                    recvs[-1][s, tail:, i * WIDTH : i * WIDTH + rows].astype(F32)[0:1]
+                    recvs[-1][s, end:, i * WIDTH : i * WIDTH + rows].astype(F32)[0:1]
                     for s in range(PLANE)
                 ],
                 axis=0,
             )
         )
-        for s in range(PLANE):
-            x_ref[s * ZN * MOST + at : s * ZN * MOST + at + rows, :] = recv_ref[s, 0:rows, :]
+    rank = rank_rows(place_ref[0], jnp.concatenate(clusters, axis=1))
+    rank_ref[...] = jnp.concatenate(
+        [rank[s : s + 1, :] for s in range(PLANE)], axis=1
+    ).astype(I32)
+    parts = []
+    at = 0
+    for chunk, recv_ref in zip(CHUNKS, recvs):
+        rows = len(chunk) * MOST
+        row = jnp.concatenate([rank[s : s + 1, at : at + rows] for s in range(PLANE)], axis=1)
+        parts.append((row.astype(I32), recv_ref[:, 0:rows, :].reshape(PLANE * rows, ALL)))
         at += rows
-    rank = rank_rows(place_ref[0], jnp.concatenate(clusters, axis=1)).astype(I32)
-    rank_ref[...] = rank
-    x = x_ref[...]
     step = 2
     for c in range(0, SPANS, step):
-        pick = one_hot(rank == iota((step * SPAN, SLOTS), 0) + c * SPAN)
-        sorted_ref[c : c + step] = dot(pick, x).astype(BF).reshape(step, SPAN, ALL)
+        got = jnp.zeros((step * SPAN, ALL), F32)
+        for row, x in parts:
+            pick = one_hot(row == iota((step * SPAN, row.shape[1]), 0) + c * SPAN)
+            got = got + dot(pick, x)
+        sorted_ref[c : c + step] = got.astype(BF).reshape(step, SPAN, ALL)
     tail_ref[...] = sorted_ref[SPANS - 1, :, WIDTH : 3 * WIDTH]
     head_ref[...] = sorted_ref[0]
 
@@ -290,27 +293,24 @@
 Q, K, V, G = (slice(t * WIDTH, (t + 1) * WIDTH) for t in range(4))
 
 
-def main_kernel(in_ref, o_ref, part_ref, d_ref):
-    d_ref[0] = jnp.zeros((SPAN, PAIR), F32)
-
-    def one(c, carry):
+def main_kernel(in_ref, o_ref, part_ref):
+    held = (jnp.zeros((SPAN, WIDTH), F32),) * 2
+    for c in range(1, SPANS):
         att, dq, dk0, dk1, dv0, dv1 = span_math(
             in_ref[c, :, Q], in_ref[c, :, G], in_ref[c - 1, :, K], in_ref[c, :, K],
             in_ref[c - 1, :, V], in_ref[c, :, V], None,
         )
         o_ref[c, :, Q] = att
         o_ref[c, :, K] = dq
-        d_ref[c - 1, :, Q] += dk0
-        d_ref[c - 1, :, K] += dv0
-        d_ref[c, :, Q] = dk1
-        d_ref[c, :, K] = dv1
-        o_ref[c - 1, :, 2 * WIDTH :] = d_ref[c - 1].astype(BF)
-        return carry
-
-    for c in range(1, SPANS):
-        one(c, 0)
-    part_ref[0] = d_ref[0]
-    part_ref[1] = d_ref[SPANS - 1]
+        dk, dv = held[0] + dk0, held[1] + dv0
+        if c == 1:
+            part_ref[0, :, Q] = dk
+            part_ref[0, :, K] = dv
+        o_ref[c - 1, :, V] = dk.astype(BF)
+        o_ref[c - 1, :, G] = dv.astype(BF)
+        held = (dk1, dv1)
+    part_ref[1, :, Q] = held[0]
+    part_ref[1, :, K] = held[1]
     o_ref[0, :, 0 : 2 * WIDTH] = jnp.zeros((SPAN, 2 * WIDTH), BF)
     o_ref[SPANS - 1, :, 2 * WIDTH :] = jnp.zeros((SPAN, 2 * WIDTH), BF)
 
@@ -433,10 +433,10 @@
     anywhere = pl.BlockSpec(memory_space=pl.ANY)
     blocks = call(
         prep_kernel,
-        [place, cluster_ids.T, queries, keys, values, out_grad],
+        [cluster_ids.T, queries, keys, values, out_grad],
         [out((4 * TOK + TILE, PAIR), BF)] * ZN,
-        [pltpu.SemaphoreType.DMA((4 * ZN,))],
-        specs={0: SMEM[0], 2: hbm, 3: hbm, 4: hbm, 5: hbm},
+        [pltpu.VMEM((TOK, ZN * PAIR), BF)] * 4 + [pltpu.SemaphoreType.DMA((4,))],
+        specs={1: hbm, 2: hbm, 3: hbm, 4: hbm},
         limit=60,
     )
     moved = {0: blocks[0]}
@@ -459,7 +459,7 @@
             [
                 pltpu.VMEM((n * TOK, ALL), BF),
                 pltpu.VMEM((PLANE, rows + extra, ALL), BF),
-                pltpu.SemaphoreType.DMA((HPZ,)),
+                pltpu.SemaphoreType.DMA((RANGES,)),
             ],
             flops=PACK_HINT[i],
             out_specs={0: hbm},
@@ -476,7 +476,6 @@
             out((SPAN, ALL), BF),
             out((1, SLOTS), I32),
         ],
-        [pltpu.VMEM((SLOTS, ALL), BF)],
         flops=2 * BLOCK * SLOTS * ALL,
         specs=SMEM,
     )
@@ -486,7 +485,6 @@
         main_kernel,
         [rows_in],
         [out((SPANS, SPAN, ALL), BF), out((2, SPAN, PAIR), F32)],
-        [pltpu.VMEM((SPANS, SPAN, PAIR), F32)],
         flops=14 * SPANS * SPAN * 2 * SPAN * WIDTH,
     )
     sends = []

time: 197 us -> 196 us (level)
  blocking collectives: 29.7 us -> 0 us
  waiting for transfers between devices: 58.1 us -> 79.1 us
  starting transfers between devices: 62 us -> 71.2 us
    all_to_all x1 -> x0, blocking collectives: 29.7 us -> none  [exchange(): lax.all_to_all(array, 'seq', split_axis=0, concat_axis=0, axis_index_grou...]
    all_to_all x4 -> x5, waiting for transfers between devices: 7.72 us -> 30.3 us  [exchange(): lax.all_to_all(array, 'seq', split_axis=0, concat_axis=0, axis_index_grou...]
    all_to_all x4 -> x5, starting transfers between devices: 22.6 us -> 29.8 us  [exchange(): lax.all_to_all(array, 'seq', split_axis=0, concat_axis=0, axis_index_grou...]
    ppermute x7, starting transfers between devices: 17.8 us -> 19.8 us  [body(): back[d] = lax.ppermute(piece, 'seq', z_pairs(-d)) if d else piece]
  transfers between devices with their start and end apart: 20 -> 21, of which waited for: 10 -> 10; matrix products, arithmetic and copies ran while one was open for 0% -> 0% of each run, Pallas kernels for 11% -> 11%
where the time goes in v4:
time: 196 us; the launch traced here: 195 us
  waiting for transfers between devices  79.1 us (40%)
  starting transfers between devices  71.2 us (36%)
  Pallas kernels  41.3 us (21%)
  local copies, waits for them, and re-layouts  2.54 us (1%)
    pallas_call x13, Pallas kernels, call(): pl.pallas_call(kernel, out_shape=tuple((pltpu.HBM(o.shape, o.dtype) if i...  41.3 us
    all_to_all x5, waiting for transfers between devices, exchange(): lax.all_to_all(array, 'seq', split_axis=0, concat_axis=0, axis_index_grou...  30.3 us
    all_to_all x5, starting transfers between devices, exchange(): lax.all_to_all(array, 'seq', split_axis=0, concat_axis=0, axis_index_grou...  29.8 us
    ppermute x7, waiting for transfers between devices, body(): moved[d] = lax.ppermute(blocks[d], 'seq', z_pairs(d))  26 us
    ppermute x7, waiting for transfers between devices, body(): back[d] = lax.ppermute(piece, 'seq', z_pairs(-d)) if d else piece  22.8 us
    ppermute x7, starting transfers between devices, body(): back[d] = lax.ppermute(piece, 'seq', z_pairs(-d)) if d else piece  19.8 us
    ppermute x7, starting transfers between devices, body(): moved[d] = lax.ppermute(blocks[d], 'seq', z_pairs(d))  16.1 us
    ppermute x2, starting transfers between devices, shift_owner(): return lax.ppermute(value, 'seq', pairs)  5.51 us
  transfers between devices with their start and end apart: 21, of which 10 were waited for; matrix products, arithmetic and copies ran while one was open for 0% of the time, Pallas kernels for 11%

profile of v4, /device:TPU:1, one launch (start us, length us, event | category | flops | bytes accessed | tf_op | source)
XLA Modules:
  0.0 195.3 jit_solution(7628472107378333477)
XLA Ops:
  0.6 3.6 %shard_map.84 = (bf16[528,256]{1,0:T(8,128)(2,1)}, bf16[528,256]{1,0:T(8,128)(2,1)}, bf16[528,256]{1,0:T(8,128)(2,1)}, bf16[528,256]{1,0:T(8,128)(2,1)}, bf16[52...) custom-call(s32[16,128]{1,0:T(8,128)} %bitcast.3, ...), custom_call_target="tpu_custom_call" | custom-call | bytes 4268032 | tf_op jit(solution)/shard_map/pallas_call | solution.py:60
  4.3 2.5 %collective-permute-start = (bf16[528,256]{1,0:T(8,128)(2,1)}, bf16[528,256]{1,0:T(8,128)(2,1)S(1)}, u32[]{:S(2)}, u32[]{:S(2)}) collective-permute-start(bf16[528,256]{1,0:T(8,128)(2,1)} %get-tuple-element.34), channel_id=1, source_target_pairs={{0,32},{2,34},{4,36},{6,38},{8,40},{10,42},{12,44},{14,46},{16,48}... | collective-permute-start | bytes 811016 | tf_op jit(solution)/shard_map/ppermute | solution.py:445
  6.8 4.0 %collective-permute-start.1 = (bf16[528,256]{1,0:T(8,128)(2,1)}, bf16[528,256]{1,0:T(8,128)(2,1)S(1)}, u32[]{:S(2)}, u32[]{:S(2)}) collective-permute-start(bf16[528,256]{1,0:T(8,128)(2,1)} %get-tuple-element.35), channel_id=1, source_target_pairs={{0,224},{2,226},{4,228},{6,230},{8,232},{10,234},{12,236},{14,238}... | collective-permute-start | bytes 811016 | tf_op jit(solution)/shard_map/ppermute | solution.py:445
  10.9 3.6 %collective-permute-start.3 = (bf16[528,256]{1,0:T(8,128)(2,1)}, bf16[528,256]{1,0:T(8,128)(2,1)S(1)}, u32[]{:S(2)}, u32[]{:S(2)}) collective-permute-start(bf16[528,256]{1,0:T(8,128)(2,1)} %get-tuple-element.38), channel_id=1, source_target_pairs={{0,192},{2,194},{4,196},{6,198},{8,200},{10,202},{12,204},{14,206}... | collective-permute-start | bytes 811016 | tf_op jit(solution)/shard_map/ppermute | solution.py:445
  14.4 0.3 collective-permute-start.4
  14.7 2.4 %collective-permute-done.refs_1_ = bf16[528,256]{1,0:T(8,128)(2,1)S(1)} collective-permute-done((bf16[528,256]{1,0:T(8,128)(2,1)}, bf16[528,256]{1,0:T(8,128)(2,1)S(1)}, u32[]{:S(2)}, u32[]{:S(2)}) %collective-permute-start) | collective-permute-done | bytes 270368 | tf_op jit(solution)/shard_map/ppermute | solution.py:445
  17.2 2.0 %collective-permute-start.5 = (bf16[528,256]{1,0:T(8,128)(2,1)}, bf16[528,256]{1,0:T(8,128)(2,1)S(1)}, u32[]{:S(2)}, u32[]{:S(2)}) collective-permute-start(bf16[528,256]{1,0:T(8,128)(2,1)} %get-tuple-element.40), channel_id=1, source_target_pairs={{0,160},{2,162},{4,164},{6,166},{8,168},{10,170},{12,172},{14,174}... | collective-permute-start | bytes 811016 | tf_op jit(solution)/shard_map/ppermute | solution.py:445
  19.2 0.0 collective-permute-done.1.refs_2_
  19.2 3.6 %collective-permute-start.6 = (bf16[528,256]{1,0:T(8,128)(2,1)}, bf16[528,256]{1,0:T(8,128)(2,1)S(1)}, u32[]{:S(2)}, u32[]{:S(2)}) collective-permute-start(bf16[528,256]{1,0:T(8,128)(2,1)} %get-tuple-element.41), channel_id=1, source_target_pairs={{0,128},{2,130},{4,132},{6,134},{8,136},{10,138},{12,140},{14,142}... | collective-permute-start | bytes 811016 | tf_op jit(solution)/shard_map/ppermute | solution.py:445
  22.8 1.9 collective-permute-done.2.refs_3_
  24.8 1.0 copy-done
  25.7 2.7 %shard_map.85 = (bf16[16,96,512]{2,1,0:T(8,128)(2,1)}, s32[8,128]{1,0:T(8,128)S(1)}, bf16[16,16,128]{2,1,0:T(8,128)(2,1)S(1)}) custom-call(bf16[528,256]{1,0:T(8,128)(2,1)S(1)} %copy-done, bf16[528,256]{1,0:T(8,128)(2,1)S(1)} %collective-permute-done.refs_1_, bf16[528,256]{1,0:T(8,128)(2,1)S(1)} %collective-permute-done.1.refs_2_, ...), custom_call_target="tpu_custom_call" | custom-call | flops 1000000 | bytes 2723840 | tf_op jit(solution)/shard_map/pallas_call | solution.py:60
  28.5 6.8 %all-to-all-start = ((bf16[16,96,512]{2,1,0:T(8,128)(2,1)}), bf16[16,96,512]{2,1,0:T(8,128)(2,1)S(1)}, u32[]{:S(2)}, u32[]{:S(2)}) async-start(bf16[16,96,512]{2,1,0:T(8,128)(2,1)} %get-tuple-element.44), calls=%async_computation | async-start | bytes 3145728 | tf_op jit(solution)/shard_map/all_to_all | solution.py:417
  35.2 0.0 collective-permute-done.3.refs_0_
  35.2 11.1 %collective-permute-done.4.refs_1_ = bf16[528,256]{1,0:T(8,128)(2,1)S(1)} collective-permute-done((bf16[528,256]{1,0:T(8,128)(2,1)}, bf16[528,256]{1,0:T(8,128)(2,1)S(1)}, u32[]{:S(2)}, u32[]{:S(2)}) %collective-permute-start.4) | collective-permute-done | bytes 270368 | tf_op jit(solution)/shard_map/ppermute | solution.py:445
  46.3 10.5 %collective-permute-done.5.refs_2_ = bf16[528,256]{1,0:T(8,128)(2,1)S(1)} collective-permute-done((bf16[528,256]{1,0:T(8,128)(2,1)}, bf16[528,256]{1,0:T(8,128)(2,1)S(1)}, u32[]{:S(2)}, u32[]{:S(2)}) %collective-permute-start.5) | collective-permute-done | bytes 270368 | tf_op jit(solution)/shard_map/ppermute | solution.py:445
  56.9 3.4 %shard_map.86 = (bf16[16,112,512]{2,1,0:T(8,128)(2,1)}, s32[8,128]{1,0:T(8,128)S(1)}, bf16[16,16,128]{2,1,0:T(8,128)(2,1)}) custom-call(bf16[528,256]{1,0:T(8,128)(2,1)S(1)} %collective-permute-done.3.refs_0_, bf16[528,256]{1,0:T(8,128)(2,1)S(1)} %collective-permute-done.4.refs_1_, bf16[528,256]{1,0:T(8,128)(2,1)S(1)} %collective-permute-done.5.refs_2_, ...), custom_call_target="tpu_custom_call" | custom-call | flops 99999997952 | bytes 3051520 | tf_op jit(solution)/shard_map/pallas_call | solution.py:60
  60.3 6.8 %all-to-all-start.1 = ((bf16[16,112,512]{2,1,0:T(8,128)(2,1)}), bf16[16,112,512]{2,1,0:T(8,128)(2,1)S(1)}, u32[]{:S(2)}, u32[]{:S(2)}) async-start(bf16[16,112,512]{2,1,0:T(8,128)(2,1)} %get-tuple-element.45), calls=%async_computation.1 | async-start | bytes 3670016 | tf_op jit(solution)/shard_map/all_to_all | solution.py:417
  67.1 0.1 pad_add_fusion.place_ref
  67.2 22.9 %all-to-all-done.1.refs_1_ = bf16[16,112,512]{2,1,0:T(8,128)(2,1)S(1)} async-done(((bf16[16,112,512]{2,1,0:T(8,128)(2,1)}), bf16[16,112,512]{2,1,0:T(8,128)(2,1)S(1)}, u32[]{:S(2)}, u32[]{:S(2)}) %all-to-all-start.1) | async-done | bytes 1835040 | tf_op jit(solution)/shard_map/all_to_all | solution.py:417
  90.1 8.1 %shard_map.87 = (bf16[8,256,512]{2,1,0:T(8,128)(2,1)S(1)}, bf16[256,256]{1,0:T(8,128)(2,1)S(1)}, bf16[256,512]{1,0:T(8,128)(2,1)S(1)}, s32[1,3072]{1,0:T(1,128)S(1)}) custom-call(s32[2]{0:T(128)S(1)} %pad_add_fusion.place_ref, bf16[16,96,512]{2,1,0:T(8,128)(2,1)S(1)} %all-to-all-done.refs_0_, bf16[16,112,512]{2,1,0:T(8,128)(2,1)S(1)} %all-to-all-done.1.refs_1_), custom_call_target="tpu_custom_call" | custom-call | flops 6442450944 | bytes 5910536 | tf_op jit(solution)/shard_map/pallas_call | solution.py:60
  98.2 1.3 collective-permute-start.8
  99.5 4.2 %collective-permute-start.7 = (bf16[256,256]{1,0:T(8,128)(2,1)S(1)}, bf16[256,256]{1,0:T(8,128)(2,1)S(1)}, u32[]{:S(2)}, u32[]{:S(2)}) collective-permute-start(bf16[256,256]{1,0:T(8,128)(2,1)S(1)} %get-tuple-element.48), channel_id=1, source_target_pairs={{0,2},{2,4},{4,6},{6,8},{8,10},{10,12},{12,14},{16,18},{18,20},{20... | collective-permute-start | bytes 393224 | tf_op jit(solution)/shard_map/ppermute | solution.py:426
  103.7 6.4 %shard_map.88 = (bf16[8,256,512]{2,1,0:T(8,128)(2,1)S(1)}, f32[2,256,256]{2,1,0:T(8,128)S(1)}) custom-call(bf16[8,256,512]{2,1,0:T(8,128)(2,1)S(1)} %get-tuple-element.47.in_ref), custom_call_target="tpu_custom_call" | custom-call | flops 1879048192 | bytes 4718592 | tf_op jit(solution)/shard_map/pallas_call | solution.py:60
  110.1 0.0 collective-permute-done.8.head_ref
  110.1 4.4 %shard_map.89 = (bf16[2048,512]{1,0:T(8,128)(2,1)}, bf16[16,48,512]{2,1,0:T(8,128)(2,1)}) custom-call(s32[2]{0:T(128)S(1)} %pad_add_fusion.place_ref, s32[1,3072]{1,0:T(1,128)S(1)} %get-tuple-element.46.rank_ref, bf16[8,256,512]{2,1,0:T(8,128)(2,1)S(1)} %get-tuple-element.47.in_ref, bf16[256,256]{1,0:T(8,128)(2,1)S(1)} %collective-permute-done.7.tail_ref, ...), custom_call_target="tpu_custom_call" | custom-call | flops 1610612736 | bytes 8007688 | tf_op jit(solution)/shard_map/pallas_call | solution.py:60
  114.5 6.0 %all-to-all-start.4 = ((bf16[16,48,512]{2,1,0:T(8,128)(2,1)}), bf16[16,48,512]{2,1,0:T(8,128)(2,1)S(1)}, u32[]{:S(2)}, u32[]{:S(2)}) async-start(bf16[16,48,512]{2,1,0:T(8,128)(2,1)} %get-tuple-element.53), calls=%async_computation.4 | async-start | bytes 1572864 | tf_op jit(solution)/shard_map/all_to_all | solution.py:417
  120.5 1.6 copy-done.1
  122.1 4.6 %shard_map.91 = bf16[16,96,512]{2,1,0:T(8,128)(2,1)} custom-call(s32[1,3072]{1,0:T(1,128)S(1)} %get-tuple-element.46.rank_ref, bf16[2048,512]{1,0:T(8,128)(2,1)S(1)} %copy-done.1), custom_call_target="tpu_custom_call" | custom-call | flops 1000000000 | bytes 3682304 | tf_op jit(solution)/shard_map/pallas_call | solution.py:60
  126.8 4.2 %all-to-all-done.4.refs_2_ = bf16[16,48,512]{2,1,0:T(8,128)(2,1)S(1)} async-done(((bf16[16,48,512]{2,1,0:T(8,128)(2,1)}), bf16[16,48,512]{2,1,0:T(8,128)(2,1)S(1)}, u32[]{:S(2)}, u32[]{:S(2)}) %all-to-all-start.4) | async-done | bytes 786464 | tf_op jit(solution)/shard_map/all_to_all | solution.py:417
  131.0 3.7 %all-to-all-start.3 = ((bf16[16,96,512]{2,1,0:T(8,128)(2,1)}), bf16[16,96,512]{2,1,0:T(8,128)(2,1)S(1)}, u32[]{:S(2)}, u32[]{:S(2)}) async-start(bf16[16,96,512]{2,1,0:T(8,128)(2,1)} %shard_map.91), calls=%async_computation.3 | async-start | bytes 3145728 | tf_op jit(solution)/shard_map/all_to_all | solution.py:417
  134.7 0.7 shard_map.92
  135.4 5.4 %collective-permute-start.9 = (bf16[512,256]{1,0:T(8,128)(2,1)S(1)}, bf16[512,256]{1,0:T(8,128)(2,1)S(1)}, u32[]{:S(2)}, u32[]{:S(2)}) collective-permute-start(bf16[512,256]{1,0:T(8,128)(2,1)S(1)} %get-tuple-element.54), channel_id=1, source_target_pairs={{0,160},{2,162},{4,164},{6,166},{8,168},{10,170},{12,172},{14,174}... | collective-permute-start | bytes 786440 | tf_op jit(solution)/shard_map/ppermute | solution.py:532
  140.8 2.8 %shard_map.90.refs_5_ = bf16[16,48,512]{2,1,0:T(8,128)(2,1)} custom-call(s32[1,3072]{1,0:T(1,128)S(1)} %get-tuple-element.46.rank_ref, bf16[2048,512]{1,0:T(8,128)(2,1)S(1)} %copy-done.2), custom_call_target="tpu_custom_call" | custom-call | flops 1000000000 | bytes 2895872 | tf_op jit(solution)/shard_map/pallas_call | solution.py:60
  143.6 13.3 %collective-permute-done.9.refs_3_ = bf16[512,256]{1,0:T(8,128)(2,1)S(1)} collective-permute-done((bf16[512,256]{1,0:T(8,128)(2,1)S(1)}, bf16[512,256]{1,0:T(8,128)(2,1)S(1)}, u32[]{:S(2)}, u32[]{:S(2)}) %collective-permute-start.9) | collective-permute-done | bytes 262176 | tf_op jit(solution)/shard_map/ppermute | solution.py:532
  157.0 1.2 shard_map.93
  158.1 1.3 collective-permute-start.11
  159.5 1.1 collective-permute-start.12
  160.6 6.6 %all-to-all-start.2 = ((bf16[16,48,512]{2,1,0:T(8,128)(2,1)}), bf16[16,48,512]{2,1,0:T(8,128)(2,1)S(1)}, u32[]{:S(2)}, u32[]{:S(2)}) async-start(bf16[16,48,512]{2,1,0:T(8,128)(2,1)} %shard_map.90.refs_5_), calls=%async_computation.2 | async-start | bytes 1572864 | tf_op jit(solution)/shard_map/all_to_all | solution.py:417
  167.2 3.0 %collective-permute-start.14 = (bf16[512,256]{1,0:T(8,128)(2,1)S(1)}, bf16[512,256]{1,0:T(8,128)(2,1)S(1)}, u32[]{:S(2)}, u32[]{:S(2)}) collective-permute-start(bf16[512,256]{1,0:T(8,128)(2,1)S(1)} %get-tuple-element.60), channel_id=1, source_target_pairs={{0,128},{2,130},{4,132},{6,134},{8,136},{10,138},{12,140},{14,142}... | collective-permute-start | bytes 786440 | tf_op jit(solution)/shard_map/ppermute | solution.py:532
  170.1 3.6 %collective-permute-start.15 = (bf16[512,256]{1,0:T(8,128)(2,1)S(1)}, bf16[512,256]{1,0:T(8,128)(2,1)S(1)}, u32[]{:S(2)}, u32[]{:S(2)}) collective-permute-start(bf16[512,256]{1,0:T(8,128)(2,1)S(1)} %get-tuple-element.61), channel_id=1, source_target_pairs={{0,32},{2,34},{4,36},{6,38},{8,40},{10,42},{12,44},{14,46},{16,48}... | collective-permute-start | bytes 786440 | tf_op jit(solution)/shard_map/ppermute | solution.py:532
  173.8 0.5 shard_map.94.refs_3_
  174.3 3.2 %all-to-all-done.2.refs_2_ = bf16[16,48,512]{2,1,0:T(8,128)(2,1)S(1)} async-done(((bf16[16,48,512]{2,1,0:T(8,128)(2,1)}), bf16[16,48,512]{2,1,0:T(8,128)(2,1)S(1)}, u32[]{:S(2)}, u32[]{:S(2)}) %all-to-all-start.2) | async-done | bytes 786464 | tf_op jit(solution)/shard_map/all_to_all | solution.py:417
  177.5 0.7 shard_map.95
  178.2 5.3 %collective-permute-start.13 = (bf16[512,256]{1,0:T(8,128)(2,1)S(1)}, bf16[512,256]{1,0:T(8,128)(2,1)S(1)}, u32[]{:S(2)}, u32[]{:S(2)}) collective-permute-start(bf16[512,256]{1,0:T(8,128)(2,1)S(1)} %get-tuple-element.59), channel_id=1, source_target_pairs={{0,224},{2,226},{4,228},{6,230},{8,232},{10,234},{12,236},{14,238}... | collective-permute-start | bytes 786440 | tf_op jit(solution)/shard_map/ppermute | solution.py:532
  183.5 0.9 collective-permute-done.14.refs_4_
  184.5 8.5 %collective-permute-done.15.refs_7_ = bf16[512,256]{1,0:T(8,128)(2,1)S(1)} collective-permute-done((bf16[512,256]{1,0:T(8,128)(2,1)S(1)}, bf16[512,256]{1,0:T(8,128)(2,1)S(1)}, u32[]{:S(2)}, u32[]{:S(2)}) %collective-permute-start.15) | collective-permute-done | bytes 262176 | tf_op jit(solution)/shard_map/ppermute | solution.py:532
  193.0 2.1 %shard_map.96 = (bf16[128,2048]{1,0:T(8,128)(2,1)}, bf16[128,2048]{1,0:T(8,128)(2,1)}, bf16[128,2048]{1,0:T(8,128)(2,1)}, bf16[128,2048]{1,0:T(8,128)(2,1)}) custom-call(s32[2]{0:T(128)S(1)} %pad_add_fusion.place_ref, bf16[512,256]{1,0:T(8,128)(2,1)S(1)} %get-tuple-element.58.refs_0_, bf16[512,256]{1,0:T(8,128)(2,1)S(1)} %collective-permute-done.13.refs_1_, ...), custom_call_target="tpu_custom_call" | custom-call | bytes 4194312 | tf_op jit(solution)/shard_map/pallas_call | solution.py:60
  (14 shorter events, 0.0 us)
Async XLA Ops:
  4.3 12.9 %collective-permute-start = (bf16[528,256]{1,0:T(8,128)(2,1)}, bf16[528,256]{1,0:T(8,128)(2,1)S(1)}, u32[]{:S(2)}, u32[]{:S(2)}) collective-permute-start(bf16[528,256]{1,0:T(8,128)(2,1)} %get-tuple-element.34), channel_id=1, source_target_pairs={{0,32},{2,34},{4,36},{6,38},{8,40},{10,42},{12,44},{14,46},{16,48}... | collective-permute-start | bytes 811016 | tf_op jit(solution)/shard_map/ppermute | solution.py:445
  6.8 12.4 %collective-permute-start.1 = (bf16[528,256]{1,0:T(8,128)(2,1)}, bf16[528,256]{1,0:T(8,128)(2,1)S(1)}, u32[]{:S(2)}, u32[]{:S(2)}) collective-permute-start(bf16[528,256]{1,0:T(8,128)(2,1)} %get-tuple-element.35), channel_id=1, source_target_pairs={{0,224},{2,226},{4,228},{6,230},{8,232},{10,234},{12,236},{14,238}... | collective-permute-start | bytes 811016 | tf_op jit(solution)/shard_map/ppermute | solution.py:445
  10.9 13.9 %collective-permute-start.2 = (bf16[528,256]{1,0:T(8,128)(2,1)}, bf16[528,256]{1,0:T(8,128)(2,1)S(1)}, u32[]{:S(2)}, u32[]{:S(2)}) collective-permute-start(bf16[528,256]{1,0:T(8,128)(2,1)} %get-tuple-element.36), channel_id=1, source_target_pairs={{0,64},{2,66},{4,68},{6,70},{8,72},{10,74},{12,76},{14,78},{16,80}... | collective-permute-start | bytes 811016 | tf_op jit(solution)/shard_map/ppermute | solution.py:445
  10.9 24.4 %collective-permute-start.3 = (bf16[528,256]{1,0:T(8,128)(2,1)}, bf16[528,256]{1,0:T(8,128)(2,1)S(1)}, u32[]{:S(2)}, u32[]{:S(2)}) collective-permute-start(bf16[528,256]{1,0:T(8,128)(2,1)} %get-tuple-element.38), channel_id=1, source_target_pairs={{0,192},{2,194},{4,196},{6,198},{8,200},{10,202},{12,204},{14,206}... | collective-permute-start | bytes 811016 | tf_op jit(solution)/shard_map/ppermute | solution.py:445
  14.4 31.9 %collective-permute-start.4 = (bf16[528,256]{1,0:T(8,128)(2,1)}, bf16[528,256]{1,0:T(8,128)(2,1)S(1)}, u32[]{:S(2)}, u32[]{:S(2)}) collective-permute-start(bf16[528,256]{1,0:T(8,128)(2,1)} %get-tuple-element.39), channel_id=1, source_target_pairs={{0,96},{2,98},{4,100},{6,102},{8,104},{10,106},{12,108},{14,110},{... | collective-permute-start | bytes 811016 | tf_op jit(solution)/shard_map/ppermute | solution.py:445
  17.2 39.7 %collective-permute-start.5 = (bf16[528,256]{1,0:T(8,128)(2,1)}, bf16[528,256]{1,0:T(8,128)(2,1)S(1)}, u32[]{:S(2)}, u32[]{:S(2)}) collective-permute-start(bf16[528,256]{1,0:T(8,128)(2,1)} %get-tuple-element.40), channel_id=1, source_target_pairs={{0,160},{2,162},{4,164},{6,166},{8,168},{10,170},{12,172},{14,174}... | collective-permute-start | bytes 811016 | tf_op jit(solution)/shard_map/ppermute | solution.py:445
  19.2 37.7 %collective-permute-start.6 = (bf16[528,256]{1,0:T(8,128)(2,1)}, bf16[528,256]{1,0:T(8,128)(2,1)S(1)}, u32[]{:S(2)}, u32[]{:S(2)}) collective-permute-start(bf16[528,256]{1,0:T(8,128)(2,1)} %get-tuple-element.41), channel_id=1, source_target_pairs={{0,128},{2,130},{4,132},{6,134},{8,136},{10,138},{12,140},{14,142}... | collective-permute-start | bytes 811016 | tf_op jit(solution)/shard_map/ppermute | solution.py:445
  24.8 1.0 copy-start
  28.5 31.8 %all-to-all-start = ((bf16[16,96,512]{2,1,0:T(8,128)(2,1)}), bf16[16,96,512]{2,1,0:T(8,128)(2,1)S(1)}, u32[]{:S(2)}, u32[]{:S(2)}) async-start(bf16[16,96,512]{2,1,0:T(8,128)(2,1)} %get-tuple-element.44), calls=%async_computation | async-start | bytes 3145728 | tf_op jit(solution)/shard_map/all_to_all | solution.py:417
  60.3 29.8 %all-to-all-start.1 = ((bf16[16,112,512]{2,1,0:T(8,128)(2,1)}), bf16[16,112,512]{2,1,0:T(8,128)(2,1)S(1)}, u32[]{:S(2)}, u32[]{:S(2)}) async-start(bf16[16,112,512]{2,1,0:T(8,128)(2,1)} %get-tuple-element.45), calls=%async_computation.1 | async-start | bytes 3670016 | tf_op jit(solution)/shard_map/all_to_all | solution.py:417
  98.2 11.9 %collective-permute-start.8 = (bf16[256,512]{1,0:T(8,128)(2,1)S(1)}, bf16[256,512]{1,0:T(8,128)(2,1)S(1)}, u32[]{:S(2)}, u32[]{:S(2)}) collective-permute-start(bf16[256,512]{1,0:T(8,128)(2,1)S(1)} %get-tuple-element.49), channel_id=1, source_target_pairs={{2,0},{4,2},{6,4},{8,6},{10,8},{12,10},{14,12},{18,16},{20,18},{22... | collective-permute-start | bytes 786440 | tf_op jit(solution)/shard_map/ppermute | solution.py:426
  99.5 10.6 %collective-permute-start.7 = (bf16[256,256]{1,0:T(8,128)(2,1)S(1)}, bf16[256,256]{1,0:T(8,128)(2,1)S(1)}, u32[]{:S(2)}, u32[]{:S(2)}) collective-permute-start(bf16[256,256]{1,0:T(8,128)(2,1)S(1)} %get-tuple-element.48), channel_id=1, source_target_pairs={{0,2},{2,4},{4,6},{6,8},{8,10},{10,12},{12,14},{16,18},{18,20},{20... | collective-permute-start | bytes 393224 | tf_op jit(solution)/shard_map/ppermute | solution.py:426
  114.5 16.4 %all-to-all-start.4 = ((bf16[16,48,512]{2,1,0:T(8,128)(2,1)}), bf16[16,48,512]{2,1,0:T(8,128)(2,1)S(1)}, u32[]{:S(2)}, u32[]{:S(2)}) async-start(bf16[16,48,512]{2,1,0:T(8,128)(2,1)} %get-tuple-element.53), calls=%async_computation.4 | async-start | bytes 1572864 | tf_op jit(solution)/shard_map/all_to_all | solution.py:417
  120.5 1.6 copy-start.1
  131.0 26.0 %all-to-all-start.3 = ((bf16[16,96,512]{2,1,0:T(8,128)(2,1)}), bf16[16,96,512]{2,1,0:T(8,128)(2,1)S(1)}, u32[]{:S(2)}, u32[]{:S(2)}) async-start(bf16[16,96,512]{2,1,0:T(8,128)(2,1)} %shard_map.91), calls=%async_computation.3 | async-start | bytes 3145728 | tf_op jit(solution)/shard_map/all_to_all | solution.py:417
  134.7 6.2 %copy-start.2 = (bf16[2048,512]{1,0:T(8,128)(2,1)S(1)}, bf16[2048,512]{1,0:T(8,128)(2,1)}, u32[]{:S(2)}) copy-start(bf16[2048,512]{1,0:T(8,128)(2,1)} %get-tuple-element.52.o_ref) | copy-start | bytes 6291460
  135.4 21.6 %collective-permute-start.9 = (bf16[512,256]{1,0:T(8,128)(2,1)S(1)}, bf16[512,256]{1,0:T(8,128)(2,1)S(1)}, u32[]{:S(2)}, u32[]{:S(2)}) collective-permute-start(bf16[512,256]{1,0:T(8,128)(2,1)S(1)} %get-tuple-element.54), channel_id=1, source_target_pairs={{0,160},{2,162},{4,164},{6,166},{8,168},{10,170},{12,172},{14,174}... | collective-permute-start | bytes 786440 | tf_op jit(solution)/shard_map/ppermute | solution.py:532
  140.8 16.1 %collective-permute-start.10 = (bf16[512,256]{1,0:T(8,128)(2,1)S(1)}, bf16[512,256]{1,0:T(8,128)(2,1)S(1)}, u32[]{:S(2)}, u32[]{:S(2)}) collective-permute-start(bf16[512,256]{1,0:T(8,128)(2,1)S(1)} %get-tuple-element.55), channel_id=1, source_target_pairs={{0,96},{2,98},{4,100},{6,102},{8,104},{10,106},{12,108},{14,110},{... | collective-permute-start | bytes 786440 | tf_op jit(solution)/shard_map/ppermute | solution.py:532
  158.1 15.7 %collective-permute-start.11 = (bf16[512,256]{1,0:T(8,128)(2,1)S(1)}, bf16[512,256]{1,0:T(8,128)(2,1)S(1)}, u32[]{:S(2)}, u32[]{:S(2)}) collective-permute-start(bf16[512,256]{1,0:T(8,128)(2,1)S(1)} %get-tuple-element.56), channel_id=1, source_target_pairs={{0,192},{2,194},{4,196},{6,198},{8,200},{10,202},{12,204},{14,206}... | collective-permute-start | bytes 786440 | tf_op jit(solution)/shard_map/ppermute | solution.py:532
  159.5 14.3 %collective-permute-start.12 = (bf16[512,256]{1,0:T(8,128)(2,1)S(1)}, bf16[512,256]{1,0:T(8,128)(2,1)S(1)}, u32[]{:S(2)}, u32[]{:S(2)}) collective-permute-start(bf16[512,256]{1,0:T(8,128)(2,1)S(1)} %get-tuple-element.57), channel_id=1, source_target_pairs={{0,64},{2,66},{4,68},{6,70},{8,72},{10,74},{12,76},{14,78},{16,80}... | collective-permute-start | bytes 786440 | tf_op jit(solution)/shard_map/ppermute | solution.py:532
  160.6 17.0 %all-to-all-start.2 = ((bf16[16,48,512]{2,1,0:T(8,128)(2,1)}), bf16[16,48,512]{2,1,0:T(8,128)(2,1)S(1)}, u32[]{:S(2)}, u32[]{:S(2)}) async-start(bf16[16,48,512]{2,1,0:T(8,128)(2,1)} %shard_map.90.refs_5_), calls=%async_computation.2 | async-start | bytes 1572864 | tf_op jit(solution)/shard_map/all_to_all | solution.py:417
  167.2 17.3 %collective-permute-start.14 = (bf16[512,256]{1,0:T(8,128)(2,1)S(1)}, bf16[512,256]{1,0:T(8,128)(2,1)S(1)}, u32[]{:S(2)}, u32[]{:S(2)}) collective-permute-start(bf16[512,256]{1,0:T(8,128)(2,1)S(1)} %get-tuple-element.60), channel_id=1, source_target_pairs={{0,128},{2,130},{4,132},{6,134},{8,136},{10,138},{12,140},{14,142}... | collective-permute-start | bytes 786440 | tf_op jit(solution)/shard_map/ppermute | solution.py:532
  170.1 22.8 %collective-permute-start.15 = (bf16[512,256]{1,0:T(8,128)(2,1)S(1)}, bf16[512,256]{1,0:T(8,128)(2,1)S(1)}, u32[]{:S(2)}, u32[]{:S(2)}) collective-permute-start(bf16[512,256]{1,0:T(8,128)(2,1)S(1)} %get-tuple-element.61), channel_id=1, source_target_pairs={{0,32},{2,34},{4,36},{6,38},{8,40},{10,42},{12,44},{14,46},{16,48}... | collective-permute-start | bytes 786440 | tf_op jit(solution)/shard_map/ppermute | solution.py:532
  178.2 14.7 %collective-permute-start.13 = (bf16[512,256]{1,0:T(8,128)(2,1)S(1)}, bf16[512,256]{1,0:T(8,128)(2,1)S(1)}, u32[]{:S(2)}, u32[]{:S(2)}) collective-permute-start(bf16[512,256]{1,0:T(8,128)(2,1)S(1)} %get-tuple-element.59), channel_id=1, source_target_pairs={{0,224},{2,226},{4,228},{6,230},{8,232},{10,234},{12,236},{14,238}... | collective-permute-start | bytes 786440 | tf_op jit(solution)/shard_map/ppermute | solution.py:532

commit v5 on v4

--- a/solution.py
+++ b/solution.py
@@ -388,23 +388,18 @@
                     ]
 
 
-def mark_kernel(place_ref, *refs):
-    mark_ref = refs[-1]
-    mark_ref[...] = jnp.broadcast_to(place_ref[0], mark_ref.shape).astype(F32)
-
-
-def join_kernel(place_ref, *refs):
-    blocks, outs, sems = refs[:ZN], refs[ZN : ZN + 4], refs[ZN + 4]
+def join_kernel(dist, place_ref, *refs):
+    blocks, outs, sems = refs[: len(dist)], refs[-5:-1], refs[-1]
     z = place_ref[0]
     copies = []
-    for d in range(ZN):
+    for i, d in enumerate(dist):
         cols = pl.ds(pl.multiple_of(((z + d) & (ZN - 1)) * PAIR, PAIR), PAIR)
         for t in range(4):
             copies.append(
                 pltpu.make_async_copy(
-                    blocks[d].at[t * TOK : (t + 1) * TOK, :],
+                    blocks[i].at[t * TOK : (t + 1) * TOK, :],
                     outs[t].at[:, cols],
-                    sems.at[d * 4 + t],
+                    sems.at[i * 4 + t],
                 )
             )
     for copy in copies:
@@ -515,6 +510,20 @@
         sends.append(send)
     back = {}
     waits = {}
+
+    def join(dist, outs, flops):
+        n = 1 + len(dist)
+        return call(
+            functools.partial(join_kernel, dist),
+            [place] + [back[d] for d in dist] + outs,
+            [out((TOK, ZN * PAIR), BF)] * 4,
+            [pltpu.SemaphoreType.DMA((4 * len(dist),))],
+            flops=flops,
+            specs={0: SMEM[0]} | {n + i: hbm for i in range(len(outs))},
+            out_specs={i: hbm for i in range(4)},
+            aliases={n + i: i for i in range(len(outs))},
+        )
+
     for step, chunk in enumerate(RETURNS):
         got = exchange(sends[step], PLANES)
         places = tuple(
@@ -533,23 +542,9 @@
         if step == 0:
             waits[1] = [back[d] for d in chunk] + [sends[2]]
         if step == 1:
-            waits[2] = list(
-                call(
-                    mark_kernel,
-                    [place] + [back[d] for d in SOON],
-                    [out((8, WIDTH), F32)],
-                    specs={0: SMEM[0]} | {j + 1: anywhere for j in range(len(SOON))},
-                    flops=10**11,
-                )
-            )
-    return call(
-        join_kernel,
-        [place] + [back[d] for d in range(ZN)],
-        [out((TOK, ZN * PAIR), BF)] * 4,
-        [pltpu.SemaphoreType.DMA((4 * ZN,))],
-        specs=SMEM,
-        out_specs={i: hbm for i in range(4)},
-    )
+            joined = join(RETURNS[0] + SOON, [], 10**11)
+            waits[2] = list(joined[:1])
+    return join(tuple(d for d in back if d not in RETURNS[0] + SOON), list(joined), 0)
 
 
 def solution(mesh):

time: 196 us -> 196 us (level)
  waiting for transfers between devices: 79.1 us -> 76.9 us
  transfers between devices with their start and end apart: 21 -> 21, of which waited for: 10 -> 9; matrix products, arithmetic and copies ran while one was open for 0% -> 0% of each run, Pallas kernels for 11% -> 12%
where the time goes in v5:
time: 196 us; the launch traced here: 195 us
  waiting for transfers between devices  76.9 us (39%)
  starting transfers between devices  71.3 us (36%)
  Pallas kernels  42 us (21%)
  local copies, waits for them, and re-layouts  3.58 us (2%)
    pallas_call x13, Pallas kernels, call(): pl.pallas_call(kernel, out_shape=tuple((pltpu.HBM(o.shape, o.dtype) if i...  42 us
    all_to_all x5, starting transfers between devices, exchange(): lax.all_to_all(array, 'seq', split_axis=0, concat_axis=0, axis_index_grou...  29.8 us
    all_to_all x5, waiting for transfers between devices, exchange(): lax.all_to_all(array, 'seq', split_axis=0, concat_axis=0, axis_index_grou...  29.2 us
    ppermute x7, waiting for transfers between devices, body(): moved[d] = lax.ppermute(blocks[d], 'seq', z_pairs(d))  26 us
    ppermute x7, waiting for transfers between devices, body(): back[d] = lax.ppermute(piece, 'seq', z_pairs(-d)) if d else piece  21.7 us
    ppermute x7, starting transfers between devices, body(): back[d] = lax.ppermute(piece, 'seq', z_pairs(-d)) if d else piece  19.8 us
    ppermute x7, starting transfers between devices, body(): moved[d] = lax.ppermute(blocks[d], 'seq', z_pairs(d))  16.1 us
    ppermute x2, starting transfers between devices, shift_owner(): return lax.ppermute(value, 'seq', pairs)  5.51 us
  transfers between devices with their start and end apart: 21, of which 9 were waited for; matrix products, arithmetic and copies ran while one was open for 0% of the time, Pallas kernels for 12%

profile of v5, /device:TPU:1, one launch (start us, length us, event | category | flops | bytes accessed | tf_op | source)
XLA Modules:
  0.0 194.9 jit_solution(487035122751890937)
XLA Ops:
  0.6 3.6 %shard_map.84 = (bf16[528,256]{1,0:T(8,128)(2,1)}, bf16[528,256]{1,0:T(8,128)(2,1)}, bf16[528,256]{1,0:T(8,128)(2,1)}, bf16[528,256]{1,0:T(8,128)(2,1)}, bf16[52...) custom-call(s32[16,128]{1,0:T(8,128)} %bitcast.3, ...), custom_call_target="tpu_custom_call" | custom-call | bytes 4268032 | tf_op jit(solution)/shard_map/pallas_call | solution.py:60
  4.3 2.5 %collective-permute-start = (bf16[528,256]{1,0:T(8,128)(2,1)}, bf16[528,256]{1,0:T(8,128)(2,1)S(1)}, u32[]{:S(2)}, u32[]{:S(2)}) collective-permute-start(bf16[528,256]{1,0:T(8,128)(2,1)} %get-tuple-element.38), channel_id=1, source_target_pairs={{0,32},{2,34},{4,36},{6,38},{8,40},{10,42},{12,44},{14,46},{16,48}... | collective-permute-start | bytes 811016 | tf_op jit(solution)/shard_map/ppermute | solution.py:440
  6.8 4.0 %collective-permute-start.1 = (bf16[528,256]{1,0:T(8,128)(2,1)}, bf16[528,256]{1,0:T(8,128)(2,1)S(1)}, u32[]{:S(2)}, u32[]{:S(2)}) collective-permute-start(bf16[528,256]{1,0:T(8,128)(2,1)} %get-tuple-element.39), channel_id=1, source_target_pairs={{0,224},{2,226},{4,228},{6,230},{8,232},{10,234},{12,236},{14,238}... | collective-permute-start | bytes 811016 | tf_op jit(solution)/shard_map/ppermute | solution.py:440
  10.9 0.0 collective-permute-start.2
  10.9 3.6 %collective-permute-start.3 = (bf16[528,256]{1,0:T(8,128)(2,1)}, bf16[528,256]{1,0:T(8,128)(2,1)S(1)}, u32[]{:S(2)}, u32[]{:S(2)}) collective-permute-start(bf16[528,256]{1,0:T(8,128)(2,1)} %get-tuple-element.42), channel_id=1, source_target_pairs={{0,192},{2,194},{4,196},{6,198},{8,200},{10,202},{12,204},{14,206}... | collective-permute-start | bytes 811016 | tf_op jit(solution)/shard_map/ppermute | solution.py:440
  14.4 0.3 collective-permute-start.4
  14.8 2.4 %collective-permute-done.refs_1_ = bf16[528,256]{1,0:T(8,128)(2,1)S(1)} collective-permute-done((bf16[528,256]{1,0:T(8,128)(2,1)}, bf16[528,256]{1,0:T(8,128)(2,1)S(1)}, u32[]{:S(2)}, u32[]{:S(2)}) %collective-permute-start) | collective-permute-done | bytes 270368 | tf_op jit(solution)/shard_map/ppermute | solution.py:440
  17.2 2.0 %collective-permute-start.5 = (bf16[528,256]{1,0:T(8,128)(2,1)}, bf16[528,256]{1,0:T(8,128)(2,1)S(1)}, u32[]{:S(2)}, u32[]{:S(2)}) collective-permute-start(bf16[528,256]{1,0:T(8,128)(2,1)} %get-tuple-element.44), channel_id=1, source_target_pairs={{0,160},{2,162},{4,164},{6,166},{8,168},{10,170},{12,172},{14,174}... | collective-permute-start | bytes 811016 | tf_op jit(solution)/shard_map/ppermute | solution.py:440
  19.2 3.6 %collective-permute-start.6 = (bf16[528,256]{1,0:T(8,128)(2,1)}, bf16[528,256]{1,0:T(8,128)(2,1)S(1)}, u32[]{:S(2)}, u32[]{:S(2)}) collective-permute-start(bf16[528,256]{1,0:T(8,128)(2,1)} %get-tuple-element.45), channel_id=1, source_target_pairs={{0,128},{2,130},{4,132},{6,134},{8,136},{10,138},{12,140},{14,142}... | collective-permute-start | bytes 811016 | tf_op jit(solution)/shard_map/ppermute | solution.py:440
  22.8 1.9 collective-permute-done.2.refs_3_
  24.8 1.0 copy-done.1
  25.7 2.7 %shard_map.85 = (bf16[16,96,512]{2,1,0:T(8,128)(2,1)}, s32[8,128]{1,0:T(8,128)S(1)}, bf16[16,16,128]{2,1,0:T(8,128)(2,1)S(1)}) custom-call(bf16[528,256]{1,0:T(8,128)(2,1)S(1)} %copy-done.1, bf16[528,256]{1,0:T(8,128)(2,1)S(1)} %collective-permute-done.refs_1_, bf16[528,256]{1,0:T(8,128)(2,1)S(1)} %collective-permute-done.1.refs_2_, ...), custom_call_target="tpu_custom_call" | custom-call | flops 1000000 | bytes 2723840 | tf_op jit(solution)/shard_map/pallas_call | solution.py:60
  28.5 6.8 %all-to-all-start = ((bf16[16,96,512]{2,1,0:T(8,128)(2,1)}), bf16[16,96,512]{2,1,0:T(8,128)(2,1)S(1)}, u32[]{:S(2)}, u32[]{:S(2)}) async-start(bf16[16,96,512]{2,1,0:T(8,128)(2,1)} %get-tuple-element.48), calls=%async_computation | async-start | bytes 3145728 | tf_op jit(solution)/shard_map/all_to_all | solution.py:412
  35.3 0.0 collective-permute-done.3.refs_0_
  35.3 11.1 %collective-permute-done.4.refs_1_ = bf16[528,256]{1,0:T(8,128)(2,1)S(1)} collective-permute-done((bf16[528,256]{1,0:T(8,128)(2,1)}, bf16[528,256]{1,0:T(8,128)(2,1)S(1)}, u32[]{:S(2)}, u32[]{:S(2)}) %collective-permute-start.4) | collective-permute-done | bytes 270368 | tf_op jit(solution)/shard_map/ppermute | solution.py:440
  46.3 10.5 %collective-permute-done.5.refs_2_ = bf16[528,256]{1,0:T(8,128)(2,1)S(1)} collective-permute-done((bf16[528,256]{1,0:T(8,128)(2,1)}, bf16[528,256]{1,0:T(8,128)(2,1)S(1)}, u32[]{:S(2)}, u32[]{:S(2)}) %collective-permute-start.5) | collective-permute-done | bytes 270368 | tf_op jit(solution)/shard_map/ppermute | solution.py:440
  56.9 0.0 collective-permute-done.6.refs_3_
  56.9 3.4 %shard_map.86 = (bf16[16,112,512]{2,1,0:T(8,128)(2,1)}, s32[8,128]{1,0:T(8,128)S(1)}, bf16[16,16,128]{2,1,0:T(8,128)(2,1)}) custom-call(bf16[528,256]{1,0:T(8,128)(2,1)S(1)} %collective-permute-done.3.refs_0_, bf16[528,256]{1,0:T(8,128)(2,1)S(1)} %collective-permute-done.4.refs_1_, bf16[528,256]{1,0:T(8,128)(2,1)S(1)} %collective-permute-done.5.refs_2_, ...), custom_call_target="tpu_custom_call" | custom-call | flops 99999997952 | bytes 3051520 | tf_op jit(solution)/shard_map/pallas_call | solution.py:60
  60.3 6.8 %all-to-all-start.1 = ((bf16[16,112,512]{2,1,0:T(8,128)(2,1)}), bf16[16,112,512]{2,1,0:T(8,128)(2,1)S(1)}, u32[]{:S(2)}, u32[]{:S(2)}) async-start(bf16[16,112,512]{2,1,0:T(8,128)(2,1)} %get-tuple-element.49), calls=%async_computation.1 | async-start | bytes 3670016 | tf_op jit(solution)/shard_map/all_to_all | solution.py:412
  67.1 0.1 pad_add_fusion.place_ref
  67.2 22.9 %all-to-all-done.1.refs_1_ = bf16[16,112,512]{2,1,0:T(8,128)(2,1)S(1)} async-done(((bf16[16,112,512]{2,1,0:T(8,128)(2,1)}), bf16[16,112,512]{2,1,0:T(8,128)(2,1)S(1)}, u32[]{:S(2)}, u32[]{:S(2)}) %all-to-all-start.1) | async-done | bytes 1835040 | tf_op jit(solution)/shard_map/all_to_all | solution.py:412
  90.1 8.1 %shard_map.87 = (bf16[8,256,512]{2,1,0:T(8,128)(2,1)S(1)}, bf16[256,256]{1,0:T(8,128)(2,1)S(1)}, bf16[256,512]{1,0:T(8,128)(2,1)S(1)}, s32[1,3072]{1,0:T(1,128)S(1)}) custom-call(s32[2]{0:T(128)S(1)} %pad_add_fusion.place_ref, bf16[16,96,512]{2,1,0:T(8,128)(2,1)S(1)} %all-to-all-done.refs_0_, bf16[16,112,512]{2,1,0:T(8,128)(2,1)S(1)} %all-to-all-done.1.refs_1_), custom_call_target="tpu_custom_call" | custom-call | flops 6442450944 | bytes 5910536 | tf_op jit(solution)/shard_map/pallas_call | solution.py:60
  98.2 1.3 collective-permute-start.8
  99.5 4.2 %collective-permute-start.7 = (bf16[256,256]{1,0:T(8,128)(2,1)S(1)}, bf16[256,256]{1,0:T(8,128)(2,1)S(1)}, u32[]{:S(2)}, u32[]{:S(2)}) collective-permute-start(bf16[256,256]{1,0:T(8,128)(2,1)S(1)} %get-tuple-element.52), channel_id=1, source_target_pairs={{0,2},{2,4},{4,6},{6,8},{8,10},{10,12},{12,14},{16,18},{18,20},{20... | collective-permute-start | bytes 393224 | tf_op jit(solution)/shard_map/ppermute | solution.py:421
  103.7 6.4 %shard_map.88 = (bf16[8,256,512]{2,1,0:T(8,128)(2,1)S(1)}, f32[2,256,256]{2,1,0:T(8,128)S(1)}) custom-call(bf16[8,256,512]{2,1,0:T(8,128)(2,1)S(1)} %get-tuple-element.51.in_ref), custom_call_target="tpu_custom_call" | custom-call | flops 1879048192 | bytes 4718592 | tf_op jit(solution)/shard_map/pallas_call | solution.py:60
  110.1 4.4 %shard_map.89 = (bf16[2048,512]{1,0:T(8,128)(2,1)}, bf16[16,48,512]{2,1,0:T(8,128)(2,1)}) custom-call(s32[2]{0:T(128)S(1)} %pad_add_fusion.place_ref, s32[1,3072]{1,0:T(1,128)S(1)} %get-tuple-element.50.rank_ref, bf16[8,256,512]{2,1,0:T(8,128)(2,1)S(1)} %get-tuple-element.51.in_ref, bf16[256,256]{1,0:T(8,128)(2,1)S(1)} %collective-permute-done.7.tail_ref, ...), custom_call_target="tpu_custom_call" | custom-call | flops 1610612736 | bytes 8007688 | tf_op jit(solution)/shard_map/pallas_call | solution.py:60
  114.6 6.0 %all-to-all-start.3 = ((bf16[16,48,512]{2,1,0:T(8,128)(2,1)}), bf16[16,48,512]{2,1,0:T(8,128)(2,1)S(1)}, u32[]{:S(2)}, u32[]{:S(2)}) async-start(bf16[16,48,512]{2,1,0:T(8,128)(2,1)} %get-tuple-element.57), calls=%async_computation.3 | async-start | bytes 1572864 | tf_op jit(solution)/shard_map/all_to_all | solution.py:412
  120.5 1.6 copy-done.2
  122.1 4.7 %shard_map.90 = bf16[16,96,512]{2,1,0:T(8,128)(2,1)} custom-call(s32[1,3072]{1,0:T(1,128)S(1)} %get-tuple-element.50.rank_ref, bf16[2048,512]{1,0:T(8,128)(2,1)S(1)} %copy-done.2), custom_call_target="tpu_custom_call" | custom-call | flops 1000000000 | bytes 3682304 | tf_op jit(solution)/shard_map/pallas_call | solution.py:60
  126.8 4.2 %all-to-all-done.3.refs_2_ = bf16[16,48,512]{2,1,0:T(8,128)(2,1)S(1)} async-done(((bf16[16,48,512]{2,1,0:T(8,128)(2,1)}), bf16[16,48,512]{2,1,0:T(8,128)(2,1)S(1)}, u32[]{:S(2)}, u32[]{:S(2)}) %all-to-all-start.3) | async-done | bytes 786464 | tf_op jit(solution)/shard_map/all_to_all | solution.py:412
  131.0 3.7 %all-to-all-start.2 = ((bf16[16,96,512]{2,1,0:T(8,128)(2,1)}), bf16[16,96,512]{2,1,0:T(8,128)(2,1)S(1)}, u32[]{:S(2)}, u32[]{:S(2)}) async-start(bf16[16,96,512]{2,1,0:T(8,128)(2,1)} %shard_map.90), calls=%async_computation.2 | async-start | bytes 3145728 | tf_op jit(solution)/shard_map/all_to_all | solution.py:412
  134.7 0.7 shard_map.91
  135.4 5.4 %collective-permute-start.9 = (bf16[512,256]{1,0:T(8,128)(2,1)S(1)}, bf16[512,256]{1,0:T(8,128)(2,1)S(1)}, u32[]{:S(2)}, u32[]{:S(2)}) collective-permute-start(bf16[512,256]{1,0:T(8,128)(2,1)S(1)} %get-tuple-element.58), channel_id=1, source_target_pairs={{0,160},{2,162},{4,164},{6,166},{8,168},{10,170},{12,172},{14,174}... | collective-permute-start | bytes 786440 | tf_op jit(solution)/shard_map/ppermute | solution.py:541
  140.9 2.8 %shard_map.92.refs_5_ = bf16[16,48,512]{2,1,0:T(8,128)(2,1)} custom-call(s32[1,3072]{1,0:T(1,128)S(1)} %get-tuple-element.50.rank_ref, bf16[2048,512]{1,0:T(8,128)(2,1)S(1)} %copy-done.3), custom_call_target="tpu_custom_call" | custom-call | flops 1000000000 | bytes 2895872 | tf_op jit(solution)/shard_map/pallas_call | solution.py:60
  143.6 13.3 %collective-permute-done.9.refs_3_.refs_0_ = bf16[512,256]{1,0:T(8,128)(2,1)S(1)} collective-permute-done((bf16[512,256]{1,0:T(8,128)(2,1)S(1)}, bf16[512,256]{1,0:T(8,128)(2,1)S(1)}, u32[]{:S(2)}, u32[]{:S(2)}) %collective-permute-start.9) | collective-permute-done | bytes 262176 | tf_op jit(solution)/shard_map/ppermute | solution.py:541
  157.0 1.2 shard_map.93
  158.1 1.3 collective-permute-start.13
  159.5 1.1 collective-permute-start.14
  160.6 6.6 %all-to-all-start.4 = ((bf16[16,48,512]{2,1,0:T(8,128)(2,1)}), bf16[16,48,512]{2,1,0:T(8,128)(2,1)S(1)}, u32[]{:S(2)}, u32[]{:S(2)}) async-start(bf16[16,48,512]{2,1,0:T(8,128)(2,1)} %shard_map.92.refs_5_), calls=%async_computation.4 | async-start | bytes 1572864 | tf_op jit(solution)/shard_map/all_to_all | solution.py:412
  167.2 3.0 %collective-permute-start.11 = (bf16[512,256]{1,0:T(8,128)(2,1)S(1)}, bf16[512,256]{1,0:T(8,128)(2,1)S(1)}, u32[]{:S(2)}, u32[]{:S(2)}) collective-permute-start(bf16[512,256]{1,0:T(8,128)(2,1)S(1)} %get-tuple-element.60), channel_id=1, source_target_pairs={{0,128},{2,130},{4,132},{6,134},{8,136},{10,138},{12,140},{14,142}... | collective-permute-start | bytes 786440 | tf_op jit(solution)/shard_map/ppermute | solution.py:541
  170.2 3.6 %collective-permute-start.12 = (bf16[512,256]{1,0:T(8,128)(2,1)S(1)}, bf16[512,256]{1,0:T(8,128)(2,1)S(1)}, u32[]{:S(2)}, u32[]{:S(2)}) collective-permute-start(bf16[512,256]{1,0:T(8,128)(2,1)S(1)} %get-tuple-element.61), channel_id=1, source_target_pairs={{0,32},{2,34},{4,36},{6,38},{8,40},{10,42},{12,44},{14,46},{16,48}... | collective-permute-start | bytes 786440 | tf_op jit(solution)/shard_map/ppermute | solution.py:541
  173.8 1.6 shard_map.94
  175.5 2.1 %all-to-all-done.4.refs_2_ = bf16[16,48,512]{2,1,0:T(8,128)(2,1)S(1)} async-done(((bf16[16,48,512]{2,1,0:T(8,128)(2,1)}), bf16[16,48,512]{2,1,0:T(8,128)(2,1)S(1)}, u32[]{:S(2)}, u32[]{:S(2)}) %all-to-all-start.4) | async-done | bytes 786464 | tf_op jit(solution)/shard_map/all_to_all | solution.py:412
  177.6 1.0 copy-done
  178.6 0.7 shard_map.95
  179.3 5.3 %collective-permute-start.15 = (bf16[512,256]{1,0:T(8,128)(2,1)S(1)}, bf16[512,256]{1,0:T(8,128)(2,1)S(1)}, u32[]{:S(2)}, u32[]{:S(2)}) collective-permute-start(bf16[512,256]{1,0:T(8,128)(2,1)S(1)} %get-tuple-element.66), channel_id=1, source_target_pairs={{0,224},{2,226},{4,228},{6,230},{8,232},{10,234},{12,236},{14,238}... | collective-permute-start | bytes 786440 | tf_op jit(solution)/shard_map/ppermute | solution.py:541
  184.7 8.4 %collective-permute-done.12.refs_1_ = bf16[512,256]{1,0:T(8,128)(2,1)S(1)} collective-permute-done((bf16[512,256]{1,0:T(8,128)(2,1)S(1)}, bf16[512,256]{1,0:T(8,128)(2,1)S(1)}, u32[]{:S(2)}, u32[]{:S(2)}) %collective-permute-start.12) | collective-permute-done | bytes 262176 | tf_op jit(solution)/shard_map/ppermute | solution.py:541
  193.0 1.6 shard_map.96
  (16 shorter events, 0.0 us)
Async XLA Ops:
  4.3 12.9 %collective-permute-start = (bf16[528,256]{1,0:T(8,128)(2,1)}, bf16[528,256]{1,0:T(8,128)(2,1)S(1)}, u32[]{:S(2)}, u32[]{:S(2)}) collective-permute-start(bf16[528,256]{1,0:T(8,128)(2,1)} %get-tuple-element.38), channel_id=1, source_target_pairs={{0,32},{2,34},{4,36},{6,38},{8,40},{10,42},{12,44},{14,46},{16,48}... | collective-permute-start | bytes 811016 | tf_op jit(solution)/shard_map/ppermute | solution.py:440
  6.8 12.4 %collective-permute-start.1 = (bf16[528,256]{1,0:T(8,128)(2,1)}, bf16[528,256]{1,0:T(8,128)(2,1)S(1)}, u32[]{:S(2)}, u32[]{:S(2)}) collective-permute-start(bf16[528,256]{1,0:T(8,128)(2,1)} %get-tuple-element.39), channel_id=1, source_target_pairs={{0,224},{2,226},{4,228},{6,230},{8,232},{10,234},{12,236},{14,238}... | collective-permute-start | bytes 811016 | tf_op jit(solution)/shard_map/ppermute | solution.py:440
  10.9 13.9 %collective-permute-start.2 = (bf16[528,256]{1,0:T(8,128)(2,1)}, bf16[528,256]{1,0:T(8,128)(2,1)S(1)}, u32[]{:S(2)}, u32[]{:S(2)}) collective-permute-start(bf16[528,256]{1,0:T(8,128)(2,1)} %get-tuple-element.40), channel_id=1, source_target_pairs={{0,64},{2,66},{4,68},{6,70},{8,72},{10,74},{12,76},{14,78},{16,80}... | collective-permute-start | bytes 811016 | tf_op jit(solution)/shard_map/ppermute | solution.py:440
  10.9 24.4 %collective-permute-start.3 = (bf16[528,256]{1,0:T(8,128)(2,1)}, bf16[528,256]{1,0:T(8,128)(2,1)S(1)}, u32[]{:S(2)}, u32[]{:S(2)}) collective-permute-start(bf16[528,256]{1,0:T(8,128)(2,1)} %get-tuple-element.42), channel_id=1, source_target_pairs={{0,192},{2,194},{4,196},{6,198},{8,200},{10,202},{12,204},{14,206}... | collective-permute-start | bytes 811016 | tf_op jit(solution)/shard_map/ppermute | solution.py:440
  14.4 31.9 %collective-permute-start.4 = (bf16[528,256]{1,0:T(8,128)(2,1)}, bf16[528,256]{1,0:T(8,128)(2,1)S(1)}, u32[]{:S(2)}, u32[]{:S(2)}) collective-permute-start(bf16[528,256]{1,0:T(8,128)(2,1)} %get-tuple-element.43), channel_id=1, source_target_pairs={{0,96},{2,98},{4,100},{6,102},{8,104},{10,106},{12,108},{14,110},{... | collective-permute-start | bytes 811016 | tf_op jit(solution)/shard_map/ppermute | solution.py:440
  17.2 39.7 %collective-permute-start.5 = (bf16[528,256]{1,0:T(8,128)(2,1)}, bf16[528,256]{1,0:T(8,128)(2,1)S(1)}, u32[]{:S(2)}, u32[]{:S(2)}) collective-permute-start(bf16[528,256]{1,0:T(8,128)(2,1)} %get-tuple-element.44), channel_id=1, source_target_pairs={{0,160},{2,162},{4,164},{6,166},{8,168},{10,170},{12,172},{14,174}... | collective-permute-start | bytes 811016 | tf_op jit(solution)/shard_map/ppermute | solution.py:440
  19.2 37.7 %collective-permute-start.6 = (bf16[528,256]{1,0:T(8,128)(2,1)}, bf16[528,256]{1,0:T(8,128)(2,1)S(1)}, u32[]{:S(2)}, u32[]{:S(2)}) collective-permute-start(bf16[528,256]{1,0:T(8,128)(2,1)} %get-tuple-element.45), channel_id=1, source_target_pairs={{0,128},{2,130},{4,132},{6,134},{8,136},{10,138},{12,140},{14,142}... | collective-permute-start | bytes 811016 | tf_op jit(solution)/shard_map/ppermute | solution.py:440
  24.8 1.0 copy-start.1
  28.5 31.8 %all-to-all-start = ((bf16[16,96,512]{2,1,0:T(8,128)(2,1)}), bf16[16,96,512]{2,1,0:T(8,128)(2,1)S(1)}, u32[]{:S(2)}, u32[]{:S(2)}) async-start(bf16[16,96,512]{2,1,0:T(8,128)(2,1)} %get-tuple-element.48), calls=%async_computation | async-start | bytes 3145728 | tf_op jit(solution)/shard_map/all_to_all | solution.py:412
  60.3 29.8 %all-to-all-start.1 = ((bf16[16,112,512]{2,1,0:T(8,128)(2,1)}), bf16[16,112,512]{2,1,0:T(8,128)(2,1)S(1)}, u32[]{:S(2)}, u32[]{:S(2)}) async-start(bf16[16,112,512]{2,1,0:T(8,128)(2,1)} %get-tuple-element.49), calls=%async_computation.1 | async-start | bytes 3670016 | tf_op jit(solution)/shard_map/all_to_all | solution.py:412
  98.2 11.9 %collective-permute-start.8 = (bf16[256,512]{1,0:T(8,128)(2,1)S(1)}, bf16[256,512]{1,0:T(8,128)(2,1)S(1)}, u32[]{:S(2)}, u32[]{:S(2)}) collective-permute-start(bf16[256,512]{1,0:T(8,128)(2,1)S(1)} %get-tuple-element.53), channel_id=1, source_target_pairs={{2,0},{4,2},{6,4},{8,6},{10,8},{12,10},{14,12},{18,16},{20,18},{22... | collective-permute-start | bytes 786440 | tf_op jit(solution)/shard_map/ppermute | solution.py:421
  99.5 10.6 %collective-permute-start.7 = (bf16[256,256]{1,0:T(8,128)(2,1)S(1)}, bf16[256,256]{1,0:T(8,128)(2,1)S(1)}, u32[]{:S(2)}, u32[]{:S(2)}) collective-permute-start(bf16[256,256]{1,0:T(8,128)(2,1)S(1)} %get-tuple-element.52), channel_id=1, source_target_pairs={{0,2},{2,4},{4,6},{6,8},{8,10},{10,12},{12,14},{16,18},{18,20},{20... | collective-permute-start | bytes 393224 | tf_op jit(solution)/shard_map/ppermute | solution.py:421
  114.6 16.4 %all-to-all-start.3 = ((bf16[16,48,512]{2,1,0:T(8,128)(2,1)}), bf16[16,48,512]{2,1,0:T(8,128)(2,1)S(1)}, u32[]{:S(2)}, u32[]{:S(2)}) async-start(bf16[16,48,512]{2,1,0:T(8,128)(2,1)} %get-tuple-element.57), calls=%async_computation.3 | async-start | bytes 1572864 | tf_op jit(solution)/shard_map/all_to_all | solution.py:412
  120.5 1.6 copy-start.2
  131.0 26.0 %all-to-all-start.2 = ((bf16[16,96,512]{2,1,0:T(8,128)(2,1)}), bf16[16,96,512]{2,1,0:T(8,128)(2,1)S(1)}, u32[]{:S(2)}, u32[]{:S(2)}) async-start(bf16[16,96,512]{2,1,0:T(8,128)(2,1)} %shard_map.90), calls=%async_computation.2 | async-start | bytes 3145728 | tf_op jit(solution)/shard_map/all_to_all | solution.py:412
  134.7 6.2 %copy-start.3 = (bf16[2048,512]{1,0:T(8,128)(2,1)S(1)}, bf16[2048,512]{1,0:T(8,128)(2,1)}, u32[]{:S(2)}) copy-start(bf16[2048,512]{1,0:T(8,128)(2,1)} %get-tuple-element.56.o_ref) | copy-start | bytes 6291460
  135.4 21.6 %collective-permute-start.9 = (bf16[512,256]{1,0:T(8,128)(2,1)S(1)}, bf16[512,256]{1,0:T(8,128)(2,1)S(1)}, u32[]{:S(2)}, u32[]{:S(2)}) collective-permute-start(bf16[512,256]{1,0:T(8,128)(2,1)S(1)} %get-tuple-element.58), channel_id=1, source_target_pairs={{0,160},{2,162},{4,164},{6,166},{8,168},{10,170},{12,172},{14,174}... | collective-permute-start | bytes 786440 | tf_op jit(solution)/shard_map/ppermute | solution.py:541
  140.9 16.1 %collective-permute-start.10 = (bf16[512,256]{1,0:T(8,128)(2,1)S(1)}, bf16[512,256]{1,0:T(8,128)(2,1)S(1)}, u32[]{:S(2)}, u32[]{:S(2)}) collective-permute-start(bf16[512,256]{1,0:T(8,128)(2,1)S(1)} %get-tuple-element.59), channel_id=1, source_target_pairs={{0,96},{2,98},{4,100},{6,102},{8,104},{10,106},{12,108},{14,110},{... | collective-permute-start | bytes 786440 | tf_op jit(solution)/shard_map/ppermute | solution.py:541
  158.1 15.7 %collective-permute-start.13 = (bf16[512,256]{1,0:T(8,128)(2,1)S(1)}, bf16[512,256]{1,0:T(8,128)(2,1)S(1)}, u32[]{:S(2)}, u32[]{:S(2)}) collective-permute-start(bf16[512,256]{1,0:T(8,128)(2,1)S(1)} %get-tuple-element.62), channel_id=1, source_target_pairs={{0,192},{2,194},{4,196},{6,198},{8,200},{10,202},{12,204},{14,206}... | collective-permute-start | bytes 786440 | tf_op jit(solution)/shard_map/ppermute | solution.py:541
  159.5 14.3 %collective-permute-start.14 = (bf16[512,256]{1,0:T(8,128)(2,1)S(1)}, bf16[512,256]{1,0:T(8,128)(2,1)S(1)}, u32[]{:S(2)}, u32[]{:S(2)}) collective-permute-start(bf16[512,256]{1,0:T(8,128)(2,1)S(1)} %get-tuple-element.63), channel_id=1, source_target_pairs={{0,64},{2,66},{4,68},{6,70},{8,72},{10,74},{12,76},{14,78},{16,80}... | collective-permute-start | bytes 786440 | tf_op jit(solution)/shard_map/ppermute | solution.py:541
  160.6 17.0 %all-to-all-start.4 = ((bf16[16,48,512]{2,1,0:T(8,128)(2,1)}), bf16[16,48,512]{2,1,0:T(8,128)(2,1)S(1)}, u32[]{:S(2)}, u32[]{:S(2)}) async-start(bf16[16,48,512]{2,1,0:T(8,128)(2,1)} %shard_map.92.refs_5_), calls=%async_computation.4 | async-start | bytes 1572864 | tf_op jit(solution)/shard_map/all_to_all | solution.py:412
  167.2 17.5 %collective-permute-start.11 = (bf16[512,256]{1,0:T(8,128)(2,1)S(1)}, bf16[512,256]{1,0:T(8,128)(2,1)S(1)}, u32[]{:S(2)}, u32[]{:S(2)}) collective-permute-start(bf16[512,256]{1,0:T(8,128)(2,1)S(1)} %get-tuple-element.60), channel_id=1, source_target_pairs={{0,128},{2,130},{4,132},{6,134},{8,136},{10,138},{12,140},{14,142}... | collective-permute-start | bytes 786440 | tf_op jit(solution)/shard_map/ppermute | solution.py:541
  170.2 22.8 %collective-permute-start.12 = (bf16[512,256]{1,0:T(8,128)(2,1)S(1)}, bf16[512,256]{1,0:T(8,128)(2,1)S(1)}, u32[]{:S(2)}, u32[]{:S(2)}) collective-permute-start(bf16[512,256]{1,0:T(8,128)(2,1)S(1)} %get-tuple-element.61), channel_id=1, source_target_pairs={{0,32},{2,34},{4,36},{6,38},{8,40},{10,42},{12,44},{14,46},{16,48}... | collective-permute-start | bytes 786440 | tf_op jit(solution)/shard_map/ppermute | solution.py:541
  177.5 1.0 copy-start
  179.3 13.7 %collective-permute-start.15 = (bf16[512,256]{1,0:T(8,128)(2,1)S(1)}, bf16[512,256]{1,0:T(8,128)(2,1)S(1)}, u32[]{:S(2)}, u32[]{:S(2)}) collective-permute-start(bf16[512,256]{1,0:T(8,128)(2,1)S(1)} %get-tuple-element.66), channel_id=1, source_target_pairs={{0,224},{2,226},{4,228},{6,230},{8,232},{10,234},{12,236},{14,238}... | collective-permute-start | bytes 786440 | tf_op jit(solution)/shard_map/ppermute | solution.py:541

commit v6 on v5

--- a/solution.py
+++ b/solution.py
@@ -37,6 +37,7 @@
 RETURNS = ((3, 5), (4, 2, 6, 7), (0, 1))
 ORDER = sum(CHUNKS, ())
 SOON = (2, 6)
+EARLY = (1, 7)
 PACK_HINT = (10**6, 10**11)
 PLANES = [[z * PLANE + i for i in range(PLANE)] for z in range(ZN)]
 
@@ -104,23 +105,30 @@
 TN = ((0,), (0,))
 
 
-def prep_kernel(ids_ref, *refs):
-    arrays, blocks, stages, sems = refs[:4], refs[4 : 4 + ZN], refs[4 + ZN : 8 + ZN], refs[8 + ZN]
+def prep_kernel(dist, ids_ref, *refs):
+    arrays, (blocks, sems) = refs[:4], (refs[-1 - len(dist) : -1], refs[-1])
     z = lax.axis_index("seq") // PLANE
-    copies = [pltpu.make_async_copy(arrays[t], stages[t], sems.at[t]) for t in range(4)]
+    copies = []
+    for i, d in enumerate(dist):
+        cols = pl.ds(pl.multiple_of(((z + d) & (ZN - 1)) * PAIR, PAIR), PAIR)
+        for t in range(4):
+            copies.append(
+                pltpu.make_async_copy(
+                    arrays[t].at[:, cols],
+                    blocks[i].at[t * TOK : (t + 1) * TOK, :],
+                    sems.at[i * 4 + t],
+                )
+            )
     for copy in copies:
         copy.start()
-    for d in range(ZN):
+    for i, d in enumerate(dist):
         at = ((z + d) & (ZN - 1)) * HPZ
         rows = [ids_ref[pl.ds(at + hh, 1), :] for hh in range(HPZ)]
         tile = jnp.concatenate(rows + [jnp.zeros((TILE - HPZ, TOK), I32)], axis=0)
-        blocks[d][4 * TOK :, 0:TOK] = tile.astype(F32).astype(BF)
-        blocks[d][4 * TOK :, TOK:] = jnp.zeros((TILE, PAIR - TOK), BF)
-    for t in range(4):
-        copies[t].wait()
-        for d in range(ZN):
-            cols = pl.ds(pl.multiple_of(((z + d) & (ZN - 1)) * PAIR, PAIR), PAIR)
-            blocks[d][t * TOK : (t + 1) * TOK, :] = stages[t][:, cols]
+        blocks[i][4 * TOK :, 0:TOK] = tile.astype(F32).astype(BF)
+        blocks[i][4 * TOK :, TOK:] = jnp.zeros((TILE, PAIR - TOK), BF)
+    for copy in copies:
+        copy.wait()
 
 
 def leave(stage_ref, out_ref, sems, i, n):
@@ -426,14 +434,18 @@
     place = jnp.stack([index // PLANE, index % RANGES]).astype(I32)
     hbm = pl.BlockSpec(memory_space=pltpu.HBM)
     anywhere = pl.BlockSpec(memory_space=pl.ANY)
-    blocks = call(
-        prep_kernel,
-        [cluster_ids.T, queries, keys, values, out_grad],
-        [out((4 * TOK + TILE, PAIR), BF)] * ZN,
-        [pltpu.VMEM((TOK, ZN * PAIR), BF)] * 4 + [pltpu.SemaphoreType.DMA((4,))],
-        specs={1: hbm, 2: hbm, 3: hbm, 4: hbm},
-        limit=60,
-    )
+    blocks = {}
+    for dist in EARLY, tuple(d for d in ORDER if d not in EARLY):
+        earlier = [blocks[EARLY[0]]] if blocks else []
+        made = call(
+            functools.partial(prep_kernel, dist),
+            [cluster_ids.T, queries, keys, values, out_grad] + earlier,
+            [out((4 * TOK + TILE, PAIR), BF)] * len(dist),
+            [pltpu.SemaphoreType.DMA((4 * len(dist),))],
+            specs={1: hbm, 2: hbm, 3: hbm, 4: hbm, 5: anywhere},
+            limit=60,
+        )
+        blocks.update(zip(dist, made))
     moved = {0: blocks[0]}
     for d in ORDER:
         if d:

time: 196 us -> 196 us (level); the launches traced: 195 us -> 192 us
  waiting for transfers between devices: 76.9 us -> 71.3 us
  Pallas kernels: 42 us -> 44.4 us
    ppermute x7, waiting for transfers between devices: 26 us -> 19.8 us  [body(): moved[d] = lax.ppermute(blocks[d], 'seq', z_pairs(d))]
    ppermute x7, starting transfers between devices: 19.8 us -> 17.3 us  [body(): back[d] = lax.ppermute(piece, 'seq', z_pairs(-d)) if d else piece]
    pallas_call x13 -> x14, Pallas kernels: 42 us -> 44.4 us  [call(): pl.pallas_call(kernel, out_shape=tuple((pltpu.HBM(o.shape, o.dtype) if i...]
  transfers between devices with their start and end apart: 21 -> 21, of which waited for: 9 -> 9; matrix products, arithmetic and copies ran while one was open for 0% -> 0% of each run, Pallas kernels for 12% -> 14%
where the time goes in v6:
time: 196 us; the launch traced here: 192 us
  starting transfers between devices  71.6 us (37%)
  waiting for transfers between devices  71.3 us (36%)
  Pallas kernels  44.4 us (23%)
  local copies, waits for them, and re-layouts  3.58 us (2%)
    pallas_call x14, Pallas kernels, call(): pl.pallas_call(kernel, out_shape=tuple((pltpu.HBM(o.shape, o.dtype) if i...  44.4 us
    all_to_all x5, starting transfers between devices, exchange(): lax.all_to_all(array, 'seq', split_axis=0, concat_axis=0, axis_index_grou...  31.4 us
    all_to_all x5, waiting for transfers between devices, exchange(): lax.all_to_all(array, 'seq', split_axis=0, concat_axis=0, axis_index_grou...  30.2 us
    ppermute x7, waiting for transfers between devices, body(): back[d] = lax.ppermute(piece, 'seq', z_pairs(-d)) if d else piece  21.4 us
    ppermute x7, waiting for transfers between devices, body(): moved[d] = lax.ppermute(blocks[d], 'seq', z_pairs(d))  19.8 us
    ppermute x7, starting transfers between devices, body(): moved[d] = lax.ppermute(blocks[d], 'seq', z_pairs(d))  17.4 us
    ppermute x7, starting transfers between devices, body(): back[d] = lax.ppermute(piece, 'seq', z_pairs(-d)) if d else piece  17.3 us
    ppermute x2, starting transfers between devices, shift_owner(): return lax.ppermute(value, 'seq', pairs)  5.51 us
  transfers between devices with their start and end apart: 21, of which 9 were waited for; matrix products, arithmetic and copies ran while one was open for 0% of the time, Pallas kernels for 14%

profile of v6, /device:TPU:1, one launch (start us, length us, event | category | flops | bytes accessed | tf_op | source)
XLA Modules:
  0.0 192.1 jit_solution(8144511164485420259)
XLA Ops:
  0.6 2.6 %shard_map.84 = (bf16[528,256]{1,0:T(8,128)(2,1)}, bf16[528,256]{1,0:T(8,128)(2,1)}) custom-call(s32[16,128]{1,0:T(8,128)} %bitcast.3, bf16[128,2048]{1,0:T(8,128)(2,1)} %refs_0_.3, bf16[128,2048]{1,0:T(8,128)(2,1)} %refs_1_.3, bf16[128,2048]{1,0:T(8,128)(2,1)} %refs_2_.3, bf16[128,2048]{1,0:T(8,128)(2,1)} %refs_3_.3), custom_call_target="tpu_custom_call" | custom-call | bytes 2646016 | tf_op jit(solution)/shard_map/pallas_call | solution.py:61
  3.3 6.5 %collective-permute-start.1 = (bf16[528,256]{1,0:T(8,128)(2,1)}, bf16[528,256]{1,0:T(8,128)(2,1)S(1)}, u32[]{:S(2)}, u32[]{:S(2)}) collective-permute-start(bf16[528,256]{1,0:T(8,128)(2,1)} %get-tuple-element.39), channel_id=1, source_target_pairs={{0,224},{2,226},{4,228},{6,230},{8,232},{10,234},{12,236},{14,238}... | collective-permute-start | bytes 811016 | tf_op jit(solution)/shard_map/ppermute | solution.py:452
  9.7 0.0 collective-permute-start
  9.8 3.5 %shard_map.85 = (bf16[528,256]{1,0:T(8,128)(2,1)}, bf16[528,256]{1,0:T(8,128)(2,1)}, bf16[528,256]{1,0:T(8,128)(2,1)}, bf16[528,256]{1,0:T(8,128)(2,1)}, bf16[52...) custom-call(s32[16,128]{1,0:T(8,128)} %bitcast.4, bf16[128,2048]{1,0:T(8,128)(2,1)} %refs_0_.3, bf16[128,2048]{1,0:T(8,128)(2,1)} %refs_1_.3, ...), custom_call_target="tpu_custom_call" | custom-call | bytes 3997696 | tf_op jit(solution)/shard_map/pallas_call | solution.py:61
  13.2 0.1 collective-permute-start.2
  13.3 3.6 %collective-permute-start.3 = (bf16[528,256]{1,0:T(8,128)(2,1)}, bf16[528,256]{1,0:T(8,128)(2,1)S(1)}, u32[]{:S(2)}, u32[]{:S(2)}) collective-permute-start(bf16[528,256]{1,0:T(8,128)(2,1)} %get-tuple-element.42), channel_id=1, source_target_pairs={{0,192},{2,194},{4,196},{6,198},{8,200},{10,202},{12,204},{14,206}... | collective-permute-start | bytes 811016 | tf_op jit(solution)/shard_map/ppermute | solution.py:452
  16.9 0.5 collective-permute-start.4
  17.4 0.0 collective-permute-done.1.refs_2_
  17.4 4.0 %collective-permute-start.5 = (bf16[528,256]{1,0:T(8,128)(2,1)}, bf16[528,256]{1,0:T(8,128)(2,1)S(1)}, u32[]{:S(2)}, u32[]{:S(2)}) collective-permute-start(bf16[528,256]{1,0:T(8,128)(2,1)} %get-tuple-element.44), channel_id=1, source_target_pairs={{0,160},{2,162},{4,164},{6,166},{8,168},{10,170},{12,172},{14,174}... | collective-permute-start | bytes 811016 | tf_op jit(solution)/shard_map/ppermute | solution.py:452
  21.4 2.8 %collective-permute-start.6 = (bf16[528,256]{1,0:T(8,128)(2,1)}, bf16[528,256]{1,0:T(8,128)(2,1)S(1)}, u32[]{:S(2)}, u32[]{:S(2)}) collective-permute-start(bf16[528,256]{1,0:T(8,128)(2,1)} %get-tuple-element.45), channel_id=1, source_target_pairs={{0,128},{2,130},{4,132},{6,134},{8,136},{10,138},{12,140},{14,142}... | collective-permute-start | bytes 811016 | tf_op jit(solution)/shard_map/ppermute | solution.py:452
  24.2 2.2 %collective-permute-done.2.refs_3_ = bf16[528,256]{1,0:T(8,128)(2,1)S(1)} collective-permute-done((bf16[528,256]{1,0:T(8,128)(2,1)}, bf16[528,256]{1,0:T(8,128)(2,1)S(1)}, u32[]{:S(2)}, u32[]{:S(2)}) %collective-permute-start.2) | collective-permute-done | bytes 270368 | tf_op jit(solution)/shard_map/ppermute | solution.py:452
  26.3 1.0 copy-done.1
  27.3 2.7 %shard_map.86 = (bf16[16,96,512]{2,1,0:T(8,128)(2,1)}, s32[8,128]{1,0:T(8,128)S(1)}, bf16[16,16,128]{2,1,0:T(8,128)(2,1)S(1)}) custom-call(bf16[528,256]{1,0:T(8,128)(2,1)S(1)} %copy-done.1, bf16[528,256]{1,0:T(8,128)(2,1)S(1)} %collective-permute-done.refs_1_, bf16[528,256]{1,0:T(8,128)(2,1)S(1)} %collective-permute-done.1.refs_2_, ...), custom_call_target="tpu_custom_call" | custom-call | flops 1000000 | bytes 2723840 | tf_op jit(solution)/shard_map/pallas_call | solution.py:61
  30.0 6.8 %all-to-all-start = ((bf16[16,96,512]{2,1,0:T(8,128)(2,1)}), bf16[16,96,512]{2,1,0:T(8,128)(2,1)S(1)}, u32[]{:S(2)}, u32[]{:S(2)}) async-start(bf16[16,96,512]{2,1,0:T(8,128)(2,1)} %get-tuple-element.48), calls=%async_computation | async-start | bytes 3145728 | tf_op jit(solution)/shard_map/all_to_all | solution.py:420
  36.8 10.0 %collective-permute-done.4.refs_1_ = bf16[528,256]{1,0:T(8,128)(2,1)S(1)} collective-permute-done((bf16[528,256]{1,0:T(8,128)(2,1)}, bf16[528,256]{1,0:T(8,128)(2,1)S(1)}, u32[]{:S(2)}, u32[]{:S(2)}) %collective-permute-start.4) | collective-permute-done | bytes 270368 | tf_op jit(solution)/shard_map/ppermute | solution.py:452
  46.8 7.6 %collective-permute-done.6.refs_3_ = bf16[528,256]{1,0:T(8,128)(2,1)S(1)} collective-permute-done((bf16[528,256]{1,0:T(8,128)(2,1)}, bf16[528,256]{1,0:T(8,128)(2,1)S(1)}, u32[]{:S(2)}, u32[]{:S(2)}) %collective-permute-start.6) | collective-permute-done | bytes 270368 | tf_op jit(solution)/shard_map/ppermute | solution.py:452
  54.4 3.4 %shard_map.87 = (bf16[16,112,512]{2,1,0:T(8,128)(2,1)}, s32[8,128]{1,0:T(8,128)S(1)}, bf16[16,16,128]{2,1,0:T(8,128)(2,1)}) custom-call(bf16[528,256]{1,0:T(8,128)(2,1)S(1)} %collective-permute-done.3.refs_0_, bf16[528,256]{1,0:T(8,128)(2,1)S(1)} %collective-permute-done.4.refs_1_, bf16[528,256]{1,0:T(8,128)(2,1)S(1)} %collective-permute-done.5.refs_2_, ...), custom_call_target="tpu_custom_call" | custom-call | flops 99999997952 | bytes 3051520 | tf_op jit(solution)/shard_map/pallas_call | solution.py:61
  57.9 6.8 %all-to-all-start.1 = ((bf16[16,112,512]{2,1,0:T(8,128)(2,1)}), bf16[16,112,512]{2,1,0:T(8,128)(2,1)S(1)}, u32[]{:S(2)}, u32[]{:S(2)}) async-start(bf16[16,112,512]{2,1,0:T(8,128)(2,1)} %get-tuple-element.49), calls=%async_computation.1 | async-start | bytes 3670016 | tf_op jit(solution)/shard_map/all_to_all | solution.py:420
  64.6 0.1 pad_add_fusion.place_ref
  64.7 21.2 %all-to-all-done.1.refs_1_ = bf16[16,112,512]{2,1,0:T(8,128)(2,1)S(1)} async-done(((bf16[16,112,512]{2,1,0:T(8,128)(2,1)}), bf16[16,112,512]{2,1,0:T(8,128)(2,1)S(1)}, u32[]{:S(2)}, u32[]{:S(2)}) %all-to-all-start.1) | async-done | bytes 1835040 | tf_op jit(solution)/shard_map/all_to_all | solution.py:420
  85.9 8.1 %shard_map.88 = (bf16[8,256,512]{2,1,0:T(8,128)(2,1)S(1)}, bf16[256,256]{1,0:T(8,128)(2,1)S(1)}, bf16[256,512]{1,0:T(8,128)(2,1)S(1)}, s32[1,3072]{1,0:T(1,128)S(1)}) custom-call(s32[2]{0:T(128)S(1)} %pad_add_fusion.place_ref, bf16[16,96,512]{2,1,0:T(8,128)(2,1)S(1)} %all-to-all-done.refs_0_, bf16[16,112,512]{2,1,0:T(8,128)(2,1)S(1)} %all-to-all-done.1.refs_1_), custom_call_target="tpu_custom_call" | custom-call | flops 6442450944 | bytes 5910536 | tf_op jit(solution)/shard_map/pallas_call | solution.py:61
  94.0 1.3 collective-permute-start.8
  95.3 4.2 %collective-permute-start.7 = (bf16[256,256]{1,0:T(8,128)(2,1)S(1)}, bf16[256,256]{1,0:T(8,128)(2,1)S(1)}, u32[]{:S(2)}, u32[]{:S(2)}) collective-permute-start(bf16[256,256]{1,0:T(8,128)(2,1)S(1)} %get-tuple-element.52), channel_id=1, source_target_pairs={{0,2},{2,4},{4,6},{6,8},{8,10},{10,12},{12,14},{16,18},{18,20},{20... | collective-permute-start | bytes 393224 | tf_op jit(solution)/shard_map/ppermute | solution.py:429
  99.5 6.4 %shard_map.89 = (bf16[8,256,512]{2,1,0:T(8,128)(2,1)S(1)}, f32[2,256,256]{2,1,0:T(8,128)S(1)}) custom-call(bf16[8,256,512]{2,1,0:T(8,128)(2,1)S(1)} %get-tuple-element.51.in_ref), custom_call_target="tpu_custom_call" | custom-call | flops 1879048192 | bytes 4718592 | tf_op jit(solution)/shard_map/pallas_call | solution.py:61
  105.9 4.4 %shard_map.90 = (bf16[2048,512]{1,0:T(8,128)(2,1)}, bf16[16,48,512]{2,1,0:T(8,128)(2,1)}) custom-call(s32[2]{0:T(128)S(1)} %pad_add_fusion.place_ref, s32[1,3072]{1,0:T(1,128)S(1)} %get-tuple-element.50.rank_ref, bf16[8,256,512]{2,1,0:T(8,128)(2,1)S(1)} %get-tuple-element.51.in_ref, bf16[256,256]{1,0:T(8,128)(2,1)S(1)} %collective-permute-done.7.tail_ref, ...), custom_call_target="tpu_custom_call" | custom-call | flops 1610612736 | bytes 8007688 | tf_op jit(solution)/shard_map/pallas_call | solution.py:61
  110.4 7.3 %all-to-all-start.3 = ((bf16[16,48,512]{2,1,0:T(8,128)(2,1)}), bf16[16,48,512]{2,1,0:T(8,128)(2,1)S(1)}, u32[]{:S(2)}, u32[]{:S(2)}) async-start(bf16[16,48,512]{2,1,0:T(8,128)(2,1)} %get-tuple-element.57), calls=%async_computation.3 | async-start | bytes 1572864 | tf_op jit(solution)/shard_map/all_to_all | solution.py:420
  117.7 1.6 copy-done.2
  119.3 4.6 %shard_map.91 = bf16[16,96,512]{2,1,0:T(8,128)(2,1)} custom-call(s32[1,3072]{1,0:T(1,128)S(1)} %get-tuple-element.50.rank_ref, bf16[2048,512]{1,0:T(8,128)(2,1)S(1)} %copy-done.2), custom_call_target="tpu_custom_call" | custom-call | flops 1000000000 | bytes 3682304 | tf_op jit(solution)/shard_map/pallas_call | solution.py:61
  123.9 4.2 %all-to-all-done.3.refs_2_ = bf16[16,48,512]{2,1,0:T(8,128)(2,1)S(1)} async-done(((bf16[16,48,512]{2,1,0:T(8,128)(2,1)}), bf16[16,48,512]{2,1,0:T(8,128)(2,1)S(1)}, u32[]{:S(2)}, u32[]{:S(2)}) %all-to-all-start.3) | async-done | bytes 786464 | tf_op jit(solution)/shard_map/all_to_all | solution.py:420
  128.1 3.7 %all-to-all-start.2 = ((bf16[16,96,512]{2,1,0:T(8,128)(2,1)}), bf16[16,96,512]{2,1,0:T(8,128)(2,1)S(1)}, u32[]{:S(2)}, u32[]{:S(2)}) async-start(bf16[16,96,512]{2,1,0:T(8,128)(2,1)} %shard_map.91), calls=%async_computation.2 | async-start | bytes 3145728 | tf_op jit(solution)/shard_map/all_to_all | solution.py:420
  131.8 0.7 shard_map.92
  132.5 10.7 %collective-permute-start.9 = (bf16[512,256]{1,0:T(8,128)(2,1)S(1)}, bf16[512,256]{1,0:T(8,128)(2,1)S(1)}, u32[]{:S(2)}, u32[]{:S(2)}) collective-permute-start(bf16[512,256]{1,0:T(8,128)(2,1)S(1)} %get-tuple-element.58), channel_id=1, source_target_pairs={{0,160},{2,162},{4,164},{6,166},{8,168},{10,170},{12,172},{14,174}... | collective-permute-start | bytes 786440 | tf_op jit(solution)/shard_map/ppermute | solution.py:553
  143.2 2.8 %shard_map.93.refs_5_ = bf16[16,48,512]{2,1,0:T(8,128)(2,1)} custom-call(s32[1,3072]{1,0:T(1,128)S(1)} %get-tuple-element.50.rank_ref, bf16[2048,512]{1,0:T(8,128)(2,1)S(1)} %copy-done.3), custom_call_target="tpu_custom_call" | custom-call | flops 1000000000 | bytes 2895872 | tf_op jit(solution)/shard_map/pallas_call | solution.py:61
  146.0 8.7 %collective-permute-done.9.refs_3_.refs_0_ = bf16[512,256]{1,0:T(8,128)(2,1)S(1)} collective-permute-done((bf16[512,256]{1,0:T(8,128)(2,1)S(1)}, bf16[512,256]{1,0:T(8,128)(2,1)S(1)}, u32[]{:S(2)}, u32[]{:S(2)}) %collective-permute-start.9) | collective-permute-done | bytes 262176 | tf_op jit(solution)/shard_map/ppermute | solution.py:553
  154.7 2.8 %collective-permute-done.10.refs_4_.refs_1_ = bf16[512,256]{1,0:T(8,128)(2,1)S(1)} collective-permute-done((bf16[512,256]{1,0:T(8,128)(2,1)S(1)}, bf16[512,256]{1,0:T(8,128)(2,1)S(1)}, u32[]{:S(2)}, u32[]{:S(2)}) %collective-permute-start.10) | collective-permute-done | bytes 262176 | tf_op jit(solution)/shard_map/ppermute | solution.py:553
  157.4 1.2 shard_map.94
  158.6 0.1 collective-permute-start.13
  158.7 2.4 %collective-permute-start.14 = (bf16[512,256]{1,0:T(8,128)(2,1)S(1)}, bf16[512,256]{1,0:T(8,128)(2,1)S(1)}, u32[]{:S(2)}, u32[]{:S(2)}) collective-permute-start(bf16[512,256]{1,0:T(8,128)(2,1)S(1)} %get-tuple-element.63), channel_id=1, source_target_pairs={{0,64},{2,66},{4,68},{6,70},{8,72},{10,74},{12,76},{14,78},{16,80}... | collective-permute-start | bytes 786440 | tf_op jit(solution)/shard_map/ppermute | solution.py:553
  161.1 6.8 %all-to-all-start.4 = ((bf16[16,48,512]{2,1,0:T(8,128)(2,1)}), bf16[16,48,512]{2,1,0:T(8,128)(2,1)S(1)}, u32[]{:S(2)}, u32[]{:S(2)}) async-start(bf16[16,48,512]{2,1,0:T(8,128)(2,1)} %shard_map.93.refs_5_), calls=%async_computation.4 | async-start | bytes 1572864 | tf_op jit(solution)/shard_map/all_to_all | solution.py:420
  167.9 0.1 collective-permute-start.11
  168.0 3.8 %collective-permute-start.12 = (bf16[512,256]{1,0:T(8,128)(2,1)S(1)}, bf16[512,256]{1,0:T(8,128)(2,1)S(1)}, u32[]{:S(2)}, u32[]{:S(2)}) collective-permute-start(bf16[512,256]{1,0:T(8,128)(2,1)S(1)} %get-tuple-element.61), channel_id=1, source_target_pairs={{0,32},{2,34},{4,36},{6,38},{8,40},{10,42},{12,44},{14,46},{16,48}... | collective-permute-start | bytes 786440 | tf_op jit(solution)/shard_map/ppermute | solution.py:553
  171.8 1.6 shard_map.95
  173.4 4.8 %all-to-all-done.4.refs_2_ = bf16[16,48,512]{2,1,0:T(8,128)(2,1)S(1)} async-done(((bf16[16,48,512]{2,1,0:T(8,128)(2,1)}), bf16[16,48,512]{2,1,0:T(8,128)(2,1)S(1)}, u32[]{:S(2)}, u32[]{:S(2)}) %all-to-all-start.4) | async-done | bytes 786464 | tf_op jit(solution)/shard_map/all_to_all | solution.py:420
  178.3 1.0 copy-done
  179.3 0.7 shard_map.96
  180.0 0.3 collective-permute-start.15
  180.4 9.9 %collective-permute-done.12.refs_1_ = bf16[512,256]{1,0:T(8,128)(2,1)S(1)} collective-permute-done((bf16[512,256]{1,0:T(8,128)(2,1)S(1)}, bf16[512,256]{1,0:T(8,128)(2,1)S(1)}, u32[]{:S(2)}, u32[]{:S(2)}) %collective-permute-start.12) | collective-permute-done | bytes 262176 | tf_op jit(solution)/shard_map/ppermute | solution.py:553
  190.3 1.6 shard_map.97
  (17 shorter events, 0.0 us)
Async XLA Ops:
  3.3 14.1 %collective-permute-start.1 = (bf16[528,256]{1,0:T(8,128)(2,1)}, bf16[528,256]{1,0:T(8,128)(2,1)S(1)}, u32[]{:S(2)}, u32[]{:S(2)}) collective-permute-start(bf16[528,256]{1,0:T(8,128)(2,1)} %get-tuple-element.39), channel_id=1, source_target_pairs={{0,224},{2,226},{4,228},{6,230},{8,232},{10,234},{12,236},{14,238}... | collective-permute-start | bytes 811016 | tf_op jit(solution)/shard_map/ppermute | solution.py:452
  9.7 11.6 %collective-permute-start = (bf16[528,256]{1,0:T(8,128)(2,1)}, bf16[528,256]{1,0:T(8,128)(2,1)S(1)}, u32[]{:S(2)}, u32[]{:S(2)}) collective-permute-start(bf16[528,256]{1,0:T(8,128)(2,1)} %get-tuple-element.37.refs_4_), channel_id=1, source_target_pairs={{0,32},{2,34},{4,36},{6,38},{8,40},{10,42},{12,44},{14,46},{16,48}... | collective-permute-start | bytes 811016 | tf_op jit(solution)/shard_map/ppermute | solution.py:452
  13.2 13.1 %collective-permute-start.2 = (bf16[528,256]{1,0:T(8,128)(2,1)}, bf16[528,256]{1,0:T(8,128)(2,1)S(1)}, u32[]{:S(2)}, u32[]{:S(2)}) collective-permute-start(bf16[528,256]{1,0:T(8,128)(2,1)} %get-tuple-element.40), channel_id=1, source_target_pairs={{0,64},{2,66},{4,68},{6,70},{8,72},{10,74},{12,76},{14,78},{16,80}... | collective-permute-start | bytes 811016 | tf_op jit(solution)/shard_map/ppermute | solution.py:452
  13.3 23.5 %collective-permute-start.3 = (bf16[528,256]{1,0:T(8,128)(2,1)}, bf16[528,256]{1,0:T(8,128)(2,1)S(1)}, u32[]{:S(2)}, u32[]{:S(2)}) collective-permute-start(bf16[528,256]{1,0:T(8,128)(2,1)} %get-tuple-element.42), channel_id=1, source_target_pairs={{0,192},{2,194},{4,196},{6,198},{8,200},{10,202},{12,204},{14,206}... | collective-permute-start | bytes 811016 | tf_op jit(solution)/shard_map/ppermute | solution.py:452
  16.9 29.9 %collective-permute-start.4 = (bf16[528,256]{1,0:T(8,128)(2,1)}, bf16[528,256]{1,0:T(8,128)(2,1)S(1)}, u32[]{:S(2)}, u32[]{:S(2)}) collective-permute-start(bf16[528,256]{1,0:T(8,128)(2,1)} %get-tuple-element.43), channel_id=1, source_target_pairs={{0,96},{2,98},{4,100},{6,102},{8,104},{10,106},{12,108},{14,110},{... | collective-permute-start | bytes 811016 | tf_op jit(solution)/shard_map/ppermute | solution.py:452
  17.4 29.4 %collective-permute-start.5 = (bf16[528,256]{1,0:T(8,128)(2,1)}, bf16[528,256]{1,0:T(8,128)(2,1)S(1)}, u32[]{:S(2)}, u32[]{:S(2)}) collective-permute-start(bf16[528,256]{1,0:T(8,128)(2,1)} %get-tuple-element.44), channel_id=1, source_target_pairs={{0,160},{2,162},{4,164},{6,166},{8,168},{10,170},{12,172},{14,174}... | collective-permute-start | bytes 811016 | tf_op jit(solution)/shard_map/ppermute | solution.py:452
  21.4 33.0 %collective-permute-start.6 = (bf16[528,256]{1,0:T(8,128)(2,1)}, bf16[528,256]{1,0:T(8,128)(2,1)S(1)}, u32[]{:S(2)}, u32[]{:S(2)}) collective-permute-start(bf16[528,256]{1,0:T(8,128)(2,1)} %get-tuple-element.45), channel_id=1, source_target_pairs={{0,128},{2,130},{4,132},{6,134},{8,136},{10,138},{12,140},{14,142}... | collective-permute-start | bytes 811016 | tf_op jit(solution)/shard_map/ppermute | solution.py:452
  26.3 1.0 copy-start.1
  30.0 27.8 %all-to-all-start = ((bf16[16,96,512]{2,1,0:T(8,128)(2,1)}), bf16[16,96,512]{2,1,0:T(8,128)(2,1)S(1)}, u32[]{:S(2)}, u32[]{:S(2)}) async-start(bf16[16,96,512]{2,1,0:T(8,128)(2,1)} %get-tuple-element.48), calls=%async_computation | async-start | bytes 3145728 | tf_op jit(solution)/shard_map/all_to_all | solution.py:420
  57.9 28.0 %all-to-all-start.1 = ((bf16[16,112,512]{2,1,0:T(8,128)(2,1)}), bf16[16,112,512]{2,1,0:T(8,128)(2,1)S(1)}, u32[]{:S(2)}, u32[]{:S(2)}) async-start(bf16[16,112,512]{2,1,0:T(8,128)(2,1)} %get-tuple-element.49), calls=%async_computation.1 | async-start | bytes 3670016 | tf_op jit(solution)/shard_map/all_to_all | solution.py:420
  94.0 11.9 %collective-permute-start.8 = (bf16[256,512]{1,0:T(8,128)(2,1)S(1)}, bf16[256,512]{1,0:T(8,128)(2,1)S(1)}, u32[]{:S(2)}, u32[]{:S(2)}) collective-permute-start(bf16[256,512]{1,0:T(8,128)(2,1)S(1)} %get-tuple-element.53), channel_id=1, source_target_pairs={{2,0},{4,2},{6,4},{8,6},{10,8},{12,10},{14,12},{18,16},{20,18},{22... | collective-permute-start | bytes 786440 | tf_op jit(solution)/shard_map/ppermute | solution.py:429
  95.3 10.6 %collective-permute-start.7 = (bf16[256,256]{1,0:T(8,128)(2,1)S(1)}, bf16[256,256]{1,0:T(8,128)(2,1)S(1)}, u32[]{:S(2)}, u32[]{:S(2)}) collective-permute-start(bf16[256,256]{1,0:T(8,128)(2,1)S(1)} %get-tuple-element.52), channel_id=1, source_target_pairs={{0,2},{2,4},{4,6},{6,8},{8,10},{10,12},{12,14},{16,18},{18,20},{20... | collective-permute-start | bytes 393224 | tf_op jit(solution)/shard_map/ppermute | solution.py:429
  110.4 17.7 %all-to-all-start.3 = ((bf16[16,48,512]{2,1,0:T(8,128)(2,1)}), bf16[16,48,512]{2,1,0:T(8,128)(2,1)S(1)}, u32[]{:S(2)}, u32[]{:S(2)}) async-start(bf16[16,48,512]{2,1,0:T(8,128)(2,1)} %get-tuple-element.57), calls=%async_computation.3 | async-start | bytes 1572864 | tf_op jit(solution)/shard_map/all_to_all | solution.py:420
  117.7 1.6 copy-start.2
  128.1 29.3 %all-to-all-start.2 = ((bf16[16,96,512]{2,1,0:T(8,128)(2,1)}), bf16[16,96,512]{2,1,0:T(8,128)(2,1)S(1)}, u32[]{:S(2)}, u32[]{:S(2)}) async-start(bf16[16,96,512]{2,1,0:T(8,128)(2,1)} %shard_map.91), calls=%async_computation.2 | async-start | bytes 3145728 | tf_op jit(solution)/shard_map/all_to_all | solution.py:420
  131.8 11.4 %copy-start.3 = (bf16[2048,512]{1,0:T(8,128)(2,1)S(1)}, bf16[2048,512]{1,0:T(8,128)(2,1)}, u32[]{:S(2)}) copy-start(bf16[2048,512]{1,0:T(8,128)(2,1)} %get-tuple-element.56.o_ref) | copy-start | bytes 6291460
  132.5 22.1 %collective-permute-start.9 = (bf16[512,256]{1,0:T(8,128)(2,1)S(1)}, bf16[512,256]{1,0:T(8,128)(2,1)S(1)}, u32[]{:S(2)}, u32[]{:S(2)}) collective-permute-start(bf16[512,256]{1,0:T(8,128)(2,1)S(1)} %get-tuple-element.58), channel_id=1, source_target_pairs={{0,160},{2,162},{4,164},{6,166},{8,168},{10,170},{12,172},{14,174}... | collective-permute-start | bytes 786440 | tf_op jit(solution)/shard_map/ppermute | solution.py:553
  143.2 14.2 %collective-permute-start.10 = (bf16[512,256]{1,0:T(8,128)(2,1)S(1)}, bf16[512,256]{1,0:T(8,128)(2,1)S(1)}, u32[]{:S(2)}, u32[]{:S(2)}) collective-permute-start(bf16[512,256]{1,0:T(8,128)(2,1)S(1)} %get-tuple-element.59), channel_id=1, source_target_pairs={{0,96},{2,98},{4,100},{6,102},{8,104},{10,106},{12,108},{14,110},{... | collective-permute-start | bytes 786440 | tf_op jit(solution)/shard_map/ppermute | solution.py:553
  158.6 13.2 %collective-permute-start.13 = (bf16[512,256]{1,0:T(8,128)(2,1)S(1)}, bf16[512,256]{1,0:T(8,128)(2,1)S(1)}, u32[]{:S(2)}, u32[]{:S(2)}) collective-permute-start(bf16[512,256]{1,0:T(8,128)(2,1)S(1)} %get-tuple-element.62), channel_id=1, source_target_pairs={{0,192},{2,194},{4,196},{6,198},{8,200},{10,202},{12,204},{14,206}... | collective-permute-start | bytes 786440 | tf_op jit(solution)/shard_map/ppermute | solution.py:553
  158.7 13.1 %collective-permute-start.14 = (bf16[512,256]{1,0:T(8,128)(2,1)S(1)}, bf16[512,256]{1,0:T(8,128)(2,1)S(1)}, u32[]{:S(2)}, u32[]{:S(2)}) collective-permute-start(bf16[512,256]{1,0:T(8,128)(2,1)S(1)} %get-tuple-element.63), channel_id=1, source_target_pairs={{0,64},{2,66},{4,68},{6,70},{8,72},{10,74},{12,76},{14,78},{16,80}... | collective-permute-start | bytes 786440 | tf_op jit(solution)/shard_map/ppermute | solution.py:553
  161.1 17.2 %all-to-all-start.4 = ((bf16[16,48,512]{2,1,0:T(8,128)(2,1)}), bf16[16,48,512]{2,1,0:T(8,128)(2,1)S(1)}, u32[]{:S(2)}, u32[]{:S(2)}) async-start(bf16[16,48,512]{2,1,0:T(8,128)(2,1)} %shard_map.93.refs_5_), calls=%async_computation.4 | async-start | bytes 1572864 | tf_op jit(solution)/shard_map/all_to_all | solution.py:420
  167.9 12.5 %collective-permute-start.11 = (bf16[512,256]{1,0:T(8,128)(2,1)S(1)}, bf16[512,256]{1,0:T(8,128)(2,1)S(1)}, u32[]{:S(2)}, u32[]{:S(2)}) collective-permute-start(bf16[512,256]{1,0:T(8,128)(2,1)S(1)} %get-tuple-element.60), channel_id=1, source_target_pairs={{0,128},{2,130},{4,132},{6,134},{8,136},{10,138},{12,140},{14,142}... | collective-permute-start | bytes 786440 | tf_op jit(solution)/shard_map/ppermute | solution.py:553
  168.0 22.3 %collective-permute-start.12 = (bf16[512,256]{1,0:T(8,128)(2,1)S(1)}, bf16[512,256]{1,0:T(8,128)(2,1)S(1)}, u32[]{:S(2)}, u32[]{:S(2)}) collective-permute-start(bf16[512,256]{1,0:T(8,128)(2,1)S(1)} %get-tuple-element.61), channel_id=1, source_target_pairs={{0,32},{2,34},{4,36},{6,38},{8,40},{10,42},{12,44},{14,46},{16,48}... | collective-permute-start | bytes 786440 | tf_op jit(solution)/shard_map/ppermute | solution.py:553
  178.3 1.0 copy-start
  180.0 10.3 %collective-permute-start.15 = (bf16[512,256]{1,0:T(8,128)(2,1)S(1)}, bf16[512,256]{1,0:T(8,128)(2,1)S(1)}, u32[]{:S(2)}, u32[]{:S(2)}) collective-permute-start(bf16[512,256]{1,0:T(8,128)(2,1)S(1)} %get-tuple-element.66), channel_id=1, source_target_pairs={{0,224},{2,226},{4,228},{6,230},{8,232},{10,234},{12,236},{14,238}... | collective-permute-start | bytes 786440 | tf_op jit(solution)/shard_map/ppermute | solution.py:553
